TPU v7x, 512 devices: a whole 4x8x8 slice. The times are simulated.
512 devices in a mesh: dom: 32 (over x, y), super: 16 (over z, core).
Axes of the slice: x: 4, y: 8, z: 8, core: 2. Of those that a mesh axis runs over, the one named last changes fastest.
Arguments:
- node_feats: bfloat16 [65536, 256], P(('dom', 'super')), may hold values from -6 to 6
- grad_out: bfloat16 [65536, 256], P(('dom', 'super')), may hold values from -6 to 6
- neighbours: int32 [65536, 32], P(('dom', 'super')), may hold values from 0 to 191
- cluster: int32 [65536], P(('dom', 'super')), may hold values from 0 to 63
- super_links: int32 [2048, 8], P('dom'), may hold values from 0 to 63, all different within a row
- w_query: bfloat16 [256, 256], replicated, may hold values from -0.375 to 0.375
- w_key: bfloat16 [256, 256], replicated, may hold values from -0.375 to 0.375
- w_value: bfloat16 [256, 256], replicated, may hold values from -0.375 to 0.375
- w_out: bfloat16 [256, 256], replicated, may hold values from -0.375 to 0.375
Outputs:
- grad_nodes: bfloat16 [65536, 256], P(('dom', 'super'))
- grad_weights: float32 [4, 256, 256], P(None, 'super')
Inputs may be any that keep to these rules, and one draw needn't show every extreme that they name: `neighbours`: entries below 32 name the last 32 nodes of the previous block of the partition, the next 128 the block's own nodes, the rest the first 32 nodes of the following block, blocks taken cyclically. `cluster`: supernodes are numbered within the node's partition. `super_links`: each row names 8 different supernodes of the same partition.
All inputs are finite; a program needn't handle non-finite values.
Results may differ from a plain program's by a relative error of at most 0.013.
Values may be sent and summed in bfloat16 or wider, within the bound.
No kernel may reach another device: no remote copies, remote signals or barrier semaphores. Data moves between devices by JAX's collectives and lax.ppermute only.
A program may use at most 128 MiB of HBM per device.

v0:
```python
import math

import jax
import jax.numpy as jnp
from jax import lax
from jax.sharding import PartitionSpec as P

WIDTH = 256
HEADS = 8
HEAD_DIM = 32
DEG = 32
CLUSTER = 32
K_TOP = 8


PRECISE = lax.Precision.HIGHEST


def extended_2(block, sides, width):
    for axis, dim in sides:
        count = lax.axis_size(axis)
        forward = [(i, i + 1) for i in range(count - 1)]
        forward.append((count - 1, 0))
        backward = [(target, source) for source, target in forward]
        low = lax.ppermute(
            lax.slice_in_dim(block, block.shape[dim] - width, None, axis=dim), axis, forward
        )
        high = lax.ppermute(lax.slice_in_dim(block, 0, width, axis=dim), axis, backward)
        block = jnp.concatenate([low, block, high], axis=dim)
    return block


def softmax_last(scores):
    exponent = jnp.exp(scores)
    return exponent / jnp.sum(exponent, -1, keepdims=True)


def neighbour_terms(queries, kv_table, row_index, grad_attn):
    rows_here = queries.shape[0]
    score_scale = 1.0 / math.sqrt(HEAD_DIM)
    gathered = jnp.take(kv_table, row_index.reshape(-1), axis=0).reshape(
        rows_here, DEG, 2, HEADS, HEAD_DIM
    )
    key_rows = gathered[:, :, 0]
    value_rows = gathered[:, :, 1]
    query_heads = queries.reshape(rows_here, HEADS, HEAD_DIM)
    grad_heads = grad_attn.reshape(rows_here, HEADS, HEAD_DIM)
    attn_prob = softmax_last(
        jnp.einsum("bhd,bjhd->bhj", query_heads, key_rows, preferred_element_type=jnp.float32)
        * score_scale
    )
    attn_weight = attn_prob.astype(jnp.bfloat16)
    attended = jnp.einsum(
        "bhj,bjhd->bhd", attn_weight, value_rows, preferred_element_type=jnp.float32
    ).reshape(rows_here, WIDTH)
    grad_values = jnp.einsum(
        "bhj,bhd->bjhd", attn_weight, grad_heads, preferred_element_type=jnp.float32
    )
    grad_prob = jnp.einsum(
        "bhd,bjhd->bhj", grad_heads, value_rows, preferred_element_type=jnp.float32
    )
    grad_score = (
        attn_prob * (grad_prob - jnp.sum(attn_prob * grad_prob, -1, keepdims=True)) * score_scale
    ).astype(jnp.bfloat16)
    grad_query = jnp.einsum(
        "bhj,bjhd->bhd", grad_score, key_rows, preferred_element_type=jnp.float32
    ).reshape(rows_here, WIDTH)
    grad_keys = jnp.einsum(
        "bhj,bhd->bjhd", grad_score, query_heads, preferred_element_type=jnp.float32
    )
    key_grads = grad_keys.reshape(rows_here * DEG, WIDTH)
    value_grads = grad_values.reshape(rows_here * DEG, WIDTH)
    return (attended, grad_query, key_grads, value_grads)


def coarse_terms(queries, coarse_kv, grad_attn):
    rows_here = queries.shape[0]
    super_count = coarse_kv.shape[0]
    score_scale = 1.0 / math.sqrt(HEAD_DIM)
    key_heads = coarse_kv[:, :WIDTH].reshape(super_count, HEADS, HEAD_DIM)
    value_heads = coarse_kv[:, WIDTH:].reshape(super_count, HEADS, HEAD_DIM)
    query_heads = queries.reshape(rows_here, HEADS, HEAD_DIM)
    grad_heads = grad_attn.reshape(rows_here, HEADS, HEAD_DIM)
    attn_prob = softmax_last(
        jnp.einsum("bhd,shd->bhs", query_heads, key_heads, preferred_element_type=jnp.float32)
        * score_scale
    )
    attn_weight = attn_prob.astype(jnp.bfloat16)
    attended = jnp.einsum(
        "bhs,shd->bhd", attn_weight, value_heads, preferred_element_type=jnp.float32
    ).reshape(rows_here, WIDTH)
    grad_values = jnp.einsum(
        "bhs,bhd->shd", attn_weight, grad_heads, preferred_element_type=jnp.float32
    ).reshape(super_count, WIDTH)
    grad_prob = jnp.einsum(
        "bhd,shd->bhs", grad_heads, value_heads, preferred_element_type=jnp.float32
    )
    grad_score = (
        attn_prob * (grad_prob - jnp.sum(attn_prob * grad_prob, -1, keepdims=True)) * score_scale
    ).astype(jnp.bfloat16)
    grad_query = jnp.einsum(
        "bhs,shd->bhd", grad_score, key_heads, preferred_element_type=jnp.float32
    ).reshape(rows_here, WIDTH)
    grad_keys = jnp.einsum(
        "bhs,bhd->shd", grad_score, query_heads, preferred_element_type=jnp.float32
    ).reshape(super_count, WIDTH)
    return (attended, grad_query, jnp.concatenate([grad_keys, grad_values], 1))


def super_forward(pooled, pooled_proj, link_table):
    super_count = pooled.shape[0]
    score_scale = 1.0 / math.sqrt(HEAD_DIM)
    query_heads = pooled_proj[:, :WIDTH].astype(jnp.float32).reshape(super_count, HEADS, HEAD_DIM)
    linked = jnp.take(pooled_proj[:, WIDTH:], link_table.reshape(-1), axis=0).astype(jnp.float32)
    linked = linked.reshape(super_count, K_TOP, 2, HEADS, HEAD_DIM)
    key_rows = linked[:, :, 0]
    value_rows = linked[:, :, 1]
    attn_prob = softmax_last(
        jnp.einsum("shd,slhd->shl", query_heads, key_rows, precision=PRECISE) * score_scale
    )
    attn_weight = attn_prob.astype(jnp.bfloat16).astype(jnp.float32)
    attended = jnp.einsum("shl,slhd->shd", attn_weight, value_rows, precision=PRECISE).reshape(
        super_count, WIDTH
    )
    super_state = (pooled.astype(jnp.float32) + attended).astype(jnp.bfloat16)
    return (super_state, (query_heads, key_rows, value_rows, attn_prob, attn_weight))


def super_backward(grad_state, link_table, saved_terms, stacked_t):
    query_heads, key_rows, value_rows, attn_prob, attn_weight = saved_terms
    super_count = grad_state.shape[0]
    score_scale = 1.0 / math.sqrt(HEAD_DIM)
    grad_heads = grad_state.reshape(super_count, HEADS, HEAD_DIM)
    grad_values = jnp.einsum("shl,shd->slhd", attn_weight, grad_heads, precision=PRECISE)
    grad_prob = jnp.einsum("shd,slhd->shl", grad_heads, value_rows, precision=PRECISE)
    grad_score = (
        attn_prob * (grad_prob - jnp.sum(attn_prob * grad_prob, -1, keepdims=True)) * score_scale
    )
    grad_query = jnp.einsum("shl,slhd->shd", grad_score, key_rows, precision=PRECISE).reshape(
        super_count, WIDTH
    )
    grad_keys = jnp.einsum("shl,shd->slhd", grad_score, query_heads, precision=PRECISE)
    link_grads = jnp.stack([grad_keys, grad_values], 2).reshape(super_count * K_TOP, 2 * WIDTH)
    grad_kv = jax.ops.segment_sum(link_grads, link_table.reshape(-1), num_segments=super_count)
    grad_pooled_proj = jnp.concatenate([grad_query, grad_kv], 1)
    grad_pooled = grad_state + jnp.dot(grad_pooled_proj, stacked_t, precision=PRECISE)
    return (grad_pooled, grad_pooled_proj)


def local(node_feats, grad_out, neighbours, cluster, super_links, w_query, w_key, w_value, w_out):
    node_rows = node_feats.shape[0]
    feat_width = node_feats.shape[1]
    groups = lax.axis_size("super")
    owner_index = lax.axis_index("super")
    super_rows = node_rows // CLUSTER
    super_count = super_rows * groups
    halo_rows = node_rows // 4
    stacked = jnp.concatenate([w_query, w_key, w_value], 1)
    stacked_t = stacked.astype(jnp.float32).T
    projected = jnp.dot(node_feats, stacked, preferred_element_type=jnp.float32).astype(
        jnp.bfloat16
    )
    queries = projected[:, :feat_width]
    extended = extended_2(projected[:, feat_width:], (("super", 0),), halo_rows)
    labels = jnp.arange(super_count, dtype=jnp.int32)
    member = cluster[None, :] == labels[:, None]
    cluster_sums = jnp.dot(
        member.astype(jnp.bfloat16), node_feats, preferred_element_type=jnp.float32
    )
    counts = jnp.sum(member.astype(jnp.float32), 1)
    cluster_sums, counts = lax.psum((cluster_sums, counts), "super")
    divisor = jnp.maximum(counts, 1.0)
    pooled = (cluster_sums / divisor[:, None]).astype(jnp.bfloat16)
    pooled_proj = jnp.dot(pooled, stacked, preferred_element_type=jnp.float32).astype(jnp.bfloat16)
    super_state, saved_terms = super_forward(pooled, pooled_proj, super_links)
    coarse = jnp.dot(
        super_state, stacked[:, feat_width:], preferred_element_type=jnp.float32
    ).astype(jnp.bfloat16)
    grad_attn = jnp.dot(grad_out, w_out.T, preferred_element_type=jnp.float32).astype(jnp.bfloat16)
    ext_rows = extended.shape[0]
    near_step = min(128, node_rows)

    def near_block(tables, offset):
        key_table, value_table = tables
        near_out, near_query, key_grads, value_grads = neighbour_terms(
            queries, extended, neighbours, grad_attn
        )
        flat_index = neighbours.reshape(-1)
        key_table = key_table + jax.ops.segment_sum(key_grads, flat_index, num_segments=ext_rows)
        value_table = value_table + jax.ops.segment_sum(
            value_grads, flat_index, num_segments=ext_rows
        )
        return ((key_table, value_table), (near_out, near_query))

    near_offsets = jnp.arange(node_rows // near_step, dtype=jnp.int32) * near_step
    empty_table = jnp.zeros((ext_rows, feat_width), jnp.float32)
    (key_table, value_table), (near_out, near_query) = lax.scan(
        near_block, (empty_table, empty_table), near_offsets
    )
    grad_table = jnp.concatenate([key_table, value_table], 1)
    far_step = min(256, node_rows)

    def far_block(coarse_grads, offset):
        far_out, far_query, far_grads = coarse_terms(queries, coarse, grad_attn)
        return (coarse_grads + far_grads, (far_out, far_query))

    far_offsets = jnp.arange(node_rows // far_step, dtype=jnp.int32) * far_step
    coarse_grads, (far_out, far_query) = lax.scan(
        far_block, jnp.zeros((super_count, 2 * feat_width), jnp.float32), far_offsets
    )
    attended = (
        near_out.reshape(node_rows, feat_width) + far_out.reshape(node_rows, feat_width)
    ).astype(jnp.bfloat16)
    grad_query = near_query.reshape(node_rows, feat_width) + far_query.reshape(
        node_rows, feat_width
    )
    grad_wout = jnp.dot(attended.T, grad_out, preferred_element_type=jnp.float32)
    edge_rows = jnp.concatenate([grad_table[:halo_rows], grad_table[halo_rows + node_rows :]], 0)
    returned = extended_2(edge_rows.astype(jnp.bfloat16), (("super", 0),), halo_rows).astype(
        edge_rows.dtype
    )
    middle_zeros = jnp.zeros((node_rows - 2 * halo_rows, 2 * feat_width), jnp.float32)
    own_grads = grad_table[halo_rows : halo_rows + node_rows]
    own_grads = own_grads + jnp.concatenate(
        [returned[:halo_rows], middle_zeros, returned[-halo_rows:]], 0
    )
    summed_grads = lax.psum(coarse_grads.astype(jnp.bfloat16), "super").astype(jnp.float32)
    grad_state = jnp.dot(
        summed_grads[:, :feat_width], stacked_t[feat_width : 2 * feat_width], precision=PRECISE
    )
    grad_state = grad_state + jnp.dot(
        summed_grads[:, feat_width:], stacked_t[2 * feat_width :], precision=PRECISE
    )
    state_weights = jnp.dot(super_state.astype(jnp.float32).T, coarse_grads, precision=PRECISE)
    grad_pooled, grad_pooled_proj = super_backward(grad_state, super_links, saved_terms, stacked_t)
    own_start = owner_index * super_rows
    own_pooled_rows = lax.dynamic_slice_in_dim(pooled, own_start, super_rows, 0).astype(jnp.float32)
    own_proj_grads = lax.dynamic_slice_in_dim(grad_pooled_proj, own_start, super_rows, 0)
    super_weights = jnp.dot(own_pooled_rows.T, own_proj_grads, precision=PRECISE)
    grad_proj = jnp.concatenate([grad_query, own_grads], 1).astype(jnp.bfloat16)
    spread = jnp.take(grad_pooled / divisor[:, None], cluster, axis=0)
    grad_nodes = (
        grad_out.astype(jnp.float32)
        + jnp.dot(grad_proj, stacked.T, preferred_element_type=jnp.float32)
        + spread
    )
    weights = jnp.dot(node_feats.T, grad_proj, preferred_element_type=jnp.float32) + super_weights
    weights = weights + jnp.concatenate(
        [jnp.zeros((feat_width, feat_width), jnp.float32), state_weights], 1
    )
    stacked_grads = jnp.stack(
        [
            weights[:, :feat_width],
            weights[:, feat_width : 2 * feat_width],
            weights[:, 2 * feat_width :],
            grad_wout,
        ]
    )
    share_rows = feat_width // groups
    summed = lax.psum(stacked_grads, ("dom", "super"))
    own_share = lax.dynamic_slice_in_dim(summed, owner_index * share_rows, share_rows, 1)
    total_nodes = node_rows * groups * lax.axis_size("dom")
    own_share = own_share * (1.0 / math.sqrt(total_nodes))
    return (grad_nodes.astype(jnp.bfloat16), own_share)


def solution(mesh):
    return jax.shard_map(
        local,
        mesh=mesh,
        in_specs=(
            P(("dom", "super"), None),
            P(("dom", "super"), None),
            P(("dom", "super"), None),
            P(("dom", "super")),
            P("dom", None),
            P(),
            P(),
            P(),
            P(),
        ),
        out_specs=(P(("dom", "super"), None), P(None, "super", None)),
        check_vma=False,
    )
```

profile of v0, /device:TPU:24, one launch (start us, length us, event | category | flops | bytes accessed | tf_op | source)
XLA Modules:
  0.0 727.2 jit_solution(2679785460536208663)
XLA Ops:
  10.0 1.1 fusion.24
  11.1 8.5 %collective-permute-start.1 = (bf16[32,512]{1,0:T(8,128)(2,1)S(1)}, bf16[32,512]{1,0:T(8,128)(2,1)S(1)}, u32[]{:S(2)}, u32[]{:S(2)}) collective-permute-start(bf16[32,512]{1,0:T(8,128)(2,1)S(1)} %get-tuple-element.68), channel_id=1, source_target_pairs={{1,0},{2,1},{3,2},{4,3},{5,4},{6,5},{7,6},{8,7},{9,8},{10,9},{11,1... | collective-permute-start | bytes 98312 | tf_op jit(solution)/shard_map/ppermute | solution.py:28
  19.6 1.6 fusion.66
  25.1 1.2 compare_select_fusion.4
  26.3 1.2 compare_and_fusion.2
  27.7 24.2 %psum.29 = f32[64]{0:T(128)S(1)} all-reduce(f32[64]{0:T(128)S(1)} %convert_reduce_fusion), channel_id=1, replica_groups=mesh['dom'=32,'super'=16] {'super'}, use_global_device_ids=true, to_apply=%region_4.5 | all-reduce | flops 64 | bytes 512 | tf_op jit(solution)/shard_map/psum | solution.py:171
  53.9 71.1 %all-reduce.5.cloned.1.call-done = f32[64,256]{1,0:T(8,128)} async-done(((f32[64,256]{1,0:T(8,128)}), f32[64,256]{1,0:T(8,128)}) %all-reduce.5.cloned.1.call-update) | async-done | bytes 65552 | tf_op jit(solution)/shard_map/psum | solution.py:171
  126.2 17.3 %gather_fusion = bf16[4096,512]{1,0:T(8,128)(2,1)} fusion(bf16[192,512]{1,0:T(8,128)(2,1)S(1)} %pad_maximum_fusion.6, s32[4096]{0:T(1024)S(1)} %broadcast_clamp_fusion), kind=kCustom, calls=%fused_computation | custom fusion | bytes 8404992 | tf_op jit(solution)/shard_map/while/body/eval_jaxpr/jit(_take)/gather | solution.py:41
  143.5 19.2 %gather.18 = bf16[128,32,2,8,32]{4,3,2,1,0:T(8,128)(2,1)} reshape(bf16[4096,512]{1,0:T(8,128)(2,1)} %gather_fusion) | data formatting | bytes 8388608 | tf_op jit(solution)/shard_map/while/body/eval_jaxpr/jit(_take)/gather | solution.py:41
  162.6 6.9 broadcast_select_fusion
  169.6 9.2 %multiply_reduce_fusion.2 = (f32[128,8,32]{1,2,0:T(8,128)S(1)}, f32[128,8,32]{1,2,0:T(8,128)S(1)}) fusion(f32[128,8,32]{2,1,0:T(8,128)S(1)} %copy.132, bf16[128,32,2,8,32]{4,3,2,1,0:T(8,128)(2,1)S(1)} %broadcast_select_fusion, f32[128,8,32]{2,1,0:T(8,128)S(1)} %copy.131), kind=kLoop, calls=%fused_computation.13 | loop fusion | flops 6225920 | bytes 4718592 | tf_op jit(solution)/shard_map/while/body/eval_jaxpr/bhd,bjhd->bhj/dot_general | solution.py:59
  178.8 4.0 convert_convert_fusion
  182.8 3.1 fusion.10
  185.9 6.6 multiply_bitcast_fusion.1
  192.5 11.0 %multiply_reduce_fusion = (f32[128,8,32]{2,1,0:T(8,128)}, f32[128,8,32]{2,1,0:T(8,128)}) fusion(f32[128,8,32]{1,2,0:T(8,128)S(1)} %get-tuple-element.75, bf16[128,32,2,8,32]{4,3,2,1,0:T(8,128)(2,1)S(1)} %broadcast_select_fusion, f32[128,8,32]{1,2,0:T(8,128)S(1)} %fusion.10), kind=kLoop, calls=%fused_computation.11 | loop fusion | flops 6225920 | bytes 4718592
  203.5 6.5 multiply_bitcast_fusion
  210.0 2.0 gather_fusion.1
  212.0 2.2 gather.20
  214.5 1.9 broadcast_select_fusion.1
  219.6 1.1 convolution_convert_fusion.2
  223.8 1.2 fusion.61
  225.0 1.5 fusion.32
  226.5 1.2 fusion.44
  228.4 1.2 copy.94
  229.6 2.1 fusion.29
  231.7 12.2 %reshape.230 = f32[4096,256]{1,0:T(8,128)} reshape(f32[128,32,8,32]{3,2,1,0:T(8,128)} %multiply_bitcast_fusion.1) | data formatting | bytes 8388608 | tf_op jit(solution)/shard_map/while/body/eval_jaxpr/reshape | solution.py:71
  243.9 22.9 %scatter_custom_fusion = f32[192,256]{1,0:T(8,128)S(1)} fusion(s32[4096]{0:T(1024)S(1)} %reshape.228, f32[4096,256]{1,0:T(8,128)} %reshape.230, f32[]{:T(128)} %constant.62.clone.1), kind=kCustom, calls=%fused_computation.105 | custom fusion | flops 1048576 | bytes 197120 | tf_op jit(solution)/shard_map/while/body/eval_jaxpr/scatter-add | solution.py:189
  267.5 12.2 %reshape.238 = f32[4096,256]{1,0:T(8,128)} reshape(f32[128,32,8,32]{3,2,1,0:T(8,128)} %multiply_bitcast_fusion) | data formatting | bytes 8388608 | tf_op jit(solution)/shard_map/while/body/eval_jaxpr/reshape | solution.py:72
  279.7 22.9 %scatter_custom_fusion.1 = f32[192,256]{1,0:T(8,128)S(1)} fusion(s32[4096]{0:T(1024)S(1)} %reshape.228, f32[4096,256]{1,0:T(8,128)} %reshape.238, f32[]{:T(128)} %constant.62.clone.1), kind=kCustom, calls=%fused_computation.103 | custom fusion | flops 1048576 | bytes 197120 | tf_op jit(solution)/shard_map/while/body/eval_jaxpr/scatter-add | solution.py:190
  303.3 1.0 convert.36
  305.1 2.8 collective-permute-start.3
  308.0 1.2 copy.129
  309.2 1.8 fusion.30
  311.1 1.1 convolution_bitcast_fusion.1
  312.2 1.6 copy.66
  313.7 106.1 %all-reduce.7.cloned.1.call-done = bf16[64,512]{0,1:T(8,128)(2,1)} async-done(((bf16[64,512]{0,1:T(8,128)(2,1)}), bf16[64,512]{0,1:T(8,128)(2,1)}) %all-reduce.7.cloned.1.call-update) | async-done | bytes 65552 | tf_op jit(solution)/shard_map/psum | solution.py:227
  420.8 1.7 convolution_add_fusion.2
  422.5 1.6 copy.67
  424.1 1.7 copy.136
  425.8 2.5 multiply_bitcast_fusion.2
  428.4 1.4 fusion.20
  431.2 2.4 pad_maximum_fusion
  433.5 3.6 reshape.246
  438.6 3.7 scatter_custom_fusion.2
  442.4 1.2 fusion.13
  443.8 1.1 pad_maximum_fusion.1
  447.2 271.4 %all-reduce.9.cloned.1.call-done = f32[4,256,256]{1,2,0:T(8,128)} async-done(((f32[4,256,256]{1,2,0:T(8,128)}), f32[4,256,256]{1,2,0:T(8,128)}) %all-reduce.9.cloned.1.call-update) | async-done | bytes 1048592 | tf_op jit(solution)/shard_map/psum | solution.py:260
  718.7 1.2 dynamic-slice_multiply_fusion
  (130 shorter events, 26.1 us)
Async XLA Ops:
  7.2 44.8 %copy-start = (bf16[256,256]{1,0:T(8,128)(2,1)S(1)}, bf16[256,256]{1,0:T(8,128)(2,1)}, u32[]{:S(2)}) copy-start(bf16[256,256]{1,0:T(8,128)(2,1)} %param.17) | copy-start | bytes 393220
  7.2 44.8 %copy-start.19 = (bf16[128,256]{1,0:T(8,128)(2,1)S(1)}, bf16[128,256]{1,0:T(8,128)(2,1)}, u32[]{:S(2)}) copy-start(bf16[128,256]{1,0:T(8,128)(2,1)} %param.10) | copy-start | bytes 196612
  7.2 117.8 %all-reduce.5.cloned.1.call-start = ((), (), s32[]{:S(2)}) async-start(), calls=%async_computation | async-start | bytes 131072 | tf_op jit(solution)/shard_map/psum | solution.py:171
  11.1 115.1 %collective-permute-start = (bf16[32,512]{1,0:T(8,128)(2,1)S(1)}, bf16[32,512]{1,0:T(8,128)(2,1)S(1)}, u32[]{:S(2)}, u32[]{:S(2)}) collective-permute-start(bf16[32,512]{1,0:T(8,128)(2,1)S(1)} %get-tuple-element.67), channel_id=1, source_target_pairs={{0,1},{1,2},{2,3},{3,4},{4,5},{5,6},{6,7},{7,8},{8,9},{9,10},{10,1... | collective-permute-start | bytes 98312 | tf_op jit(solution)/shard_map/ppermute | solution.py:25
  11.1 115.0 %collective-permute-start.1 = (bf16[32,512]{1,0:T(8,128)(2,1)S(1)}, bf16[32,512]{1,0:T(8,128)(2,1)S(1)}, u32[]{:S(2)}, u32[]{:S(2)}) collective-permute-start(bf16[32,512]{1,0:T(8,128)(2,1)S(1)} %get-tuple-element.68), channel_id=1, source_target_pairs={{1,0},{2,1},{3,2},{4,3},{5,4},{6,5},{7,6},{8,7},{9,8},{10,9},{11,1... | collective-permute-start | bytes 98312 | tf_op jit(solution)/shard_map/ppermute | solution.py:28
  21.3 398.5 %all-reduce.7.cloned.1.call-start = ((), (), s32[]{:S(2)}) async-start(), calls=%async_computation.1 | async-start | bytes 262144 | tf_op jit(solution)/shard_map/psum | solution.py:227
  51.9 91.6 %copy-start.22 = (f32[64]{0:T(128)}, f32[64]{0:T(128)S(1)}, u32[]{:S(2)}) copy-start(f32[64]{0:T(128)S(1)} %broadcast_maximum_fusion) | copy-start | bytes 772
  125.9 93.6 %copy-start.11 = (bf16[64,256]{1,0:T(8,128)(2,1)}, bf16[64,256]{1,0:T(8,128)(2,1)S(1)}, u32[]{:S(2)}) copy-start(bf16[64,256]{1,0:T(8,128)(2,1)S(1)} %divide_convert_fusion) | copy-start | bytes 98308
  126.2 17.3 %copy-start.2 = (bf16[64,768]{1,0:T(8,128)(2,1)}, bf16[64,768]{1,0:T(8,128)(2,1)S(1)}, u32[]{:S(2)}) copy-start(bf16[64,768]{1,0:T(8,128)(2,1)S(1)} %convolution_convert_fusion.1) | copy-start | bytes 294916
  203.5 6.5 slice-start
  212.0 2.2 slice-start.1
  217.0 2.5 copy-start.21
  217.9 0.7 copy-start.4
  219.6 6.9 copy-start.13
  220.8 1.9 copy-start.18
  222.9 3.6 copy-start.16
  279.7 29.5 %copy-start.17 = (bf16[64,256]{0,1:T(8,128)(2,1)S(1)}, bf16[64,256]{0,1:T(8,128)(2,1)}, u32[]{:S(2)}) copy-start(bf16[64,256]{0,1:T(8,128)(2,1)} %copy-done.16) | copy-start | bytes 98308
  305.0 132.4 %collective-permute-start.2 = (bf16[32,512]{1,0:T(8,128)(2,1)}, bf16[32,512]{1,0:T(8,128)(2,1)}, u32[]{:S(2)}, u32[]{:S(2)}) collective-permute-start(bf16[32,512]{1,0:T(8,128)(2,1)} %get-tuple-element.65), channel_id=1, source_target_pairs={{0,1},{1,2},{2,3},{3,4},{4,5},{5,6},{6,7},{7,8},{8,9},{9,10},{10,1... | collective-permute-start | bytes 98312 | tf_op jit(solution)/shard_map/ppermute | solution.py:25
  305.1 132.3 %collective-permute-start.3 = (bf16[32,512]{1,0:T(8,128)(2,1)}, bf16[32,512]{1,0:T(8,128)(2,1)}, u32[]{:S(2)}, u32[]{:S(2)}) collective-permute-start(bf16[32,512]{1,0:T(8,128)(2,1)} %get-tuple-element.66), channel_id=1, source_target_pairs={{1,0},{2,1},{3,2},{4,3},{5,4},{6,5},{7,6},{8,7},{9,8},{10,9},{11,1... | collective-permute-start | bytes 98312 | tf_op jit(solution)/shard_map/ppermute | solution.py:28
  308.0 410.7 %all-reduce.9.cloned.1.call-start = ((), (), s32[]{:S(2)}) async-start(), calls=%async_computation.2 | async-start | bytes 2097152 | tf_op jit(solution)/shard_map/psum | solution.py:260
  425.8 2.5 copy-start.12
  433.5 4.7 copy-start.3
  433.5 4.8 copy-start.8
  433.5 4.8 copy-start.14
  437.4 5.0 copy-start.6
  438.3 4.1 copy-start.9
  443.6 1.3 copy-start.24
  443.6 1.3 copy-start.5
  443.6 1.3 copy-start.7
  443.7 1.3 copy-start.23
  443.7 2.5 copy-start.10
  443.7 2.5 copy-start.15
  443.7 2.5 copy-start.20
  443.8 2.5 copy-start.25
  444.9 275.8 %copy-start.1 = (bf16[256,256]{1,0:T(8,128)(2,1)S(1)}, bf16[256,256]{1,0:T(8,128)(2,1)}, u32[]{:S(2)}) copy-start(bf16[256,256]{1,0:T(8,128)(2,1)} %param.17) | copy-start | bytes 393220
Sparse Core Ops, SparseCore 0:
  21.4 103.5 all-reduce.4
  308.1 111.6 all-reduce.6
  445.0 273.5 all-reduce.8
where the time goes:
time: 729 us; the launch traced here: 727 us
  waiting for transfers between devices  449 us (62%)
  other arithmetic  119 us (16%)
  local copies, waits for them, and re-layouts  87.6 us (12%)
  blocking collectives  24.2 us (3%)
  matrix products  21.5 us (3%)
  between operations  14.5 us (2%)
  starting transfers between devices  11.6 us (2%)
    psum x1, waiting for transfers between devices, local(): summed = lax.psum(stacked_grads, ('dom', 'super'))  271 us
    psum x1, waiting for transfers between devices, local(): lax.psum(coarse_grads.astype(jnp.bfloat16), 'super').astype(jnp.float32)  106 us
    psum x1, waiting for transfers between devices, local(): cluster_sums, counts = lax.psum((cluster_sums, counts), 'super')  71.1 us
    gather x2, local copies, waits for them, and re-layouts, neighbour_terms(): jnp.take(kv_table, row_index.reshape(-1), axis=0)  36.4 us
    psum x1, blocking collectives, local(): cluster_sums, counts = lax.psum((cluster_sums, counts), 'super')  24.2 us
    scatter-add x1, other arithmetic, near_block(): jax.ops.segment_sum(value_grads, flat_index, num_segments=ext_rows)  22.9 us
    scatter-add x1, other arithmetic, near_block(): jax.ops.segment_sum(key_grads, flat_index, num_segments=ext_rows)  22.9 us
  transfers between devices with their start and end apart: 7, of which 3 were waited for; matrix products, arithmetic and copies ran while one was open for 5% of the time, Pallas kernels for 0%

commit v1 on v0

v1 whole, which is shorter than its diff:
```python
import functools
import math

import jax
import jax.numpy as jnp
from jax import lax
from jax.experimental import pallas as pl
from jax.experimental.pallas import tpu as pltpu
from jax.sharding import Mesh, PartitionSpec as P

WIDTH = 256
HEADS = 8
HEAD_DIM = 32
NODES = 128
HALO = 32
EXT = NODES + 2 * HALO
SUP = 64
SUM_ROWS = SUP + 16
STACK = HEADS * NODES
SCORE_SCALE = 1.0 / math.sqrt(HEAD_DIM)
NEVER = -1e30
BF = jnp.bfloat16
F32 = jnp.float32


def mm(a, b):
    return jnp.dot(a, b, preferred_element_type=F32)


def mm_nt(a, b):
    return lax.dot_general(a, b, (((1,), (1,)), ((), ())), preferred_element_type=F32)


def iota(shape, dim):
    return lax.broadcasted_iota(jnp.int32, shape, dim)


def flip(a):
    return a.astype(F32).T.astype(a.dtype)


def rows_of(h):
    return slice(h * HEAD_DIM, (h + 1) * HEAD_DIM)


def lanes_of(h):
    return slice(h * NODES, (h + 1) * NODES)


def stack_lanes(ref, flipped):
    ref[...] = jnp.zeros(ref.shape, ref.dtype)
    for h in range(HEADS):
        ref[rows_of(h), lanes_of(h)] = flipped[rows_of(h)]


def stack_rows(ref, rows):
    head = lax.shift_right_logical(iota(rows.shape, 1), 5)
    wide = rows.astype(F32)
    for h in range(HEADS):
        ref[lanes_of(h), :] = jnp.where(head == h, wide, 0.0).astype(rows.dtype)


def call(body, name, outs, scratch, flops, *args):
    size = sum(a.size * a.dtype.itemsize for a in args)
    return pl.pallas_call(
        body,
        name=name,
        out_shape=tuple(jax.ShapeDtypeStruct(s, d) for s, d in outs),
        scratch_shapes=[pltpu.VMEM(s, d) for s, d in scratch],
        compiler_params=pltpu.CompilerParams(vmem_limit_bytes=32 * 1024 * 1024),
        cost_estimate=pl.CostEstimate(flops=flops, bytes_accessed=size, transcendentals=0),
    )(*args)


def sums_body(x_ref, cluster_ref, out_ref):
    member = (cluster_ref[...] == iota((SUP, NODES), 0)).astype(F32)
    sums = mm(member.astype(BF), x_ref[...]).astype(BF)
    counts = jnp.sum(member, 1, keepdims=True)
    diagonal = iota((SUP, WIDTH), 0) == iota((SUP, WIDTH), 1)
    count_row = jnp.sum(jnp.where(diagonal, counts, 0.0), 0, keepdims=True)
    count_rows = jnp.broadcast_to(count_row, (SUM_ROWS - SUP, WIDTH)).astype(BF)
    for peer in range(out_ref.shape[0]):
        out_ref[peer, :SUP] = sums
        out_ref[peer, SUP:] = count_rows


def near_body(
    low_ref, x_ref, high_ref, grad_ref, slots_ref, wq_ref, wk_ref, wv_ref, wo_ref,
    q_ref, qt_ref, a_ref, at_ref, out_t_ref, gq_t_ref, wkv_ref, base_ref, back_low_ref, back_high_ref,
    q_lanes, a_lanes, q_rows, a_rows, weight_all, score_all,
):
    ext = jnp.concatenate([low_ref[...], x_ref[...], high_ref[...]], 0)
    wk = wk_ref[...]
    wv = wv_ref[...]
    queries = mm(x_ref[...], wq_ref[...]).astype(BF)
    keys = mm(ext, wk).astype(BF)
    vals = mm(ext, wv).astype(BF)
    grad_attn = mm_nt(grad_ref[...], wo_ref[...]).astype(BF)
    q_t = flip(queries)
    a_t = flip(grad_attn)
    keys_t = flip(keys)
    vals_t = flip(vals)
    q_ref[...] = queries
    qt_ref[...] = q_t
    a_ref[...] = grad_attn
    at_ref[...] = a_t
    stack_lanes(q_lanes, q_t)
    stack_lanes(a_lanes, a_t)
    stack_rows(q_rows, queries)
    stack_rows(a_rows, grad_attn)
    slots = slots_ref[...]
    row = iota((EXT, NODES), 0)
    count = jnp.zeros((EXT, NODES), F32)
    for j in range(slots.shape[0]):
        count = count + jnp.where(slots[j : j + 1] == row, 1.0, 0.0)
    log_count = jnp.where(count > 0.0, jnp.log(jnp.maximum(count, 1.0)), NEVER)
    for h in range(HEADS):
        score = mm(keys, q_lanes[:, lanes_of(h)])
        e = jnp.exp(score * SCORE_SCALE + log_count)
        prob = e * (1.0 / jnp.sum(e, 0, keepdims=True))
        weight = prob.astype(BF)
        g = mm(vals, a_lanes[:, lanes_of(h)])
        centre = jnp.sum(prob * g, 0, keepdims=True)
        d_score = (prob * (g - centre) * SCORE_SCALE).astype(BF)
        weight_all[:, lanes_of(h)] = weight
        score_all[:, lanes_of(h)] = d_score
        out_t_ref[rows_of(h)] = mm(vals_t[rows_of(h)], weight)
        gq_t_ref[rows_of(h)] = mm(keys_t[rows_of(h)], d_score)
    grad_keys = mm(score_all[...], q_rows[...]).astype(BF)
    grad_vals = mm(weight_all[...], a_rows[...]).astype(BF)
    ext_t = flip(ext)
    wkv_ref[0] = mm(ext_t, grad_keys)
    wkv_ref[1] = mm(ext_t, grad_vals)
    back = mm_nt(grad_keys, wk) + mm_nt(grad_vals, wv)
    base_ref[...] = grad_ref[...].astype(F32) + back[HALO : HALO + NODES]
    back_low_ref[...] = back[:HALO].astype(BF)
    back_high_ref[...] = back[HALO + NODES :].astype(BF)


def far_body(
    parts_ref, links_ref, x_ref, grad_ref, wq_ref, wk_ref, wv_ref,
    q_ref, qt_ref, a_ref, at_ref, near_t_ref, near_gq_ref, wkv_ref, base_ref,
    weights_ref, pooled_grad_ref, nodes_ref,
    lanes_a, lanes_b, rows_a, rows_b, weight_all, score_all, s_weight, s_prob, s_score, s_rows,
):
    wq = wq_ref[...]
    wk = wk_ref[...]
    wv = wv_ref[...]
    totals = jnp.sum(parts_ref[...].astype(F32), 0)
    diagonal = iota((SUP, WIDTH), 0) == iota((SUP, WIDTH), 1)
    counts = jnp.sum(jnp.where(diagonal, totals[SUP : SUP + 1], 0.0), 1, keepdims=True)
    inverse = 1.0 / jnp.maximum(counts, 1.0)
    pooled = (totals[:SUP] * inverse).astype(BF)
    pad = jnp.zeros((NODES - SUP, WIDTH), BF)

    s_q = jnp.concatenate([mm(pooled, wq).astype(BF), pad], 0)
    s_k = mm(pooled, wk).astype(BF)
    s_v = mm(pooled, wv).astype(BF)
    s_kt = flip(s_k)
    s_vt = flip(s_v)
    stack_lanes(lanes_a, flip(s_q))
    stack_rows(s_rows, s_q)
    links = links_ref[...]
    target = iota((SUP, NODES), 0)
    linked = iota((SUP, NODES), 1) >= SUP
    for l in range(links.shape[0]):
        linked = jnp.logical_or(linked, links[l : l + 1] == target)
    allowed = jnp.where(linked, 0.0, NEVER)
    state_t = []
    for h in range(HEADS):
        e = jnp.exp(mm(s_k, lanes_a[:, lanes_of(h)]) * SCORE_SCALE + allowed)
        prob = e * (1.0 / jnp.sum(e, 0, keepdims=True))
        weight = prob.astype(BF)
        s_prob[:, lanes_of(h)] = prob
        s_weight[:, lanes_of(h)] = weight
        state_t.append(mm(s_vt[rows_of(h)], weight))
    state = (pooled.astype(F32) + jnp.concatenate(state_t, 0).T[:SUP]).astype(BF)

    c_k = mm(state, wk).astype(BF)
    c_v = mm(state, wv).astype(BF)
    c_kt = flip(c_k)
    c_vt = flip(c_v)
    stack_lanes(lanes_a, qt_ref[...])
    stack_lanes(lanes_b, at_ref[...])
    stack_rows(rows_a, q_ref[...])
    stack_rows(rows_b, a_ref[...])
    out_t = []
    gq_t = []
    for h in range(HEADS):
        e = jnp.exp(mm(c_k, lanes_a[:, lanes_of(h)]) * SCORE_SCALE)
        prob = e * (1.0 / jnp.sum(e, 0, keepdims=True))
        weight = prob.astype(BF)
        g = mm(c_v, lanes_b[:, lanes_of(h)])
        centre = jnp.sum(prob * g, 0, keepdims=True)
        d_score = (prob * (g - centre) * SCORE_SCALE).astype(BF)
        weight_all[:, lanes_of(h)] = weight
        score_all[:, lanes_of(h)] = d_score
        out_t.append(mm(c_vt[rows_of(h)], weight))
        gq_t.append(mm(c_kt[rows_of(h)], d_score))
    grad_ck = mm(score_all[...], rows_a[...]).astype(BF)
    grad_cv = mm(weight_all[...], rows_b[...]).astype(BF)

    grad_state = mm_nt(grad_ck, wk) + mm_nt(grad_cv, wv)
    gs = jnp.concatenate([grad_state.astype(BF), pad], 0)
    stack_lanes(lanes_b, flip(gs))
    stack_rows(rows_b, gs)
    gsq_t = []
    for h in range(HEADS):
        prob = s_prob[:, lanes_of(h)]
        g = mm(s_v, lanes_b[:, lanes_of(h)])
        centre = jnp.sum(prob * g, 0, keepdims=True)
        d_score = (prob * (g - centre) * SCORE_SCALE).astype(BF)
        s_score[:, lanes_of(h)] = d_score
        gsq_t.append(mm(s_kt[rows_of(h)], d_score))
    gsq = jnp.concatenate(gsq_t, 0).T[:SUP].astype(BF)
    gsk = mm(s_score[...], s_rows[...]).astype(BF)
    gsv = mm(s_weight[...], rows_b[...]).astype(BF)
    projections = jnp.concatenate([wq, wk, wv], 1)
    grad_pooled = grad_state + mm_nt(jnp.concatenate([gsq, gsk, gsv], 1), projections)
    pooled_grad_ref[...] = (grad_pooled * inverse).astype(BF)

    gq = (near_gq_ref[...] + jnp.concatenate(gq_t, 0)).T.astype(BF)
    attended_t = (near_t_ref[...] + jnp.concatenate(out_t, 0)).astype(BF)
    pooled_t = flip(pooled)
    state_flip = flip(state)
    weights_ref[0] = (mm(flip(x_ref[...]), gq) + mm(pooled_t, gsq)).astype(BF)
    weights_ref[1] = (wkv_ref[0] + mm(pooled_t, gsk) + mm(state_flip, grad_ck)).astype(BF)
    weights_ref[2] = (wkv_ref[1] + mm(pooled_t, gsv) + mm(state_flip, grad_cv)).astype(BF)
    weights_ref[3] = mm(attended_t, grad_ref[...]).astype(BF)
    nodes_ref[...] = base_ref[...] + mm_nt(gq, wq)


def final_body(scale, parts_ref, out_ref):
    rows = parts_ref.shape[0] // out_ref.shape[0]
    for w in range(out_ref.shape[0]):
        part = parts_ref[w * rows : (w + 1) * rows].astype(F32)
        out_ref[w] = jnp.sum(part, 0) * scale


def nodes_body(pieces_ref, base_ref, low_ref, high_ref, parts_ref, cluster_ref, share_ref, out_ref):
    share = jnp.sum(pieces_ref[...].astype(F32), 0).astype(BF)
    for peer in range(share_ref.shape[0]):
        share_ref[peer] = share
    grad_pooled = jnp.sum(parts_ref[...].astype(F32), 0)
    coarse = grad_pooled.astype(BF)
    fine = (grad_pooled - coarse.astype(F32)).astype(BF)
    member = (cluster_ref[...] == iota((SUP, NODES), 0)).astype(F32).T.astype(BF)
    spread = mm(jnp.concatenate([member, member], 1), jnp.concatenate([coarse, fine], 0))
    total = base_ref[...] + spread
    out_ref[:HALO] = (total[:HALO] + low_ref[...].astype(F32)).astype(BF)
    out_ref[HALO : NODES - HALO] = total[HALO : NODES - HALO].astype(BF)
    out_ref[NODES - HALO :] = (total[NODES - HALO :] + high_ref[...].astype(F32)).astype(BF)


def swap(parts, axes):
    return lax.all_to_all(parts, axes, 0, 0, tiled=True)


def local(sizes, node_feats, grad_out, neighbours, cluster, super_links, w_query, w_key, w_value, w_out):
    n_x, n_y, n_z, n_c = sizes
    n_super = n_z * n_c
    n_dom = n_x * n_y
    supers = ("z", "c")
    up = [(i, (i + 1) % n_super) for i in range(n_super)]
    down = [(i, (i + n_super - 1) % n_super) for i in range(n_super)]
    cluster_row = cluster.reshape(1, NODES)
    (sums,) = call(
        sums_body, "cluster_sums", [((n_super, SUM_ROWS, WIDTH), BF)], [], 1 << 22, node_feats, cluster_row
    )
    low = lax.ppermute(node_feats[NODES - HALO :], supers, up)
    high = lax.ppermute(node_feats[:HALO], supers, down)
    sums, low, high = lax.optimization_barrier((sums, low, high))
    parts = swap(sums, supers)
    q, q_t, a, a_t, near_t, near_gq, wkv, base, back_low, back_high = call(
        near_body,
        "near_attention",
        [
            ((NODES, WIDTH), BF), ((WIDTH, NODES), BF), ((NODES, WIDTH), BF), ((WIDTH, NODES), BF),
            ((WIDTH, NODES), F32), ((WIDTH, NODES), F32), ((2, WIDTH, WIDTH), F32), ((NODES, WIDTH), F32),
            ((HALO, WIDTH), BF), ((HALO, WIDTH), BF),
        ],
        [
            ((WIDTH, STACK), BF), ((WIDTH, STACK), BF), ((STACK, WIDTH), BF), ((STACK, WIDTH), BF),
            ((EXT, STACK), BF), ((EXT, STACK), BF),
        ],
        10 << 30,
        low, node_feats, high, grad_out, neighbours.T, w_query, w_key, w_value, w_out,
    )
    from_high = lax.ppermute(back_low, supers, down)
    from_low = lax.ppermute(back_high, supers, up)
    links = jnp.pad(super_links.T, ((0, 0), (0, NODES - SUP)))
    weights, pooled_share, own = call(
        far_body,
        "far_attention",
        [((4, WIDTH, WIDTH), BF), ((SUP, WIDTH), BF), ((NODES, WIDTH), F32)],
        [
            ((WIDTH, STACK), BF), ((WIDTH, STACK), BF), ((STACK, WIDTH), BF), ((STACK, WIDTH), BF),
            ((SUP, STACK), BF), ((SUP, STACK), BF), ((SUP, STACK), BF), ((SUP, STACK), F32), ((SUP, STACK), BF),
            ((STACK, WIDTH), BF),
        ],
        10 << 30,
        parts, links, node_feats, grad_out, w_query, w_key, w_value,
        q, q_t, a, a_t, near_t, near_gq, wkv, base,
    )
    share_rows = WIDTH // n_super
    pieces = swap(weights.reshape(4 * n_super, share_rows, WIDTH), ("x",) + supers)
    pooled_parts = lax.all_gather(pooled_share, supers)
    shares, grad_nodes = call(
        nodes_body,
        "grad_nodes",
        [((n_dom, share_rows, WIDTH), BF), ((NODES, WIDTH), BF)],
        [],
        1 << 30,
        pieces, own, from_low, from_high, pooled_parts, cluster_row,
    )
    shares = swap(shares, ("x", "y"))
    scale = 1.0 / math.sqrt(NODES * n_super * n_dom)
    (grad_weights,) = call(
        functools.partial(final_body, scale), "grad_weights", [((4, share_rows, WIDTH), F32)], [], 1 << 20, shares
    )
    return grad_nodes, grad_weights


def solution(mesh):
    n_dom = mesh.shape["dom"]
    n_super = mesh.shape["super"]
    sizes = (4, n_dom // 4, n_super // 2, 2)
    fine = Mesh(mesh.devices.reshape(sizes), ("x", "y", "z", "c"))
    everyone = ("x", "y", "z", "c")
    return jax.shard_map(
        functools.partial(local, sizes),
        mesh=fine,
        in_specs=(
            P(everyone, None),
            P(everyone, None),
            P(everyone, None),
            P(everyone),
            P(("x", "y"), None),
            P(),
            P(),
            P(),
            P(),
        ),
        out_specs=(P(everyone, None), P(None, ("z", "c"), None)),
        check_vma=False,
    )
```

time: 729 us -> 102 us (0.14)
  the two profiles are of different devices: /device:TPU:24 before, /device:TPU:8 now
where the time goes in v1:
time: 102 us; the launch traced here: 101 us
  blocking collectives  46.6 us (46%)
  starting transfers between devices  23.2 us (23%)
  waiting for transfers between devices  17.7 us (17%)
  Pallas kernels  11.6 us (11%)
  local copies, waits for them, and re-layouts  1.48 us (1%)
    all_gather x1, blocking collectives, local(): pooled_parts = lax.all_gather(pooled_share, supers)  23.7 us
    all_to_all x1, blocking collectives, swap(): return lax.all_to_all(parts, axes, 0, 0, tiled=True)  22.9 us
    all_to_all x2, waiting for transfers between devices, swap(): return lax.all_to_all(parts, axes, 0, 0, tiled=True)  15 us
    all_to_all x2, starting transfers between devices, swap(): return lax.all_to_all(parts, axes, 0, 0, tiled=True)  11.8 us
    pallas_call x5, Pallas kernels, call(): pl.pallas_call(body, name=name, out_shape=tuple((jax.ShapeDtypeStruct(s,...  11.6 us
    ppermute x1, starting transfers between devices, local(): high = lax.ppermute(node_feats[:HALO], supers, down)  8.48 us
    ppermute x1, starting transfers between devices, local(): from_high = lax.ppermute(back_low, supers, down)  2.9 us
    ppermute x1, waiting for transfers between devices, local(): low = lax.ppermute(node_feats[NODES - HALO:], supers, up)  2.66 us
  transfers between devices with their start and end apart: 6, of which 2 were waited for; matrix products, arithmetic and copies ran while one was open for 0% of the time, Pallas kernels for 4%

profile of v1, /device:TPU:8, one launch (start us, length us, event | category | flops | bytes accessed | tf_op | source)
XLA Modules:
  0.0 101.3 jit_solution(11800960282267087818)
XLA Ops:
  0.6 0.0 copy-start
  0.6 0.8 fusion
  1.4 8.5 %collective-permute-start.1 = (bf16[32,256]{1,0:T(8,128)(2,1)S(1)}, bf16[32,256]{1,0:T(8,128)(2,1)S(1)}, u32[]{:S(2)}, u32[]{:S(2)}) collective-permute-start(bf16[32,256]{1,0:T(8,128)(2,1)S(1)} %get-tuple-element.38), channel_id=1, source_target_pairs={{0,15},{1,0},{2,1},{3,2},{4,3},{5,4},{6,5},{7,6},{8,7},{9,8},{10,9... | collective-permute-start | bytes 49160 | tf_op jit(solution)/shard_map/ppermute | solution.py:271
  9.9 0.0 copy-start.1
  9.9 0.0 collective-permute-start
  9.9 0.0 copy-done
  9.9 0.6 copy-done.1
  10.6 1.0 cluster_sums.1
  11.6 0.0 copy-start.2
  11.6 0.0 copy-start.3
  11.6 0.0 copy-start.4
  11.6 0.0 copy-start.5
  11.6 0.0 copy-start.6
  11.6 0.0 copy-start.7
  11.6 0.0 collective-permute-done.1.high_ref
  11.6 2.7 %collective-permute-done.low_ref = bf16[32,256]{1,0:T(8,128)(2,1)S(1)} collective-permute-done((bf16[32,256]{1,0:T(8,128)(2,1)S(1)}, bf16[32,256]{1,0:T(8,128)(2,1)S(1)}, u32[]{:S(2)}, u32[]{:S(2)}) %collective-permute-start) | collective-permute-done | bytes 16416 | tf_op jit(solution)/shard_map/ppermute | solution.py:270
  14.3 0.0 copy-start.8
  14.3 3.7 %all-to-all-start = ((bf16[16,80,256]{2,1,0:T(8,128)(2,1)}), bf16[16,80,256]{2,1,0:T(8,128)(2,1)S(1)}, u32[]{:S(2)}, u32[]{:S(2)}) async-start(bf16[16,80,256]{2,1,0:T(8,128)(2,1)} %cluster_sums.1), calls=%async_computation | async-start | bytes 1310720 | tf_op jit(solution)/shard_map/all_to_all | solution.py:256
  18.0 0.0 copy-done.8
  18.0 0.0 copy-done.2
  18.0 0.0 copy-done.3
  18.1 0.0 copy-done.4
  18.1 0.0 copy-done.5
  18.1 0.0 copy-done.6
  18.1 0.0 copy-done.7
  18.1 3.2 %near_attention.1 = (bf16[128,256]{1,0:T(8,128)(2,1)S(1)}, bf16[256,128]{1,0:T(8,128)(2,1)S(1)}, bf16[128,256]{1,0:T(8,128)(2,1)S(1)}, bf16[256,128]{1,0:T(8,128...) custom-call(bf16[32,256]{1,0:T(8,128)(2,1)S(1)} %collective-permute-, ...), custom_call_target="tpu_custom_call" | custom-call | flops 10737418240 | bytes 704512 | tf_op jit(solution)/shard_map/near_attention/pallas_call | solution.py:65
  21.3 15.0 %all-to-all-done.parts_ref = bf16[16,80,256]{2,1,0:T(8,128)(2,1)S(1)} async-done(((bf16[16,80,256]{2,1,0:T(8,128)(2,1)}), bf16[16,80,256]{2,1,0:T(8,128)(2,1)S(1)}, u32[]{:S(2)}, u32[]{:S(2)}) %all-to-all-start) | async-done | bytes 655392 | tf_op jit(solution)/shard_map/all_to_all | solution.py:256
  36.3 5.7 %far_attention.1 = (bf16[4,256,256]{2,1,0:T(8,128)(2,1)}, bf16[64,256]{1,0:T(8,128)(2,1)S(1)}, f32[128,256]{1,0:T(8,128)S(1)}) custom-call(bf16[16,80,256]{2,1,0:T(8,128)(2,1)S(1)} %all-to-all-done.parts_ref, s32[8,128]{1,0:T(8,128)S(1)} %pad.4.links_ref, bf16[128,256]{1,0:T(8,128)(2,1)S(1)} %copy-done, bf16[128,256]{1,0:T(8,128)(2,1)S(1)} %copy-done.6, ...), custom_call_target="tpu_custom_call" | custom-call | flops 10737418240 | bytes 2363392 | tf_op jit(solution)/shard_map/far_attention/pallas_call | solution.py:65
  42.0 8.1 %all-to-all-start.1 = ((bf16[64,16,256]{2,1,0:T(8,128)(2,1)}), bf16[64,16,256]{2,1,0:T(8,128)(2,1)S(1)}, u32[]{:S(2)}, u32[]{:S(2)}) async-start(bf16[64,16,256]{2,1,0:T(8,128)(2,1)} %bitcast.3), calls=%async_computation.1 | async-start | bytes 1048576 | tf_op jit(solution)/shard_map/all_to_all | solution.py:256
  50.1 0.1 collective-permute-start.2
  50.1 2.9 %collective-permute-start.3 = (bf16[32,256]{1,0:T(8,128)(2,1)S(1)}, bf16[32,256]{1,0:T(8,128)(2,1)S(1)}, u32[]{:S(2)}, u32[]{:S(2)}) collective-permute-start(bf16[32,256]{1,0:T(8,128)(2,1)S(1)} %get-tuple-element.34), channel_id=1, source_target_pairs={{0,15},{1,0},{2,1},{3,2},{4,3},{5,4},{6,5},{7,6},{8,7},{9,8},{10,9... | collective-permute-start | bytes 49160 | tf_op jit(solution)/shard_map/ppermute | solution.py:289
  53.0 23.7 %all-gather = bf16[1024,256]{1,0:T(8,128)(2,1)S(1)} all-gather(bf16[64,256]{1,0:T(8,128)(2,1)S(1)} %get-tuple-element.35), channel_id=2, replica_groups=mesh['x'=4,'y'=8,'z'=8,'c'=2] {'z','c'}, dimensions={0}, use_global_device_ids=true | all-gather | bytes 557056 | tf_op jit(solution)/shard_map/all_gather | solution.py:307
  76.8 0.0 collective-permute-done.2.low_ref
  76.8 0.0 collective-permute-done.3.high_ref
  76.8 0.0 all-to-all-done.1.pieces_ref
  76.8 1.0 grad_nodes.1
  77.8 22.9 %all_to_all.15.parts_ref = bf16[32,16,256]{2,1,0:T(8,128)(2,1)S(1)} all-to-all(bf16[32,16,256]{2,1,0:T(8,128)(2,1)S(1)} %get-tuple-element.37), channel_id=1, replica_groups=mesh['x'=4,'y'=8,'z'=8,'c'=2] {'x','y'}, dimensions={0} | all-to-all | bytes 524288 | tf_op jit(solution)/shard_map/all_to_all | solution.py:256
  100.6 0.7 grad_weights.1
  (1 shorter events, 0.0 us)
Async XLA Ops:
  0.6 9.3 %copy-start = (bf16[128,256]{1,0:T(8,128)(2,1)S(1)}, bf16[128,256]{1,0:T(8,128)(2,1)}, u32[]{:S(2)}) copy-start(bf16[128,256]{1,0:T(8,128)(2,1)} %x_ref.5) | copy-start | bytes 196612
  1.4 10.2 %collective-permute-start.1 = (bf16[32,256]{1,0:T(8,128)(2,1)S(1)}, bf16[32,256]{1,0:T(8,128)(2,1)S(1)}, u32[]{:S(2)}, u32[]{:S(2)}) collective-permute-start(bf16[32,256]{1,0:T(8,128)(2,1)S(1)} %get-tuple-element.38), channel_id=1, source_target_pairs={{0,15},{1,0},{2,1},{3,2},{4,3},{5,4},{6,5},{7,6},{8,7},{9,8},{10,9... | collective-permute-start | bytes 49160 | tf_op jit(solution)/shard_map/ppermute | solution.py:271
  9.9 0.7 copy-start.1
  9.9 4.4 %collective-permute-start = (bf16[32,256]{1,0:T(8,128)(2,1)S(1)}, bf16[32,256]{1,0:T(8,128)(2,1)S(1)}, u32[]{:S(2)}, u32[]{:S(2)}) collective-permute-start(bf16[32,256]{1,0:T(8,128)(2,1)S(1)} %get-tuple-element.39), channel_id=1, source_target_pairs={{0,1},{1,2},{2,3},{3,4},{4,5},{5,6},{6,7},{7,8},{8,9},{9,10},{10,1... | collective-permute-start | bytes 49160 | tf_op jit(solution)/shard_map/ppermute | solution.py:270
  11.6 6.5 %copy-start.2 = (bf16[256,256]{1,0:T(8,128)(2,1)S(1)}, bf16[256,256]{1,0:T(8,128)(2,1)}, u32[]{:S(2)}) copy-start(bf16[256,256]{1,0:T(8,128)(2,1)} %wo_ref.1) | copy-start | bytes 393220
  11.6 6.5 %copy-start.3 = (bf16[256,256]{1,0:T(8,128)(2,1)S(1)}, bf16[256,256]{1,0:T(8,128)(2,1)}, u32[]{:S(2)}) copy-start(bf16[256,256]{1,0:T(8,128)(2,1)} %wq_ref.3) | copy-start | bytes 393220
  11.6 6.5 %copy-start.4 = (bf16[256,256]{1,0:T(8,128)(2,1)S(1)}, bf16[256,256]{1,0:T(8,128)(2,1)}, u32[]{:S(2)}) copy-start(bf16[256,256]{1,0:T(8,128)(2,1)} %wk_ref.3) | copy-start | bytes 393220
  11.6 6.5 %copy-start.5 = (bf16[256,256]{1,0:T(8,128)(2,1)S(1)}, bf16[256,256]{1,0:T(8,128)(2,1)}, u32[]{:S(2)}) copy-start(bf16[256,256]{1,0:T(8,128)(2,1)} %wv_ref.3) | copy-start | bytes 393220
  11.6 6.5 %copy-start.6 = (bf16[128,256]{1,0:T(8,128)(2,1)S(1)}, bf16[128,256]{1,0:T(8,128)(2,1)}, u32[]{:S(2)}) copy-start(bf16[128,256]{1,0:T(8,128)(2,1)} %grad_ref.3) | copy-start | bytes 196612
  11.6 6.5 %copy-start.7 = (s32[128,32]{0,1:T(8,128)S(1)}, s32[128,32]{0,1:T(8,128)}, u32[]{:S(2)}) copy-start(s32[128,32]{0,1:T(8,128)} %param.11) | copy-start | bytes 49156
  14.3 3.7 %copy-start.8 = (s32[64,8]{0,1:T(8,128)S(1)}, s32[64,8]{0,1:T(8,128)}, u32[]{:S(2)}) copy-start(s32[64,8]{0,1:T(8,128)} %param.13) | copy-start | bytes 6148
  14.3 22.0 %all-to-all-start = ((bf16[16,80,256]{2,1,0:T(8,128)(2,1)}), bf16[16,80,256]{2,1,0:T(8,128)(2,1)S(1)}, u32[]{:S(2)}, u32[]{:S(2)}) async-start(bf16[16,80,256]{2,1,0:T(8,128)(2,1)} %cluster_sums.1), calls=%async_computation | async-start | bytes 1310720 | tf_op jit(solution)/shard_map/all_to_all | solution.py:256
  42.0 34.8 %all-to-all-start.1 = ((bf16[64,16,256]{2,1,0:T(8,128)(2,1)}), bf16[64,16,256]{2,1,0:T(8,128)(2,1)S(1)}, u32[]{:S(2)}, u32[]{:S(2)}) async-start(bf16[64,16,256]{2,1,0:T(8,128)(2,1)} %bitcast.3), calls=%async_computation.1 | async-start | bytes 1048576 | tf_op jit(solution)/shard_map/all_to_all | solution.py:256
  50.1 26.7 %collective-permute-start.2 = (bf16[32,256]{1,0:T(8,128)(2,1)S(1)}, bf16[32,256]{1,0:T(8,128)(2,1)S(1)}, u32[]{:S(2)}, u32[]{:S(2)}) collective-permute-start(bf16[32,256]{1,0:T(8,128)(2,1)S(1)} %get-tuple-element.33), channel_id=1, source_target_pairs={{0,1},{1,2},{2,3},{3,4},{4,5},{5,6},{6,7},{7,8},{8,9},{9,10},{10,1... | collective-permute-start | bytes 49160 | tf_op jit(solution)/shard_map/ppermute | solution.py:290
  50.1 26.6 %collective-permute-start.3 = (bf16[32,256]{1,0:T(8,128)(2,1)S(1)}, bf16[32,256]{1,0:T(8,128)(2,1)S(1)}, u32[]{:S(2)}, u32[]{:S(2)}) collective-permute-start(bf16[32,256]{1,0:T(8,128)(2,1)S(1)} %get-tuple-element.34), channel_id=1, source_target_pairs={{0,15},{1,0},{2,1},{3,2},{4,3},{5,4},{6,5},{7,6},{8,7},{9,8},{10,9... | collective-permute-start | bytes 49160 | tf_op jit(solution)/shard_map/ppermute | solution.py:289

commit v2 on v1

--- a/solution.py
+++ b/solution.py
@@ -62,8 +62,11 @@
 
 def call(body, name, outs, scratch, flops, *args):
     size = sum(a.size * a.dtype.itemsize for a in args)
+    vmem = pl.BlockSpec(memory_space=pltpu.VMEM)
+    smem = pl.BlockSpec(memory_space=pltpu.SMEM)
     return pl.pallas_call(
         body,
+        in_specs=[smem if a.ndim == 1 else vmem for a in args],
         name=name,
         out_shape=tuple(jax.ShapeDtypeStruct(s, d) for s, d in outs),
         scratch_shapes=[pltpu.VMEM(s, d) for s, d in scratch],
@@ -74,14 +77,18 @@
 
 def sums_body(x_ref, cluster_ref, out_ref):
     member = (cluster_ref[...] == iota((SUP, NODES), 0)).astype(F32)
-    sums = mm(member.astype(BF), x_ref[...]).astype(BF)
+    sums = mm(member.astype(BF), x_ref[...])
     counts = jnp.sum(member, 1, keepdims=True)
     diagonal = iota((SUP, WIDTH), 0) == iota((SUP, WIDTH), 1)
     count_row = jnp.sum(jnp.where(diagonal, counts, 0.0), 0, keepdims=True)
-    count_rows = jnp.broadcast_to(count_row, (SUM_ROWS - SUP, WIDTH)).astype(BF)
+    out_ref[:SUP] = sums
+    out_ref[SUP:] = jnp.broadcast_to(count_row, (SUM_ROWS - SUP, WIDTH))
+
+
+def chip_sums_body(parts_ref, out_ref):
+    total = (parts_ref[0] + parts_ref[1]).astype(BF)
     for peer in range(out_ref.shape[0]):
-        out_ref[peer, :SUP] = sums
-        out_ref[peer, SUP:] = count_rows
+        out_ref[peer] = total
 
 
 def near_body(
@@ -139,8 +146,8 @@
 
 def far_body(
     parts_ref, links_ref, x_ref, grad_ref, wq_ref, wk_ref, wv_ref,
-    q_ref, qt_ref, a_ref, at_ref, near_t_ref, near_gq_ref, wkv_ref, base_ref,
-    weights_ref, pooled_grad_ref, nodes_ref,
+    q_ref, qt_ref, a_ref, at_ref, near_t_ref, near_gq_ref, wkv_ref, base_ref, core_ref,
+    mine_ref, mine_pooled_ref, theirs_ref, nodes_ref,
     lanes_a, lanes_b, rows_a, rows_b, weight_all, score_all, s_weight, s_prob, s_score, s_rows,
 ):
     wq = wq_ref[...]
@@ -217,16 +224,33 @@
     gsv = mm(s_weight[...], rows_b[...]).astype(BF)
     projections = jnp.concatenate([wq, wk, wv], 1)
     grad_pooled = grad_state + mm_nt(jnp.concatenate([gsq, gsk, gsv], 1), projections)
-    pooled_grad_ref[...] = (grad_pooled * inverse).astype(BF)
+    share = grad_pooled * inverse
 
     gq = (near_gq_ref[...] + jnp.concatenate(gq_t, 0)).T.astype(BF)
     attended_t = (near_t_ref[...] + jnp.concatenate(out_t, 0)).astype(BF)
     pooled_t = flip(pooled)
     state_flip = flip(state)
-    weights_ref[0] = (mm(flip(x_ref[...]), gq) + mm(pooled_t, gsq)).astype(BF)
-    weights_ref[1] = (wkv_ref[0] + mm(pooled_t, gsk) + mm(state_flip, grad_ck)).astype(BF)
-    weights_ref[2] = (wkv_ref[1] + mm(pooled_t, gsv) + mm(state_flip, grad_cv)).astype(BF)
-    weights_ref[3] = mm(attended_t, grad_ref[...]).astype(BF)
+    grads = [
+        mm(flip(x_ref[...]), gq) + mm(pooled_t, gsq),
+        wkv_ref[0] + mm(pooled_t, gsk) + mm(state_flip, grad_ck),
+        wkv_ref[1] + mm(pooled_t, gsv) + mm(state_flip, grad_cv),
+        mm(attended_t, grad_ref[...]),
+    ]
+    core = core_ref[0]
+    groups = mine_ref.shape[1]
+    rows = mine_ref.shape[2]
+    first = jnp.broadcast_to(core, (groups, rows, WIDTH)) == 0
+    for w in range(4):
+        pairs = grads[w].reshape(groups, 2, rows, WIDTH)
+        low, high = pairs[:, 0], pairs[:, 1]
+        mine_ref[w] = jnp.where(first, low, high)
+        theirs_ref[w * groups * rows : (w + 1) * groups * rows] = (
+            jnp.where(first, high, low).reshape(groups * rows, WIDTH).astype(BF)
+        )
+    half = SUP // 2
+    first = jnp.broadcast_to(core, (half, WIDTH)) == 0
+    mine_pooled_ref[...] = jnp.where(first, share[:half], share[half:])
+    theirs_ref[4 * groups * rows :] = jnp.where(first, share[half:], share[:half]).astype(BF)
     nodes_ref[...] = base_ref[...] + mm_nt(gq, wq)
 
 
@@ -237,11 +261,20 @@
         out_ref[w] = jnp.sum(part, 0) * scale
 
 
+def chip_grads_body(mine_ref, mine_pooled_ref, both_ref, core_ref, weights_ref, pooled_ref):
+    received = both_ref[1 - core_ref[0]].astype(F32)
+    size = received.shape[0] - mine_pooled_ref.shape[0]
+    weights_ref[...] = (mine_ref[...] + received[:size].reshape(mine_ref.shape)).astype(BF)
+    pooled_ref[...] = (mine_pooled_ref[...] + received[size:]).astype(BF)
+
+
 def nodes_body(pieces_ref, base_ref, low_ref, high_ref, parts_ref, cluster_ref, share_ref, out_ref):
     share = jnp.sum(pieces_ref[...].astype(F32), 0).astype(BF)
     for peer in range(share_ref.shape[0]):
         share_ref[peer] = share
-    grad_pooled = jnp.sum(parts_ref[...].astype(F32), 0)
+    parts = parts_ref[...].astype(F32)
+    parts = parts.reshape(parts.shape[0] // 2, 2 * parts.shape[1], WIDTH)
+    grad_pooled = jnp.sum(parts, 0)
     coarse = grad_pooled.astype(BF)
     fine = (grad_pooled - coarse.astype(F32)).astype(BF)
     member = (cluster_ref[...] == iota((SUP, NODES), 0)).astype(F32).T.astype(BF)
@@ -265,12 +298,15 @@
     down = [(i, (i + n_super - 1) % n_super) for i in range(n_super)]
     cluster_row = cluster.reshape(1, NODES)
     (sums,) = call(
-        sums_body, "cluster_sums", [((n_super, SUM_ROWS, WIDTH), BF)], [], 1 << 22, node_feats, cluster_row
-    )
+        sums_body, "cluster_sums", [((SUM_ROWS, WIDTH), F32)], [], 1 << 22, node_feats, cluster_row
+    )
+    (sums,) = call(
+        chip_sums_body, "chip_sums", [((n_z, SUM_ROWS, WIDTH), BF)], [], 1 << 20, lax.all_gather(sums, "c")
+    )
+    core = lax.axis_index("c").reshape(1)
     low = lax.ppermute(node_feats[NODES - HALO :], supers, up)
     high = lax.ppermute(node_feats[:HALO], supers, down)
-    sums, low, high = lax.optimization_barrier((sums, low, high))
-    parts = swap(sums, supers)
+    parts = swap(sums, "z")
     q, q_t, a, a_t, near_t, near_gq, wkv, base, back_low, back_high = call(
         near_body,
         "near_attention",
@@ -289,10 +325,15 @@
     from_high = lax.ppermute(back_low, supers, down)
     from_low = lax.ppermute(back_high, supers, up)
     links = jnp.pad(super_links.T, ((0, 0), (0, NODES - SUP)))
-    weights, pooled_share, own = call(
+    share_rows = WIDTH // n_super
+    weight_rows = 4 * n_z * share_rows
+    mine, mine_pooled, theirs, own = call(
         far_body,
         "far_attention",
-        [((4, WIDTH, WIDTH), BF), ((SUP, WIDTH), BF), ((NODES, WIDTH), F32)],
+        [
+            ((4, n_z, share_rows, WIDTH), F32), ((SUP // 2, WIDTH), F32),
+            ((weight_rows + SUP // 2, WIDTH), BF), ((NODES, WIDTH), F32),
+        ],
         [
             ((WIDTH, STACK), BF), ((WIDTH, STACK), BF), ((STACK, WIDTH), BF), ((STACK, WIDTH), BF),
             ((SUP, STACK), BF), ((SUP, STACK), BF), ((SUP, STACK), BF), ((SUP, STACK), F32), ((SUP, STACK), BF),
@@ -300,10 +341,17 @@
         ],
         10 << 30,
         parts, links, node_feats, grad_out, w_query, w_key, w_value,
-        q, q_t, a, a_t, near_t, near_gq, wkv, base,
-    )
-    share_rows = WIDTH // n_super
-    pieces = swap(weights.reshape(4 * n_super, share_rows, WIDTH), ("x",) + supers)
+        q, q_t, a, a_t, near_t, near_gq, wkv, base, core,
+    )
+    weights, pooled_share = call(
+        chip_grads_body,
+        "chip_grads",
+        [((4, n_z, share_rows, WIDTH), BF), ((SUP // 2, WIDTH), BF)],
+        [],
+        1 << 20,
+        mine, mine_pooled, lax.all_gather(theirs, "c"), core,
+    )
+    pieces = swap(weights.reshape(4 * n_z, share_rows, WIDTH), ("x", "z"))
     pooled_parts = lax.all_gather(pooled_share, supers)
     shares, grad_nodes = call(
         nodes_body,

time: 102 us -> 88.4 us (0.87)
  waiting for transfers between devices: 17.7 us -> 9.92 us
  starting transfers between devices: 23.2 us -> 19.9 us
  blocking collectives: 46.6 us -> 43.9 us
    all_gather x1, blocking collectives: 23.7 us -> 17.1 us  [local(): pooled_parts = lax.all_gather(pooled_share, supers)]
    all_to_all x2, waiting for transfers between devices: 15 us -> 9.91 us  [swap(): return lax.all_to_all(parts, axes, 0, 0, tiled=True)]
    all_gather x0 -> x2, blocking collectives: none -> 4.12 us  [the longest x1 2.2 us: local(): lax.all_gather(theirs, 'c')]
    all_to_all x2, starting transfers between devices: 11.8 us -> 8.46 us  [swap(): return lax.all_to_all(parts, axes, 0, 0, tiled=True)]
    ppermute x1, waiting for transfers between devices: 2.66 us -> 0.01 us  [local(): low = lax.ppermute(node_feats[NODES - HALO:], supers, up)]
    pallas_call x5 -> x7, Pallas kernels: 11.6 us -> 11.3 us  [call(): pl.pallas_call(body, in_specs=[smem if a.ndim == 1 else vmem for a in arg...]
  transfers between devices with their start and end apart: 6 -> 6, of which waited for: 2 -> 1; matrix products, arithmetic and copies ran while one was open for 0% -> 0% of each run, Pallas kernels for 4% -> 5%
where the time goes in v2:
time: 88.4 us; the launch traced here: 87.9 us
  blocking collectives  43.9 us (50%)
  starting transfers between devices  19.9 us (23%)
  Pallas kernels  11.3 us (13%)
  waiting for transfers between devices  9.92 us (11%)
  local copies, waits for them, and re-layouts  2.09 us (2%)
    all_to_all x1, blocking collectives, swap(): return lax.all_to_all(parts, axes, 0, 0, tiled=True)  22.7 us
    all_gather x1, blocking collectives, local(): pooled_parts = lax.all_gather(pooled_share, supers)  17.1 us
    pallas_call x7, Pallas kernels, call(): pl.pallas_call(body, in_specs=[smem if a.ndim == 1 else vmem for a in arg...  11.3 us
    all_to_all x2, waiting for transfers between devices, swap(): return lax.all_to_all(parts, axes, 0, 0, tiled=True)  9.91 us
    ppermute x1, starting transfers between devices, local(): high = lax.ppermute(node_feats[:HALO], supers, down)  8.48 us
    all_to_all x2, starting transfers between devices, swap(): return lax.all_to_all(parts, axes, 0, 0, tiled=True)  8.46 us
    ppermute x1, starting transfers between devices, local(): from_high = lax.ppermute(back_low, supers, down)  2.94 us
    all_gather x1, blocking collectives, local(): lax.all_gather(theirs, 'c')  2.2 us
  transfers between devices with their start and end apart: 6, of which 1 were waited for; matrix products, arithmetic and copies ran while one was open for 0% of the time, Pallas kernels for 5%

profile of v2, /device:TPU:8, one launch (start us, length us, event | category | flops | bytes accessed | tf_op | source)
XLA Modules:
  0.0 87.9 jit_solution(18030496186960831235)
XLA Ops:
  0.6 0.0 copy-start
  0.6 0.8 fusion
  1.4 8.5 %collective-permute-start.1 = (bf16[32,256]{1,0:T(8,128)(2,1)S(1)}, bf16[32,256]{1,0:T(8,128)(2,1)S(1)}, u32[]{:S(2)}, u32[]{:S(2)}) collective-permute-start(bf16[32,256]{1,0:T(8,128)(2,1)S(1)} %get-tuple-element.38), channel_id=1, source_target_pairs={{0,15},{1,0},{2,1},{3,2},{4,3},{5,4},{6,5},{7,6},{8,7},{9,8},{10,9... | collective-permute-start | bytes 49160 | tf_op jit(solution)/shard_map/ppermute | solution.py:308
  9.9 0.0 copy-start.1
  9.9 0.0 collective-permute-start
  9.9 0.0 copy-done
  9.9 0.6 copy-done.1
  10.6 0.1 cluster_sums.1
  10.7 1.9 %all-gather = f32[160,256]{1,0:T(8,128)S(1)} all-gather(f32[80,256]{1,0:T(8,128)S(1)} %cluster_sums.1), channel_id=2, replica_groups=mesh['x'=4,'y'=8,'z'=8,'c'=2] {'c'}, dimensions={0}, use_global_device_ids=true | all-gather | bytes 245760 | tf_op jit(solution)/shard_map/all_gather | solution.py:304
  12.6 0.8 chip_sums.1
  13.4 0.0 copy-start.8
  13.4 0.0 copy-start.2
  13.4 0.0 copy-start.3
  13.4 0.0 copy-start.4
  13.4 0.0 copy-start.5
  13.4 0.0 copy-start.6
  13.4 3.8 %all-to-all-start = ((bf16[8,80,256]{2,1,0:T(8,128)(2,1)}), bf16[8,80,256]{2,1,0:T(8,128)(2,1)S(1)}, u32[]{:S(2)}, u32[]{:S(2)}) async-start(bf16[8,80,256]{2,1,0:T(8,128)(2,1)} %chip_sums.1), calls=%async_computation | async-start | bytes 655360 | tf_op jit(solution)/shard_map/all_to_all | solution.py:289
  17.2 0.0 copy-start.7
  17.2 0.0 copy-done.8
  17.2 0.0 collective-permute-done.1.high_ref
  17.2 0.0 collective-permute-done.low_ref
  17.2 0.0 copy-done.2
  17.2 0.0 copy-done.3
  17.2 0.0 copy-done.4
  17.3 0.0 copy-done.5
  17.3 0.0 copy-done.6
  17.3 0.6 copy-done.7
  17.9 3.2 %near_attention.1 = (bf16[128,256]{1,0:T(8,128)(2,1)S(1)}, bf16[256,128]{1,0:T(8,128)(2,1)S(1)}, bf16[128,256]{1,0:T(8,128)(2,1)S(1)}, bf16[256,128]{1,0:T(8,128...) custom-call(bf16[32,256]{1,0:T(8,128)(2,1)S(1)} %collective-permute-, ...), custom_call_target="tpu_custom_call" | custom-call | flops 10737418240 | bytes 704512 | tf_op jit(solution)/shard_map/near_attention/pallas_call | solution.py:67
  21.1 9.9 %all-to-all-done.parts_ref = bf16[8,80,256]{2,1,0:T(8,128)(2,1)S(1)} async-done(((bf16[8,80,256]{2,1,0:T(8,128)(2,1)}), bf16[8,80,256]{2,1,0:T(8,128)(2,1)S(1)}, u32[]{:S(2)}, u32[]{:S(2)}) %all-to-all-start) | async-done | bytes 327712 | tf_op jit(solution)/shard_map/all_to_all | solution.py:289
  31.0 4.9 %far_attention.1 = (f32[4,8,16,256]{3,2,1,0:T(8,128)S(1)}, f32[32,256]{1,0:T(8,128)S(1)}, bf16[544,256]{1,0:T(8,128)(2,1)S(1)}, f32[128,256]{1,0:T(8,128)S(1)}) custom-call(bf16[8,80,256]{2,1,0:T(8,128)(2,1)S(1)} %all-to-all-done.parts_ref, s32[8,128]{1,0:T(8,128)S(1)} %pad.4.links_ref, bf16[128,256]{1,0:T(8,128)(2,1)S(1)} %copy-done, ...), custom_call_target="tpu_custom_call" | custom-call | flops 10737418240 | bytes 2035716 | tf_op jit(solution)/shard_map/far_attention/pallas_call | solution.py:67
  35.9 2.2 %all-gather.1 = bf16[1088,256]{1,0:T(8,128)(2,1)S(1)} all-gather(bf16[544,256]{1,0:T(8,128)(2,1)S(1)} %get-tuple-element.30), channel_id=3, replica_groups=mesh['x'=4,'y'=8,'z'=8,'c'=2] {'c'}, dimensions={0}, use_global_device_ids=true | all-gather | bytes 835584 | tf_op jit(solution)/shard_map/all_gather | solution.py:352
  38.1 0.8 chip_grads.1
  38.9 4.7 %all-to-all-start.1 = ((bf16[32,16,256]{2,1,0:T(8,128)(2,1)}), bf16[32,16,256]{2,1,0:T(8,128)(2,1)S(1)}, u32[]{:S(2)}, u32[]{:S(2)}) async-start(bf16[32,16,256]{2,1,0:T(8,128)(2,1)} %bitcast.6), calls=%async_computation.1 | async-start | bytes 524288 | tf_op jit(solution)/shard_map/all_to_all | solution.py:289
  43.6 0.0 collective-permute-start.2
  43.6 2.9 %collective-permute-start.3 = (bf16[32,256]{1,0:T(8,128)(2,1)S(1)}, bf16[32,256]{1,0:T(8,128)(2,1)S(1)}, u32[]{:S(2)}, u32[]{:S(2)}) collective-permute-start(bf16[32,256]{1,0:T(8,128)(2,1)S(1)} %get-tuple-element.34), channel_id=1, source_target_pairs={{0,15},{1,0},{2,1},{3,2},{4,3},{5,4},{6,5},{7,6},{8,7},{9,8},{10,9... | collective-permute-start | bytes 49160 | tf_op jit(solution)/shard_map/ppermute | solution.py:325
  46.5 17.1 %all-gather.2 = bf16[512,256]{1,0:T(8,128)(2,1)S(1)} all-gather(bf16[32,256]{1,0:T(8,128)(2,1)S(1)} %get-tuple-element.35), channel_id=4, replica_groups=mesh['x'=4,'y'=8,'z'=8,'c'=2] {'z','c'}, dimensions={0}, use_global_device_ids=true | all-gather | bytes 278528 | tf_op jit(solution)/shard_map/all_gather | solution.py:355
  63.6 0.0 collective-permute-done.2.low_ref
  63.6 0.0 collective-permute-done.3.high_ref
  63.6 0.0 all-to-all-done.1.pieces_ref
  63.6 0.9 %grad_nodes.1 = (bf16[32,16,256]{2,1,0:T(8,128)(2,1)S(1)}, bf16[128,256]{1,0:T(8,128)(2,1)}) custom-call(bf16[32,16,256]{2,1,0:T(8,128)(2,1)S(1)} %all-to-all-done.1.pieces_ref, f32[128,256]{1,0:T(8,128)S(1)} %get-tuple-element.32.base_ref, bf16[32,256]{1,0:T(8,128)(2,1)S(1)} %collective-permute-done.2.low_ref, ...), custom_call_target="tpu_custom_call" | custom-call | flops 1073741824 | bytes 688640 | tf_op jit(solution)/shard_map/grad_nodes/pallas_call | solution.py:67
  64.6 22.7 %all_to_all.15.parts_ref = bf16[32,16,256]{2,1,0:T(8,128)(2,1)S(1)} all-to-all(bf16[32,16,256]{2,1,0:T(8,128)(2,1)S(1)} %get-tuple-element.37), channel_id=1, replica_groups=mesh['x'=4,'y'=8,'z'=8,'c'=2] {'x','y'}, dimensions={0} | all-to-all | bytes 524288 | tf_op jit(solution)/shard_map/all_to_all | solution.py:289
  87.3 0.7 grad_weights.1
  (1 shorter events, 0.0 us)
Async XLA Ops:
  0.6 9.3 %copy-start = (bf16[128,256]{1,0:T(8,128)(2,1)S(1)}, bf16[128,256]{1,0:T(8,128)(2,1)}, u32[]{:S(2)}) copy-start(bf16[128,256]{1,0:T(8,128)(2,1)} %x_ref.5) | copy-start | bytes 196612
  1.4 15.8 %collective-permute-start.1 = (bf16[32,256]{1,0:T(8,128)(2,1)S(1)}, bf16[32,256]{1,0:T(8,128)(2,1)S(1)}, u32[]{:S(2)}, u32[]{:S(2)}) collective-permute-start(bf16[32,256]{1,0:T(8,128)(2,1)S(1)} %get-tuple-element.38), channel_id=1, source_target_pairs={{0,15},{1,0},{2,1},{3,2},{4,3},{5,4},{6,5},{7,6},{8,7},{9,8},{10,9... | collective-permute-start | bytes 49160 | tf_op jit(solution)/shard_map/ppermute | solution.py:308
  9.9 0.7 copy-start.1
  9.9 7.3 %collective-permute-start = (bf16[32,256]{1,0:T(8,128)(2,1)S(1)}, bf16[32,256]{1,0:T(8,128)(2,1)S(1)}, u32[]{:S(2)}, u32[]{:S(2)}) collective-permute-start(bf16[32,256]{1,0:T(8,128)(2,1)S(1)} %get-tuple-element.39), channel_id=1, source_target_pairs={{0,1},{1,2},{2,3},{3,4},{4,5},{5,6},{6,7},{7,8},{8,9},{9,10},{10,1... | collective-permute-start | bytes 49160 | tf_op jit(solution)/shard_map/ppermute | solution.py:307
  13.4 3.8 %copy-start.8 = (s32[64,8]{0,1:T(8,128)S(1)}, s32[64,8]{0,1:T(8,128)}, u32[]{:S(2)}) copy-start(s32[64,8]{0,1:T(8,128)} %param.13) | copy-start | bytes 6148
  13.4 3.9 %copy-start.2 = (bf16[256,256]{1,0:T(8,128)(2,1)S(1)}, bf16[256,256]{1,0:T(8,128)(2,1)}, u32[]{:S(2)}) copy-start(bf16[256,256]{1,0:T(8,128)(2,1)} %wo_ref.1) | copy-start | bytes 393220
  13.4 3.9 %copy-start.3 = (bf16[256,256]{1,0:T(8,128)(2,1)S(1)}, bf16[256,256]{1,0:T(8,128)(2,1)}, u32[]{:S(2)}) copy-start(bf16[256,256]{1,0:T(8,128)(2,1)} %wq_ref.3) | copy-start | bytes 393220
  13.4 3.9 %copy-start.4 = (bf16[256,256]{1,0:T(8,128)(2,1)S(1)}, bf16[256,256]{1,0:T(8,128)(2,1)}, u32[]{:S(2)}) copy-start(bf16[256,256]{1,0:T(8,128)(2,1)} %wk_ref.3) | copy-start | bytes 393220
  13.4 3.9 %copy-start.5 = (bf16[256,256]{1,0:T(8,128)(2,1)S(1)}, bf16[256,256]{1,0:T(8,128)(2,1)}, u32[]{:S(2)}) copy-start(bf16[256,256]{1,0:T(8,128)(2,1)} %wv_ref.3) | copy-start | bytes 393220
  13.4 3.9 %copy-start.6 = (bf16[128,256]{1,0:T(8,128)(2,1)S(1)}, bf16[128,256]{1,0:T(8,128)(2,1)}, u32[]{:S(2)}) copy-start(bf16[128,256]{1,0:T(8,128)(2,1)} %grad_ref.3) | copy-start | bytes 196612
  13.4 17.6 %all-to-all-start = ((bf16[8,80,256]{2,1,0:T(8,128)(2,1)}), bf16[8,80,256]{2,1,0:T(8,128)(2,1)S(1)}, u32[]{:S(2)}, u32[]{:S(2)}) async-start(bf16[8,80,256]{2,1,0:T(8,128)(2,1)} %chip_sums.1), calls=%async_computation | async-start | bytes 655360 | tf_op jit(solution)/shard_map/all_to_all | solution.py:289
  17.2 0.7 copy-start.7
  38.9 24.8 %all-to-all-start.1 = ((bf16[32,16,256]{2,1,0:T(8,128)(2,1)}), bf16[32,16,256]{2,1,0:T(8,128)(2,1)S(1)}, u32[]{:S(2)}, u32[]{:S(2)}) async-start(bf16[32,16,256]{2,1,0:T(8,128)(2,1)} %bitcast.6), calls=%async_computation.1 | async-start | bytes 524288 | tf_op jit(solution)/shard_map/all_to_all | solution.py:289
  43.6 20.0 %collective-permute-start.2 = (bf16[32,256]{1,0:T(8,128)(2,1)S(1)}, bf16[32,256]{1,0:T(8,128)(2,1)S(1)}, u32[]{:S(2)}, u32[]{:S(2)}) collective-permute-start(bf16[32,256]{1,0:T(8,128)(2,1)S(1)} %get-tuple-element.33), channel_id=1, source_target_pairs={{0,1},{1,2},{2,3},{3,4},{4,5},{5,6},{6,7},{7,8},{8,9},{9,10},{10,1... | collective-permute-start | bytes 49160 | tf_op jit(solution)/shard_map/ppermute | solution.py:326
  43.6 20.0 %collective-permute-start.3 = (bf16[32,256]{1,0:T(8,128)(2,1)S(1)}, bf16[32,256]{1,0:T(8,128)(2,1)S(1)}, u32[]{:S(2)}, u32[]{:S(2)}) collective-permute-start(bf16[32,256]{1,0:T(8,128)(2,1)S(1)} %get-tuple-element.34), channel_id=1, source_target_pairs={{0,15},{1,0},{2,1},{3,2},{4,3},{5,4},{6,5},{7,6},{8,7},{9,8},{10,9... | collective-permute-start | bytes 49160 | tf_op jit(solution)/shard_map/ppermute | solution.py:325

commit v3 on v2

v3 whole, which is shorter than its diff:
```python
import functools
import math

import jax
import jax.numpy as jnp
from jax import lax
from jax.experimental import pallas as pl
from jax.experimental.pallas import tpu as pltpu
from jax.sharding import Mesh, PartitionSpec as P

WIDTH = 256
HEADS = 8
HEAD_DIM = 32
NODES = 128
HALO = 32
EXT = NODES + 2 * HALO
SUP = 64
SUM_ROWS = SUP + 8
STACK = HEADS * NODES
SCORE_SCALE = 1.0 / math.sqrt(HEAD_DIM)
NEVER = -1e30
BF = jnp.bfloat16
F32 = jnp.float32


def mm(a, b):
    return jnp.dot(a, b, preferred_element_type=F32)


def mm_nt(a, b):
    return lax.dot_general(a, b, (((1,), (1,)), ((), ())), preferred_element_type=F32)


def iota(shape, dim):
    return lax.broadcasted_iota(jnp.int32, shape, dim)


def flip(a):
    return a.astype(F32).T.astype(a.dtype)


def rows_of(h):
    return slice(h * HEAD_DIM, (h + 1) * HEAD_DIM)


def lanes_of(h):
    return slice(h * NODES, (h + 1) * NODES)


def stack_lanes(ref, flipped):
    ref[...] = jnp.zeros(ref.shape, ref.dtype)
    for h in range(HEADS):
        ref[rows_of(h), lanes_of(h)] = flipped[rows_of(h)]


def stack_rows(ref, rows):
    head = lax.shift_right_logical(iota(rows.shape, 1), 5)
    wide = rows.astype(F32)
    for h in range(HEADS):
        ref[lanes_of(h), :] = jnp.where(head == h, wide, 0.0).astype(rows.dtype)


def call(body, name, outs, scratch, flops, *args, outside=()):
    size = sum(a.size * a.dtype.itemsize for a in args)
    vmem = pl.BlockSpec(memory_space=pltpu.VMEM)
    smem = pl.BlockSpec(memory_space=pltpu.SMEM)
    anywhere = pl.BlockSpec(memory_space=pltpu.HBM)
    return pl.pallas_call(
        body,
        in_specs=[anywhere if i in outside else smem if a.ndim == 1 else vmem for i, a in enumerate(args)],
        name=name,
        out_shape=tuple(jax.ShapeDtypeStruct(s, d) for s, d in outs),
        scratch_shapes=[pltpu.VMEM(*s) if isinstance(s, tuple) else s for s in scratch],
        compiler_params=pltpu.CompilerParams(vmem_limit_bytes=32 * 1024 * 1024),
        cost_estimate=pl.CostEstimate(flops=flops, bytes_accessed=size, transcendentals=0),
    )(*args)


def sums_body(x_any, cluster_any, out_ref, low_ref, high_ref, x_ref, cluster_ref, sems):
    copies = [
        pltpu.make_async_copy(cluster_any, cluster_ref, sems.at[0]),
        pltpu.make_async_copy(x_any, x_ref, sems.at[1]),
    ]
    for copy in copies:
        copy.start()
    for copy in copies:
        copy.wait()
    member = (cluster_ref[...] == iota((SUP, NODES), 0)).astype(F32)
    sums = mm(member.astype(BF), x_ref[...])
    counts = jnp.sum(member, 1, keepdims=True)
    diagonal = iota((SUP, WIDTH), 0) == iota((SUP, WIDTH), 1)
    count_row = jnp.sum(jnp.where(diagonal, counts, 0.0), 0, keepdims=True)
    out_ref[:SUP] = sums
    out_ref[SUP:] = jnp.broadcast_to(count_row, (SUM_ROWS - SUP, WIDTH))
    low_ref[...] = x_ref[:HALO]
    high_ref[...] = x_ref[NODES - HALO :]


def chip_sums_body(parts_ref, out_ref):
    total = (parts_ref[0] + parts_ref[1]).astype(BF)
    for peer in range(out_ref.shape[0]):
        out_ref[peer] = total


def near_body(
    low_ref, x_ref, high_ref, grad_ref, slots_ref, links_ref, core_ref, wq_ref, wk_ref, wv_ref, wo_ref,
    qt_ref, at_ref, xt_ref, wt_ref, out_t_ref, gq_t_ref, wkv_ref, base_ref, allowed_ref, inner_ref, outer_ref,
    q_lanes, a_lanes, q_rows, a_rows, weight_all, score_all,
):
    ext = jnp.concatenate([low_ref[...], x_ref[...], high_ref[...]], 0)
    wk = wk_ref[...]
    wv = wv_ref[...]
    queries = mm(x_ref[...], wq_ref[...]).astype(BF)
    keys = mm(ext, wk).astype(BF)
    vals = mm(ext, wv).astype(BF)
    grad_attn = mm_nt(grad_ref[...], wo_ref[...]).astype(BF)
    q_t = flip(queries)
    a_t = flip(grad_attn)
    keys_t = flip(keys)
    vals_t = flip(vals)
    qt_ref[...] = q_t
    at_ref[...] = a_t
    stack_lanes(q_lanes, q_t)
    stack_lanes(a_lanes, a_t)
    stack_rows(q_rows, queries)
    stack_rows(a_rows, grad_attn)
    slots = slots_ref[...]
    row = iota((EXT, NODES), 0)
    count = jnp.zeros((EXT, NODES), F32)
    for j in range(slots.shape[0]):
        count = count + jnp.where(slots[j : j + 1] == row, 1.0, 0.0)
    log_count = jnp.where(count > 0.0, jnp.log(jnp.maximum(count, 1.0)), NEVER)
    for h in range(HEADS):
        score = mm(keys, q_lanes[:, lanes_of(h)])
        e = jnp.exp(score * SCORE_SCALE + log_count)
        prob = e * (1.0 / jnp.sum(e, 0, keepdims=True))
        weight = prob.astype(BF)
        g = mm(vals, a_lanes[:, lanes_of(h)])
        centre = jnp.sum(prob * g, 0, keepdims=True)
        d_score = (prob * (g - centre) * SCORE_SCALE).astype(BF)
        weight_all[:, lanes_of(h)] = weight
        score_all[:, lanes_of(h)] = d_score
        out_t_ref[rows_of(h)] = mm(vals_t[rows_of(h)], weight)
        gq_t_ref[rows_of(h)] = mm(keys_t[rows_of(h)], d_score)
    grad_keys = mm(score_all[...], q_rows[...]).astype(BF)
    grad_vals = mm(weight_all[...], a_rows[...]).astype(BF)
    ext_t = flip(ext)
    xt_ref[...] = ext_t[:, HALO : HALO + NODES]
    wt_ref[:WIDTH] = flip(wq_ref[...])
    wt_ref[WIDTH : 2 * WIDTH] = flip(wk)
    wt_ref[2 * WIDTH :] = flip(wv)
    wkv_ref[0] = mm(ext_t, grad_keys)
    wkv_ref[1] = mm(ext_t, grad_vals)
    back = mm_nt(grad_keys, wk) + mm_nt(grad_vals, wv)
    base_ref[...] = grad_ref[...].astype(F32) + back[HALO : HALO + NODES]
    below, above = back[:HALO], back[HALO + NODES :]
    first = jnp.broadcast_to(core_ref[0], below.shape) == 0
    inner_ref[...] = jnp.where(first, above, below).astype(BF)
    outer_ref[...] = jnp.where(first, below, above).astype(BF)
    links = links_ref[...]
    target = iota((SUP, SUP), 0)
    linked = links[:1] == target
    for l in range(1, links.shape[0]):
        linked = jnp.logical_or(linked, links[l : l + 1] == target)
    allowed_ref[...] = jnp.where(linked, 0.0, NEVER)


def softmax_rows(scores):
    e = jnp.exp(scores)
    return e * (1.0 / jnp.sum(e, 0, keepdims=True))


def score_grad(prob, g):
    return (prob * (g - jnp.sum(prob * g, 0, keepdims=True)) * SCORE_SCALE).astype(BF)


def far_body(
    parts_ref, allowed_ref, grad_ref, wq_ref, wk_ref, wv_ref, wt_ref,
    qt_ref, at_ref, xt_ref, near_t_ref, near_gq_ref, wkv_ref, inner_ref, core_ref,
    mine_ref, mine_pooled_ref, theirs_ref, gq_t_ref,
):
    heads = [rows_of(h) for h in range(HEADS)]
    wq = wq_ref[...]
    wk = wk_ref[...]
    wv = wv_ref[...]
    wt = wt_ref[...]
    totals = jnp.sum(parts_ref[...].astype(F32), 0)
    diagonal = iota((SUP, WIDTH), 0) == iota((SUP, WIDTH), 1)
    counts = jnp.sum(jnp.where(diagonal, totals[SUP : SUP + 1], 0.0), 1, keepdims=True)
    inverse = 1.0 / jnp.maximum(counts, 1.0)
    pooled = (totals[:SUP] * inverse).astype(BF)
    pooled_t = flip(pooled)

    s_proj_t = mm(wt, pooled_t).astype(BF)
    s_qt, s_kt, s_vt = (s_proj_t[i * WIDTH : (i + 1) * WIDTH] for i in range(3))
    s_k = mm(pooled, wk).astype(BF)
    s_v = mm(pooled, wv).astype(BF)
    allowed = allowed_ref[...]
    s_prob = [softmax_rows(mm(s_k[:, h], s_qt[h]) * SCORE_SCALE + allowed) for h in heads]
    s_weight = [p.astype(BF) for p in s_prob]
    moved_t = jnp.concatenate([mm(s_vt[h], w) for h, w in zip(heads, s_weight)], 0)
    state_t = (pooled_t.astype(F32) + moved_t).astype(BF)
    state = flip(state_t)

    c_proj_t = mm(wt[WIDTH:], state_t).astype(BF)
    c_kt, c_vt = c_proj_t[:WIDTH], c_proj_t[WIDTH:]
    c_k = mm(state, wk).astype(BF)
    c_v = mm(state, wv).astype(BF)
    q_t = qt_ref[...]
    a_t = at_ref[...]
    out_t = []
    gq_t = []
    gck_t = []
    gcv_t = []
    for h in heads:
        prob = softmax_rows(mm(c_k[:, h], q_t[h]) * SCORE_SCALE)
        weight = prob.astype(BF)
        d_score = score_grad(prob, mm(c_v[:, h], a_t[h]))
        out_t.append(mm(c_vt[h], weight))
        gq_t.append(mm(c_kt[h], d_score))
        gck_t.append(mm_nt(q_t[h], d_score))
        gcv_t.append(mm_nt(a_t[h], weight))
    gck_t = jnp.concatenate(gck_t, 0).astype(BF)
    gcv_t = jnp.concatenate(gcv_t, 0).astype(BF)

    grad_state_t = mm(jnp.concatenate([wk, wv], 1), jnp.concatenate([gck_t, gcv_t], 0))
    gs_t = grad_state_t.astype(BF)
    gsq_t = []
    gsk_t = []
    gsv_t = []
    for h, prob, weight in zip(heads, s_prob, s_weight):
        d_score = score_grad(prob, mm(s_v[:, h], gs_t[h]))
        gsq_t.append(mm(s_kt[h], d_score))
        gsk_t.append(mm_nt(s_qt[h], d_score))
        gsv_t.append(mm_nt(gs_t[h], weight))
    gsq_t = jnp.concatenate(gsq_t, 0).astype(BF)
    gsk_t = jnp.concatenate(gsk_t, 0).astype(BF)
    gsv_t = jnp.concatenate(gsv_t, 0).astype(BF)
    grad_pooled_t = grad_state_t + mm(
        jnp.concatenate([wq, wk, wv], 1), jnp.concatenate([gsq_t, gsk_t, gsv_t], 0)
    )
    share = grad_pooled_t.T * inverse

    gq_t = (near_gq_ref[...] + jnp.concatenate(gq_t, 0)).astype(BF)
    gq_t_ref[...] = gq_t
    attended_t = (near_t_ref[...] + jnp.concatenate(out_t, 0)).astype(BF)
    grads = [
        mm_nt(xt_ref[...], gq_t) + mm_nt(pooled_t, gsq_t),
        wkv_ref[0] + mm_nt(jnp.concatenate([pooled_t, state_t], 1), jnp.concatenate([gsk_t, gck_t], 1)),
        wkv_ref[1] + mm_nt(jnp.concatenate([pooled_t, state_t], 1), jnp.concatenate([gsv_t, gcv_t], 1)),
        mm(attended_t, grad_ref[...]),
    ]
    core = core_ref[0]
    groups = mine_ref.shape[1]
    rows = mine_ref.shape[2]
    first = jnp.broadcast_to(core, (groups, rows, WIDTH)) == 0
    for w in range(4):
        pairs = grads[w].reshape(groups, 2, rows, WIDTH)
        low, high = pairs[:, 0], pairs[:, 1]
        mine_ref[w] = jnp.where(first, low, high)
        theirs_ref[w * groups * rows : (w + 1) * groups * rows] = (
            jnp.where(first, high, low).reshape(groups * rows, WIDTH).astype(BF)
        )
    half = SUP // 2
    first = jnp.broadcast_to(core, (half, WIDTH)) == 0
    mine_pooled_ref[...] = jnp.where(first, share[:half], share[half:])
    end = 4 * groups * rows + half
    theirs_ref[4 * groups * rows : end] = jnp.where(first, share[half:], share[:half]).astype(BF)
    theirs_ref[end:] = inner_ref[...]


def own_body(base_ref, gq_t_ref, wq_ref, inner_ref, outer_ref, core_ref, out_ref):
    own = base_ref[...] + mm_nt(flip(gq_t_ref[...]), wq_ref[...])
    inner, outer = inner_ref[...].astype(F32), outer_ref[...].astype(F32)
    first = jnp.broadcast_to(core_ref[0], inner.shape) == 0
    out_ref[:HALO] = own[:HALO] + jnp.where(first, outer, inner)
    out_ref[HALO : NODES - HALO] = own[HALO : NODES - HALO]
    out_ref[NODES - HALO :] = own[NODES - HALO :] + jnp.where(first, inner, outer)


def chip_grads_body(mine_ref, mine_pooled_ref, both_ref, core_ref, out_ref, inner_ref):
    received = both_ref[1 - core_ref[0]].astype(F32)
    n_w, n_z, rows, _ = mine_ref.shape
    size = n_w * n_z * rows
    weights = mine_ref[...] + received[:size].reshape(mine_ref.shape)
    pooled = mine_pooled_ref[...] + received[size : size + mine_pooled_ref.shape[0]]
    inner_ref[...] = received[size + mine_pooled_ref.shape[0] :].astype(BF)
    quarter = pooled.shape[0] // n_w
    for w in range(n_w):
        piece = pooled[w * quarter : (w + 1) * quarter]
        for z in range(n_z):
            out_ref[w * n_z + z] = jnp.concatenate([weights[w, z], piece], 0).astype(BF)


def shares_body(n_w, pieces_ref, own_ref, out_ref, pooled_ref):
    n_z = pieces_ref.shape[0] // n_w
    sums = [jnp.sum(pieces_ref[w * n_z : (w + 1) * n_z].astype(F32), 0) for w in range(n_w)]
    rows = out_ref.shape[1]
    share = sum(part[:rows] for part in sums).astype(BF)
    for y in range(out_ref.shape[0]):
        out_ref[y] = share
    pooled_ref[...] = jnp.concatenate([part[rows:] for part in sums], 0).astype(BF)


def columns_body(parts_ref, pooled_ref, out_ref):
    share = jnp.sum(parts_ref[...].astype(F32), 0)
    pooled = pooled_ref[...].astype(F32)
    n_w = out_ref.shape[0]
    quarter = pooled.shape[1] // n_w
    for w in range(n_w):
        rows = slice(w * quarter, (w + 1) * quarter)
        out_ref[w] = jnp.concatenate([share, pooled[0, rows], pooled[1, rows]], 0).astype(BF)


def final_body(scale, parts_ref, own_ref, cluster_ref, weights_ref, nodes_ref):
    n_w, rows, _ = weights_ref.shape
    quarter = (parts_ref.shape[1] - rows) // 2
    parts = parts_ref[...].astype(F32)
    weights_ref[...] = parts[:, :rows] * scale
    halves = [parts[w, rows + c * quarter : rows + (c + 1) * quarter] for c in range(2) for w in range(n_w)]
    pooled = jnp.concatenate(halves, 0).astype(BF)
    member = (cluster_ref[...] == iota((SUP, NODES), 0)).astype(F32).T.astype(BF)
    nodes_ref[...] = (own_ref[...] + mm(member, pooled)).astype(BF)


def swap(parts, axes):
    return lax.all_to_all(parts, axes, 0, 0, tiled=True)


def local(sizes, node_feats, grad_out, neighbours, cluster, super_links, w_query, w_key, w_value, w_out):
    n_x, n_y, n_z, n_c = sizes
    n_super = n_z * n_c
    n_dom = n_x * n_y
    supers = ("z", "c")
    up = [(i, (i + 1) % n_super) for i in range(n_super)]
    down = [(i, (i + n_super - 1) % n_super) for i in range(n_super)]
    cluster_row = cluster.reshape(1, NODES)
    sums, first_rows, last_rows = call(
        sums_body,
        "cluster_sums",
        [((SUM_ROWS, WIDTH), F32), ((HALO, WIDTH), BF), ((HALO, WIDTH), BF)],
        [((NODES, WIDTH), BF), ((1, NODES), jnp.int32), pltpu.SemaphoreType.DMA((2,))],
        1 << 22,
        node_feats, cluster_row,
        outside=(0, 1),
    )
    (sums,) = call(
        chip_sums_body, "chip_sums", [((n_z, SUM_ROWS, WIDTH), BF)], [], 1 << 20, lax.all_gather(sums, "c")
    )
    core = lax.axis_index("c").reshape(1)
    low = lax.ppermute(last_rows, supers, up)
    high = lax.ppermute(first_rows, supers, down)
    parts = swap(sums, "z")
    q_t, a_t, x_t, w_t, near_t, near_gq, wkv, base, allowed, inner, outer = call(
        near_body,
        "near_attention",
        [
            ((WIDTH, NODES), BF), ((WIDTH, NODES), BF), ((WIDTH, NODES), BF), ((3 * WIDTH, WIDTH), BF),
            ((WIDTH, NODES), F32), ((WIDTH, NODES), F32), ((2, WIDTH, WIDTH), F32), ((NODES, WIDTH), F32),
            ((SUP, SUP), F32), ((HALO, WIDTH), BF), ((HALO, WIDTH), BF),
        ],
        [
            ((WIDTH, STACK), BF), ((WIDTH, STACK), BF), ((STACK, WIDTH), BF), ((STACK, WIDTH), BF),
            ((EXT, STACK), BF), ((EXT, STACK), BF),
        ],
        10 << 30,
        low, node_feats, high, grad_out, neighbours.T, super_links.T, core, w_query, w_key, w_value, w_out,
    )
    outward = [(2 * z, (2 * z - 1) % n_super) for z in range(n_z)]
    outward += [(2 * z + 1, (2 * z + 2) % n_super) for z in range(n_z)]
    outer = lax.ppermute(outer, supers, outward)
    share_rows = WIDTH // n_super
    weight_rows = 4 * n_z * share_rows
    half = (SUP // 2, WIDTH)
    mine, mine_pooled, theirs, gq_t = call(
        far_body,
        "far_attention",
        [
            ((4, n_z, share_rows, WIDTH), F32), (half, F32), ((weight_rows + SUP // 2 + HALO, WIDTH), BF),
            ((WIDTH, NODES), BF),
        ],
        [],
        10 << 30,
        parts, allowed, grad_out, w_query, w_key, w_value, w_t,
        q_t, a_t, x_t, near_t, near_gq, wkv, inner, core,
    )
    message_rows = share_rows + SUP // 2 // n_x
    pieces, inner = call(
        chip_grads_body,
        "chip_grads",
        [((n_x * n_z, message_rows, WIDTH), BF), ((HALO, WIDTH), BF)],
        [],
        1 << 20,
        mine, mine_pooled, lax.all_gather(theirs, "c"), core,
    )
    pieces = swap(pieces, ("x", "z"))
    (own,) = call(
        own_body, "own_nodes", [((NODES, WIDTH), F32)], [], 1 << 28, base, gq_t, w_query, inner, outer, core
    )
    shares, pooled = call(
        functools.partial(shares_body, n_x),
        "weight_shares",
        [((n_y, share_rows, WIDTH), BF), (half, BF)],
        [],
        1 << 20,
        pieces, own,
        outside=(1,),
    )
    shares = swap(shares, "y")
    (columns,) = call(
        columns_body,
        "weight_columns",
        [((n_x, message_rows + SUP // 2 // n_x, WIDTH), BF)],
        [],
        1 << 20,
        shares, lax.all_gather(pooled, "c"),
    )
    columns = swap(columns, "x")
    scale = 1.0 / math.sqrt(NODES * n_super * n_dom)
    grad_weights, grad_nodes = call(
        functools.partial(final_body, scale),
        "gradients",
        [((4, share_rows, WIDTH), F32), ((NODES, WIDTH), BF)],
        [],
        1 << 20,
        columns, own, cluster_row,
    )
    return grad_nodes, grad_weights


def solution(mesh):
    n_dom = mesh.shape["dom"]
    n_super = mesh.shape["super"]
    sizes = (4, n_dom // 4, n_super // 2, 2)
    fine = Mesh(mesh.devices.reshape(sizes), ("x", "y", "z", "c"))
    everyone = ("x", "y", "z", "c")
    return jax.shard_map(
        functools.partial(local, sizes),
        mesh=fine,
        in_specs=(
            P(everyone, None),
            P(everyone, None),
            P(everyone, None),
            P(everyone),
            P(("x", "y"), None),
            P(),
            P(),
            P(),
            P(),
        ),
        out_specs=(P(everyone, None), P(None, ("z", "c"), None)),
        check_vma=False,
    )
```

time: 88.4 us -> 83.8 us (0.948)
  the two profiles are of different devices: /device:TPU:8 before, /device:TPU:64 now
where the time goes in v3:
time: 83.8 us; the launch traced here: 83.3 us
  starting transfers between devices  27.6 us (33%)
  waiting for transfers between devices  27.3 us (33%)
  blocking collectives  14.4 us (17%)
  Pallas kernels  11.1 us (13%)
  local copies, waits for them, and re-layouts  2.12 us (3%)
    all_to_all x3, starting transfers between devices, swap(): return lax.all_to_all(parts, axes, 0, 0, tiled=True)  23.9 us
    all_to_all x3, waiting for transfers between devices, swap(): return lax.all_to_all(parts, axes, 0, 0, tiled=True)  20.5 us
    pallas_call x9, Pallas kernels, call(): pl.pallas_call(body, in_specs=[anywhere if i in outside else smem if a.nd...  11.1 us
    all_to_all x1, blocking collectives, swap(): return lax.all_to_all(parts, axes, 0, 0, tiled=True)  8.06 us
    ppermute x1, waiting for transfers between devices, local(): outer = lax.ppermute(outer, supers, outward)  6.77 us
    all_gather x1, blocking collectives, local(): lax.all_gather(sums, 'c')  2.29 us
    all_gather x1, blocking collectives, local(): lax.all_gather(theirs, 'c')  2.23 us
    unnamed x20, local copies, waits for them, and re-layouts  2.12 us
  transfers between devices with their start and end apart: 6, of which 4 were waited for; matrix products, arithmetic and copies ran while one was open for 0% of the time, Pallas kernels for 5%

profile of v3, /device:TPU:64, one launch (start us, length us, event | category | flops | bytes accessed | tf_op | source)
XLA Modules:
  0.0 83.3 jit_solution(1386067274471539307)
XLA Ops:
  0.6 0.0 copy-start.2
  0.6 0.6 copy-done.2
  1.3 0.0 copy-start
  1.3 0.8 %copy-done = bf16[128,256]{1,0:T(8,128)(2,1)S(1)} copy-done((bf16[128,256]{1,0:T(8,128)(2,1)S(1)}, bf16[128,256]{1,0:T(8,128)(2,1)}, u32[]{:S(2)}) %copy-start) | copy-done | bytes 65560
  2.1 0.2 cluster_sums.1
  2.4 0.0 collective-permute-start
  2.4 1.7 %collective-permute-start.1 = (bf16[32,256]{1,0:T(8,128)(2,1)S(1)}, bf16[32,256]{1,0:T(8,128)(2,1)S(1)}, u32[]{:S(2)}, u32[]{:S(2)}) collective-permute-start(bf16[32,256]{1,0:T(8,128)(2,1)S(1)} %get-tuple-element.28), channel_id=1, source_target_pairs={{0,15},{1,0},{2,1},{3,2},{4,3},{5,4},{6,5},{7,6},{8,7},{9,8},{10,9... | collective-permute-start | bytes 49160 | tf_op jit(solution)/shard_map/ppermute | solution.py:352
  4.1 2.3 %all-gather = f32[144,256]{1,0:T(8,128)S(1)} all-gather(f32[72,256]{1,0:T(8,128)S(1)} %get-tuple-element.26), channel_id=2, replica_groups=mesh['x'=4,'y'=8,'z'=8,'c'=2] {'c'}, dimensions={0}, use_global_device_ids=true | all-gather | bytes 221184 | tf_op jit(solution)/shard_map/all_gather | solution.py:348
  6.4 0.0 copy-start.7
  6.4 0.0 copy-start.8
  6.4 0.7 chip_sums.1
  7.1 0.0 copy-start.1
  7.1 0.0 copy-start.3
  7.1 0.0 copy-start.4
  7.1 0.0 copy-start.5
  7.2 0.0 copy-start.6
  7.2 10.9 %all-to-all-start = ((bf16[8,72,256]{2,1,0:T(8,128)(2,1)}), bf16[8,72,256]{2,1,0:T(8,128)(2,1)S(1)}, u32[]{:S(2)}, u32[]{:S(2)}) async-start(bf16[8,72,256]{2,1,0:T(8,128)(2,1)} %chip_sums.1), calls=%async_computation | async-start | bytes 589824 | tf_op jit(solution)/shard_map/all_to_all | solution.py:327
  18.1 0.0 copy-start.9
  18.1 0.0 collective-permute-done.low_ref
  18.1 0.0 collective-permute-done.1.high_ref
  18.1 0.0 copy-done.7
  18.1 0.0 copy-done.8
  18.1 0.0 copy-done.1
  18.1 0.0 copy-done.3
  18.1 0.0 copy-done.4
  18.1 0.0 copy-done.5
  18.1 0.0 copy-done.6
  18.2 0.6 copy-done.9
  18.7 3.2 %near_attention.1 = (bf16[256,128]{1,0:T(8,128)(2,1)S(1)}, bf16[256,128]{1,0:T(8,128)(2,1)S(1)}, bf16[256,128]{1,0:T(8,128)(2,1)S(1)}, bf16[768,256]{1,0:T(8,128...) custom-call(bf16[32,256]{1,0:T(8,128)(2,1)S(1)} %collective-permute-, ...), custom_call_target="tpu_custom_call" | custom-call | flops 10737418240 | bytes 706564 | tf_op jit(solution)/shard_map/near_attention/pallas_call | solution.py:68
  22.0 7.6 %all-to-all-done.parts_ref = bf16[8,72,256]{2,1,0:T(8,128)(2,1)S(1)} async-done(((bf16[8,72,256]{2,1,0:T(8,128)(2,1)}), bf16[8,72,256]{2,1,0:T(8,128)(2,1)S(1)}, u32[]{:S(2)}, u32[]{:S(2)}) %all-to-all-start) | async-done | bytes 294944 | tf_op jit(solution)/shard_map/all_to_all | solution.py:327
  29.5 4.4 %far_attention.1 = (f32[4,8,16,256]{3,2,1,0:T(8,128)S(1)}, f32[32,256]{1,0:T(8,128)S(1)}, bf16[576,256]{1,0:T(8,128)(2,1)S(1)}, bf16[256,128]{1,0:T(8,128)(2,1)S(1)}) custom-call(bf16[8,72,256]{2,1,0:T(8,128)(2,1)S(1)} %all-to-all-done.parts_ref, f32[64,64]{1,0:T(8,128)S(1)} %get-tuple-element.29.allowed_ref, bf16[128,256]{1,0:T(8,128)(2,1)S(1)} %copy-done.7, ...), custom_call_target="tpu_custom_call" | custom-call | flops 10737418240 | bytes 2162692 | tf_op jit(solution)/shard_map/far_attention/pallas_call | solution.py:68
  33.9 2.2 %all-gather.1 = bf16[1152,256]{1,0:T(8,128)(2,1)S(1)} all-gather(bf16[576,256]{1,0:T(8,128)(2,1)S(1)} %get-tuple-element.40), channel_id=3, replica_groups=mesh['x'=4,'y'=8,'z'=8,'c'=2] {'c'}, dimensions={0}, use_global_device_ids=true | all-gather | bytes 884736 | tf_op jit(solution)/shard_map/all_gather | solution.py:394
  36.1 0.8 chip_grads.1
  36.9 5.9 %all-to-all-start.1 = ((bf16[32,24,256]{2,1,0:T(8,128)(2,1)}), bf16[32,24,256]{2,1,0:T(8,128)(2,1)S(1)}, u32[]{:S(2)}, u32[]{:S(2)}) async-start(bf16[32,24,256]{2,1,0:T(8,128)(2,1)} %get-tuple-element.41), calls=%async_computation.1 | async-start | bytes 786432 | tf_op jit(solution)/shard_map/all_to_all | solution.py:327
  42.9 1.9 %collective-permute-start.2 = (bf16[32,256]{1,0:T(8,128)(2,1)S(1)}, bf16[32,256]{1,0:T(8,128)(2,1)S(1)}, u32[]{:S(2)}, u32[]{:S(2)}) collective-permute-start(bf16[32,256]{1,0:T(8,128)(2,1)S(1)} %get-tuple-element.45), channel_id=1, source_target_pairs={{0,15},{2,1},{4,3},{6,5},{8,7},{10,9},{12,11},{14,13},{1,2},{3,4},... | collective-permute-start | bytes 49160 | tf_op jit(solution)/shard_map/ppermute | solution.py:371
  44.8 6.8 %collective-permute-done.2.outer_ref = bf16[32,256]{1,0:T(8,128)(2,1)S(1)} collective-permute-done((bf16[32,256]{1,0:T(8,128)(2,1)S(1)}, bf16[32,256]{1,0:T(8,128)(2,1)S(1)}, u32[]{:S(2)}, u32[]{:S(2)}) %collective-permute-start.2) | collective-permute-done | bytes 16416 | tf_op jit(solution)/shard_map/ppermute | solution.py:371
  51.6 0.2 own_nodes.1.own_ref
  51.8 6.4 %all-to-all-done.1.pieces_ref = bf16[32,24,256]{2,1,0:T(8,128)(2,1)S(1)} async-done(((bf16[32,24,256]{2,1,0:T(8,128)(2,1)}), bf16[32,24,256]{2,1,0:T(8,128)(2,1)S(1)}, u32[]{:S(2)}, u32[]{:S(2)}) %all-to-all-start.1) | async-done | bytes 393248 | tf_op jit(solution)/shard_map/all_to_all | solution.py:327
  58.2 0.7 weight_shares.1
  58.8 7.1 %all-to-all-start.2 = ((bf16[8,16,256]{2,1,0:T(8,128)(2,1)}), bf16[8,16,256]{2,1,0:T(8,128)(2,1)S(1)}, u32[]{:S(2)}, u32[]{:S(2)}) async-start(bf16[8,16,256]{2,1,0:T(8,128)(2,1)} %get-tuple-element.46), calls=%async_computation.2 | async-start | bytes 131072 | tf_op jit(solution)/shard_map/all_to_all | solution.py:327
  66.0 1.8 %all-gather.2 = bf16[64,256]{1,0:T(8,128)(2,1)S(1)} all-gather(bf16[32,256]{1,0:T(8,128)(2,1)S(1)} %get-tuple-element.47), channel_id=4, replica_groups=mesh['x'=4,'y'=8,'z'=8,'c'=2] {'c'}, dimensions={0}, use_global_device_ids=true | all-gather | bytes 49152 | tf_op jit(solution)/shard_map/all_gather | solution.py:416
  67.8 6.6 %all-to-all-done.2.parts_ref = bf16[8,16,256]{2,1,0:T(8,128)(2,1)S(1)} async-done(((bf16[8,16,256]{2,1,0:T(8,128)(2,1)}), bf16[8,16,256]{2,1,0:T(8,128)(2,1)S(1)}, u32[]{:S(2)}, u32[]{:S(2)}) %all-to-all-start.2) | async-done | bytes 65568 | tf_op jit(solution)/shard_map/all_to_all | solution.py:327
  74.3 8.1 %all_to_all.20.parts_ref = bf16[4,32,256]{2,1,0:T(8,128)(2,1)S(1)} all-to-all(bf16[4,32,256]{2,1,0:T(8,128)(2,1)S(1)} %weight_columns.1), channel_id=1, replica_groups=mesh['x'=4,'y'=8,'z'=8,'c'=2] {'x'}, dimensions={0} | all-to-all | bytes 131072 | tf_op jit(solution)/shard_map/all_to_all | solution.py:327
  82.4 0.9 %gradients.1 = (f32[4,16,256]{2,1,0:T(8,128)}, bf16[128,256]{1,0:T(8,128)(2,1)}) custom-call(bf16[4,32,256]{2,1,0:T(8,128)(2,1)S(1)} %all_to_all.20.parts_ref, f32[128,256]{1,0:T(8,128)S(1)} %own_nodes.1.own_ref, s32[1,128]{1,0:T(1,128)S(1)} %bitcast.11), custom_call_target="tpu_custom_call" | custom-call | flops 1048576 | bytes 197120 | tf_op jit(solution)/shard_map/gradients/pallas_call | solution.py:68
  (1 shorter events, 0.0 us)
Async XLA Ops:
  0.6 0.7 copy-start.2
  1.3 0.8 %copy-start = (bf16[128,256]{1,0:T(8,128)(2,1)S(1)}, bf16[128,256]{1,0:T(8,128)(2,1)}, u32[]{:S(2)}) copy-start(bf16[128,256]{1,0:T(8,128)(2,1)} %x_ref.1) | copy-start | bytes 196612
  2.4 15.7 %collective-permute-start = (bf16[32,256]{1,0:T(8,128)(2,1)S(1)}, bf16[32,256]{1,0:T(8,128)(2,1)S(1)}, u32[]{:S(2)}, u32[]{:S(2)}) collective-permute-start(bf16[32,256]{1,0:T(8,128)(2,1)S(1)} %get-tuple-element.27), channel_id=1, source_target_pairs={{0,1},{1,2},{2,3},{3,4},{4,5},{5,6},{6,7},{7,8},{8,9},{9,10},{10,1... | collective-permute-start | bytes 49160 | tf_op jit(solution)/shard_map/ppermute | solution.py:351
  2.4 15.7 %collective-permute-start.1 = (bf16[32,256]{1,0:T(8,128)(2,1)S(1)}, bf16[32,256]{1,0:T(8,128)(2,1)S(1)}, u32[]{:S(2)}, u32[]{:S(2)}) collective-permute-start(bf16[32,256]{1,0:T(8,128)(2,1)S(1)} %get-tuple-element.28), channel_id=1, source_target_pairs={{0,15},{1,0},{2,1},{3,2},{4,3},{5,4},{6,5},{7,6},{8,7},{9,8},{10,9... | collective-permute-start | bytes 49160 | tf_op jit(solution)/shard_map/ppermute | solution.py:352
  6.4 11.7 %copy-start.7 = (bf16[128,256]{1,0:T(8,128)(2,1)S(1)}, bf16[128,256]{1,0:T(8,128)(2,1)}, u32[]{:S(2)}) copy-start(bf16[128,256]{1,0:T(8,128)(2,1)} %grad_ref.3) | copy-start | bytes 196612
  6.4 11.7 %copy-start.8 = (s32[128,32]{0,1:T(8,128)S(1)}, s32[128,32]{0,1:T(8,128)}, u32[]{:S(2)}) copy-start(s32[128,32]{0,1:T(8,128)} %param.11) | copy-start | bytes 49156
  7.1 11.0 %copy-start.1 = (bf16[128,256]{1,0:T(8,128)(2,1)S(1)}, bf16[128,256]{1,0:T(8,128)(2,1)}, u32[]{:S(2)}) copy-start(bf16[128,256]{1,0:T(8,128)(2,1)} %x_ref.1) | copy-start | bytes 196612
  7.1 11.0 %copy-start.3 = (bf16[256,256]{1,0:T(8,128)(2,1)S(1)}, bf16[256,256]{1,0:T(8,128)(2,1)}, u32[]{:S(2)}) copy-start(bf16[256,256]{1,0:T(8,128)(2,1)} %wo_ref.1) | copy-start | bytes 393220
  7.1 11.0 %copy-start.4 = (bf16[256,256]{1,0:T(8,128)(2,1)S(1)}, bf16[256,256]{1,0:T(8,128)(2,1)}, u32[]{:S(2)}) copy-start(bf16[256,256]{1,0:T(8,128)(2,1)} %wk_ref.3) | copy-start | bytes 393220
  7.1 11.0 %copy-start.5 = (bf16[256,256]{1,0:T(8,128)(2,1)S(1)}, bf16[256,256]{1,0:T(8,128)(2,1)}, u32[]{:S(2)}) copy-start(bf16[256,256]{1,0:T(8,128)(2,1)} %wv_ref.3) | copy-start | bytes 393220
  7.2 11.0 %copy-start.6 = (bf16[256,256]{1,0:T(8,128)(2,1)S(1)}, bf16[256,256]{1,0:T(8,128)(2,1)}, u32[]{:S(2)}) copy-start(bf16[256,256]{1,0:T(8,128)(2,1)} %wq_ref.5) | copy-start | bytes 393220
  7.2 22.3 %all-to-all-start = ((bf16[8,72,256]{2,1,0:T(8,128)(2,1)}), bf16[8,72,256]{2,1,0:T(8,128)(2,1)S(1)}, u32[]{:S(2)}, u32[]{:S(2)}) async-start(bf16[8,72,256]{2,1,0:T(8,128)(2,1)} %chip_sums.1), calls=%async_computation | async-start | bytes 589824 | tf_op jit(solution)/shard_map/all_to_all | solution.py:327
  18.1 0.7 copy-start.9
  36.9 21.2 %all-to-all-start.1 = ((bf16[32,24,256]{2,1,0:T(8,128)(2,1)}), bf16[32,24,256]{2,1,0:T(8,128)(2,1)S(1)}, u32[]{:S(2)}, u32[]{:S(2)}) async-start(bf16[32,24,256]{2,1,0:T(8,128)(2,1)} %get-tuple-element.41), calls=%async_computation.1 | async-start | bytes 786432 | tf_op jit(solution)/shard_map/all_to_all | solution.py:327
  42.9 8.7 %collective-permute-start.2 = (bf16[32,256]{1,0:T(8,128)(2,1)S(1)}, bf16[32,256]{1,0:T(8,128)(2,1)S(1)}, u32[]{:S(2)}, u32[]{:S(2)}) collective-permute-start(bf16[32,256]{1,0:T(8,128)(2,1)S(1)} %get-tuple-element.45), channel_id=1, source_target_pairs={{0,15},{2,1},{4,3},{6,5},{8,7},{10,9},{12,11},{14,13},{1,2},{3,4},... | collective-permute-start | bytes 49160 | tf_op jit(solution)/shard_map/ppermute | solution.py:371
  58.8 15.5 %all-to-all-start.2 = ((bf16[8,16,256]{2,1,0:T(8,128)(2,1)}), bf16[8,16,256]{2,1,0:T(8,128)(2,1)S(1)}, u32[]{:S(2)}, u32[]{:S(2)}) async-start(bf16[8,16,256]{2,1,0:T(8,128)(2,1)} %get-tuple-element.46), calls=%async_computation.2 | async-start | bytes 131072 | tf_op jit(solution)/shard_map/all_to_all | solution.py:327

commit v4 on v3

--- a/solution.py
+++ b/solution.py
@@ -17,6 +17,8 @@
 SUP = 64
 SUM_ROWS = SUP + 8
 STACK = HEADS * NODES
+CHIP_ROWS = (256, 256, 128, 128, 256, 256, 512, 64)
+CHIP_AT = tuple(sum(CHIP_ROWS[:i]) for i in range(len(CHIP_ROWS) + 1))
 SCORE_SCALE = 1.0 / math.sqrt(HEAD_DIM)
 NEVER = -1e30
 BF = jnp.bfloat16
@@ -45,6 +47,14 @@
 
 def lanes_of(h):
     return slice(h * NODES, (h + 1) * NODES)
+
+
+def split_rows(m, core):
+    pairs = m.reshape(m.shape[0] // 32, 2, 16, m.shape[1])
+    low, high = pairs[:, 0], pairs[:, 1]
+    first = jnp.broadcast_to(core, low.shape) == 0
+    shape = (m.shape[0] // 2, m.shape[1])
+    return jnp.where(first, low, high).reshape(shape), jnp.where(first, high, low).reshape(shape)
 
 
 def stack_lanes(ref, flipped):
@@ -104,8 +114,8 @@
 
 def near_body(
     low_ref, x_ref, high_ref, grad_ref, slots_ref, links_ref, core_ref, wq_ref, wk_ref, wv_ref, wo_ref,
-    qt_ref, at_ref, xt_ref, wt_ref, out_t_ref, gq_t_ref, wkv_ref, base_ref, allowed_ref, inner_ref, outer_ref,
-    q_lanes, a_lanes, q_rows, a_rows, weight_all, score_all,
+    qt_ref, at_ref, xt_ref, wt_ref, out_t_ref, gq_t_ref, wkv_ref, base_ref, allowed_ref, chip_ref, outer_ref,
+    q_lanes, a_lanes, q_rows, a_rows, weight_all, score_all, near_t,
 ):
     ext = jnp.concatenate([low_ref[...], x_ref[...], high_ref[...]], 0)
     wk = wk_ref[...]
@@ -140,22 +150,39 @@
         d_score = (prob * (g - centre) * SCORE_SCALE).astype(BF)
         weight_all[:, lanes_of(h)] = weight
         score_all[:, lanes_of(h)] = d_score
-        out_t_ref[rows_of(h)] = mm(vals_t[rows_of(h)], weight)
+        near_t[rows_of(h)] = mm(vals_t[rows_of(h)], weight)
         gq_t_ref[rows_of(h)] = mm(keys_t[rows_of(h)], d_score)
     grad_keys = mm(score_all[...], q_rows[...]).astype(BF)
     grad_vals = mm(weight_all[...], a_rows[...]).astype(BF)
-    ext_t = flip(ext)
-    xt_ref[...] = ext_t[:, HALO : HALO + NODES]
+    core = core_ref[0]
+    ext_t = ext.astype(F32).T
     wt_ref[:WIDTH] = flip(wq_ref[...])
     wt_ref[WIDTH : 2 * WIDTH] = flip(wk)
     wt_ref[2 * WIDTH :] = flip(wv)
-    wkv_ref[0] = mm(ext_t, grad_keys)
-    wkv_ref[1] = mm(ext_t, grad_vals)
+    x_mine, x_other = split_rows(ext_t[:, HALO : HALO + NODES], core)
+    xt_ref[...] = x_mine.astype(BF)
+    near_mine, near_other = split_rows(near_t[...], core)
+    out_t_ref[...] = near_mine
+    ext_t = ext_t.astype(BF)
+    key_mine, key_other = split_rows(mm(ext_t, grad_keys), core)
+    val_mine, val_other = split_rows(mm(ext_t, grad_vals), core)
+    wkv_ref[0] = key_mine
+    wkv_ref[1] = val_mine
+    chip = [
+        q_t, a_t, x_other, near_other, gq_t_ref[...], grad_ref[:, :NODES], grad_ref[:, NODES:],
+        key_other[:, :NODES], key_other[:, NODES:], val_other[:, :NODES], val_other[:, NODES:],
+    ]
+    at = 0
+    for part in chip:
+        chip_ref[at : at + part.shape[0]] = part.astype(BF)
+        at += part.shape[0]
     back = mm_nt(grad_keys, wk) + mm_nt(grad_vals, wv)
     base_ref[...] = grad_ref[...].astype(F32) + back[HALO : HALO + NODES]
     below, above = back[:HALO], back[HALO + NODES :]
-    first = jnp.broadcast_to(core_ref[0], below.shape) == 0
-    inner_ref[...] = jnp.where(first, above, below).astype(BF)
+    first = jnp.broadcast_to(core, below.shape) == 0
+    inner = jnp.where(first, above, below).astype(BF)
+    chip_ref[at : at + HALO] = inner[:, :NODES]
+    chip_ref[at + HALO :] = inner[:, NODES:]
     outer_ref[...] = jnp.where(first, below, above).astype(BF)
     links = links_ref[...]
     target = iota((SUP, SUP), 0)
@@ -175,10 +202,21 @@
 
 
 def far_body(
-    parts_ref, allowed_ref, grad_ref, wq_ref, wk_ref, wv_ref, wt_ref,
-    qt_ref, at_ref, xt_ref, near_t_ref, near_gq_ref, wkv_ref, inner_ref, core_ref,
-    mine_ref, mine_pooled_ref, theirs_ref, gq_t_ref,
+    parts_ref, allowed_ref, both_ref, grad_ref, wq_ref, wk_ref, wv_ref, wt_ref,
+    qt_ref, at_ref, xt_ref, near_t_ref, near_gq_ref, wkv_ref, core_ref,
+    message_ref, gq_t_ref, inner_ref,
 ):
+    core = core_ref[0]
+    sibling = both_ref.at[1 - core]
+
+    def section(i):
+        return sibling[CHIP_AT[i] : CHIP_AT[i + 1]]
+
+    def folded(i):
+        rows = section(i)
+        half = rows.shape[0] // 2
+        return jnp.concatenate([rows[:half], rows[half:]], 1)
+
     heads = [rows_of(h) for h in range(HEADS)]
     wq = wq_ref[...]
     wk = wk_ref[...]
@@ -199,24 +237,29 @@
     s_prob = [softmax_rows(mm(s_k[:, h], s_qt[h]) * SCORE_SCALE + allowed) for h in heads]
     s_weight = [p.astype(BF) for p in s_prob]
     moved_t = jnp.concatenate([mm(s_vt[h], w) for h, w in zip(heads, s_weight)], 0)
-    state_t = (pooled_t.astype(F32) + moved_t).astype(BF)
+    state_t = pooled_t.astype(F32) + moved_t
+    low_rank = jnp.concatenate(
+        [split_rows(pooled_t.astype(F32), core)[0], split_rows(state_t, core)[0]], 1
+    ).astype(BF)
+    state_t = state_t.astype(BF)
     state = flip(state_t)
 
-    c_proj_t = mm(wt[WIDTH:], state_t).astype(BF)
-    c_kt, c_vt = c_proj_t[:WIDTH], c_proj_t[WIDTH:]
+    c_proj_t = mm(wt[WIDTH:], state_t)
+    c_kt = c_proj_t[:WIDTH].astype(BF)
+    c_vt = split_rows(c_proj_t[WIDTH:], core)[0].astype(BF)
     c_k = mm(state, wk).astype(BF)
     c_v = mm(state, wv).astype(BF)
-    q_t = qt_ref[...]
-    a_t = at_ref[...]
+    q_t = jnp.concatenate([qt_ref[...], section(0)], 1)
+    a_t = jnp.concatenate([at_ref[...], section(1)], 1)
     out_t = []
     gq_t = []
     gck_t = []
     gcv_t = []
-    for h in heads:
+    for i, h in enumerate(heads):
         prob = softmax_rows(mm(c_k[:, h], q_t[h]) * SCORE_SCALE)
         weight = prob.astype(BF)
         d_score = score_grad(prob, mm(c_v[:, h], a_t[h]))
-        out_t.append(mm(c_vt[h], weight))
+        out_t.append(mm(c_vt[i * 16 : (i + 1) * 16], weight))
         gq_t.append(mm(c_kt[h], d_score))
         gck_t.append(mm_nt(q_t[h], d_score))
         gcv_t.append(mm_nt(a_t[h], weight))
@@ -241,32 +284,36 @@
     )
     share = grad_pooled_t.T * inverse
 
-    gq_t = (near_gq_ref[...] + jnp.concatenate(gq_t, 0)).astype(BF)
-    gq_t_ref[...] = gq_t
-    attended_t = (near_t_ref[...] + jnp.concatenate(out_t, 0)).astype(BF)
+    near_gq = jnp.concatenate([near_gq_ref[...], section(4).astype(F32)], 1)
+    gq_t = (near_gq + jnp.concatenate(gq_t, 0)).astype(BF)
+    gq_t_ref[...] = gq_t[:, :NODES]
+    near_t = jnp.concatenate([near_t_ref[...], section(3).astype(F32)], 1)
+    attended_t = (near_t + jnp.concatenate(out_t, 0)).astype(BF)
+    x_t = jnp.concatenate([xt_ref[...], section(2)], 1)
+    grad_out = jnp.concatenate([grad_ref[...], folded(5)], 0)
+    near_kv = section(6).astype(F32)
+    rows = near_kv.shape[0] // 4
+    near_k = wkv_ref[0] + jnp.concatenate([near_kv[:rows], near_kv[rows : 2 * rows]], 1)
+    near_v = wkv_ref[1] + jnp.concatenate([near_kv[2 * rows : 3 * rows], near_kv[3 * rows :]], 1)
+    inner_ref[...] = folded(7)
     grads = [
-        mm_nt(xt_ref[...], gq_t) + mm_nt(pooled_t, gsq_t),
-        wkv_ref[0] + mm_nt(jnp.concatenate([pooled_t, state_t], 1), jnp.concatenate([gsk_t, gck_t], 1)),
-        wkv_ref[1] + mm_nt(jnp.concatenate([pooled_t, state_t], 1), jnp.concatenate([gsv_t, gcv_t], 1)),
-        mm(attended_t, grad_ref[...]),
+        mm_nt(jnp.concatenate([x_t, low_rank[:, :SUP]], 1), jnp.concatenate([gq_t, gsq_t], 1)),
+        near_k + mm_nt(low_rank, jnp.concatenate([gsk_t, gck_t], 1)),
+        near_v + mm_nt(low_rank, jnp.concatenate([gsv_t, gcv_t], 1)),
+        mm(attended_t, grad_out),
     ]
-    core = core_ref[0]
-    groups = mine_ref.shape[1]
-    rows = mine_ref.shape[2]
-    first = jnp.broadcast_to(core, (groups, rows, WIDTH)) == 0
-    for w in range(4):
-        pairs = grads[w].reshape(groups, 2, rows, WIDTH)
-        low, high = pairs[:, 0], pairs[:, 1]
-        mine_ref[w] = jnp.where(first, low, high)
-        theirs_ref[w * groups * rows : (w + 1) * groups * rows] = (
-            jnp.where(first, high, low).reshape(groups * rows, WIDTH).astype(BF)
-        )
     half = SUP // 2
     first = jnp.broadcast_to(core, (half, WIDTH)) == 0
-    mine_pooled_ref[...] = jnp.where(first, share[:half], share[half:])
-    end = 4 * groups * rows + half
-    theirs_ref[4 * groups * rows : end] = jnp.where(first, share[half:], share[:half]).astype(BF)
-    theirs_ref[end:] = inner_ref[...]
+    pooled_half = jnp.where(first, share[:half], share[half:])
+    quarter = half // len(grads)
+    message_rows = message_ref.shape[1]
+    n_z = message_ref.shape[0] // len(grads)
+    own_rows = message_rows - quarter
+    for w, grad in enumerate(grads):
+        piece = pooled_half[w * quarter : (w + 1) * quarter]
+        for z in range(n_z):
+            rows = grad[z * own_rows : (z + 1) * own_rows]
+            message_ref[w * n_z + z] = jnp.concatenate([rows, piece], 0).astype(BF)
 
 
 def own_body(base_ref, gq_t_ref, wq_ref, inner_ref, outer_ref, core_ref, out_ref):
@@ -276,20 +323,6 @@
     out_ref[:HALO] = own[:HALO] + jnp.where(first, outer, inner)
     out_ref[HALO : NODES - HALO] = own[HALO : NODES - HALO]
     out_ref[NODES - HALO :] = own[NODES - HALO :] + jnp.where(first, inner, outer)
-
-
-def chip_grads_body(mine_ref, mine_pooled_ref, both_ref, core_ref, out_ref, inner_ref):
-    received = both_ref[1 - core_ref[0]].astype(F32)
-    n_w, n_z, rows, _ = mine_ref.shape
-    size = n_w * n_z * rows
-    weights = mine_ref[...] + received[:size].reshape(mine_ref.shape)
-    pooled = mine_pooled_ref[...] + received[size : size + mine_pooled_ref.shape[0]]
-    inner_ref[...] = received[size + mine_pooled_ref.shape[0] :].astype(BF)
-    quarter = pooled.shape[0] // n_w
-    for w in range(n_w):
-        piece = pooled[w * quarter : (w + 1) * quarter]
-        for z in range(n_z):
-            out_ref[w * n_z + z] = jnp.concatenate([weights[w, z], piece], 0).astype(BF)
 
 
 def shares_body(n_w, pieces_ref, own_ref, out_ref, pooled_ref):
@@ -351,17 +384,17 @@
     low = lax.ppermute(last_rows, supers, up)
     high = lax.ppermute(first_rows, supers, down)
     parts = swap(sums, "z")
-    q_t, a_t, x_t, w_t, near_t, near_gq, wkv, base, allowed, inner, outer = call(
+    q_t, a_t, x_t, w_t, near_t, near_gq, wkv, base, allowed, chip, outer = call(
         near_body,
         "near_attention",
         [
-            ((WIDTH, NODES), BF), ((WIDTH, NODES), BF), ((WIDTH, NODES), BF), ((3 * WIDTH, WIDTH), BF),
-            ((WIDTH, NODES), F32), ((WIDTH, NODES), F32), ((2, WIDTH, WIDTH), F32), ((NODES, WIDTH), F32),
-            ((SUP, SUP), F32), ((HALO, WIDTH), BF), ((HALO, WIDTH), BF),
+            ((WIDTH, NODES), BF), ((WIDTH, NODES), BF), ((WIDTH // 2, NODES), BF), ((3 * WIDTH, WIDTH), BF),
+            ((WIDTH // 2, NODES), F32), ((WIDTH, NODES), F32), ((2, WIDTH // 2, WIDTH), F32), ((NODES, WIDTH), F32),
+            ((SUP, SUP), F32), ((CHIP_AT[-1], NODES), BF), ((HALO, WIDTH), BF),
         ],
         [
             ((WIDTH, STACK), BF), ((WIDTH, STACK), BF), ((STACK, WIDTH), BF), ((STACK, WIDTH), BF),
-            ((EXT, STACK), BF), ((EXT, STACK), BF),
+            ((EXT, STACK), BF), ((EXT, STACK), BF), ((WIDTH, NODES), F32),
         ],
         10 << 30,
         low, node_feats, high, grad_out, neighbours.T, super_links.T, core, w_query, w_key, w_value, w_out,
@@ -370,28 +403,16 @@
     outward += [(2 * z + 1, (2 * z + 2) % n_super) for z in range(n_z)]
     outer = lax.ppermute(outer, supers, outward)
     share_rows = WIDTH // n_super
-    weight_rows = 4 * n_z * share_rows
     half = (SUP // 2, WIDTH)
-    mine, mine_pooled, theirs, gq_t = call(
+    message_rows = share_rows + SUP // 2 // n_x
+    pieces, gq_t, inner = call(
         far_body,
         "far_attention",
-        [
-            ((4, n_z, share_rows, WIDTH), F32), (half, F32), ((weight_rows + SUP // 2 + HALO, WIDTH), BF),
-            ((WIDTH, NODES), BF),
-        ],
+        [((n_x * n_z, message_rows, WIDTH), BF), ((WIDTH, NODES), BF), ((HALO, WIDTH), BF)],
         [],
         10 << 30,
-        parts, allowed, grad_out, w_query, w_key, w_value, w_t,
-        q_t, a_t, x_t, near_t, near_gq, wkv, inner, core,
-    )
-    message_rows = share_rows + SUP // 2 // n_x
-    pieces, inner = call(
-        chip_grads_body,
-        "chip_grads",
-        [((n_x * n_z, message_rows, WIDTH), BF), ((HALO, WIDTH), BF)],
-        [],
-        1 << 20,
-        mine, mine_pooled, lax.all_gather(theirs, "c"), core,
+        parts, allowed, lax.all_gather(chip, "c"), grad_out, w_query, w_key, w_value, w_t,
+        q_t, a_t, x_t, near_t, near_gq, wkv, core,
     )
     pieces = swap(pieces, ("x", "z"))
     (own,) = call(

time: 83.8 us -> 80.8 us (0.964)
  waiting for transfers between devices: 27.3 us -> 24 us
    all_to_all x3, waiting for transfers between devices: 20.5 us -> 18 us  [swap(): return lax.all_to_all(parts, axes, 0, 0, tiled=True)]
    pallas_call x9 -> x8, Pallas kernels: 11.1 us -> 11.1 us  [call(): pl.pallas_call(body, in_specs=[anywhere if i in outside else smem if a.nd...]
where the time goes in v4:
time: 80.8 us; the launch traced here: 80.3 us
  starting transfers between devices  27.6 us (34%)
  waiting for transfers between devices  24 us (30%)
  blocking collectives  14.7 us (18%)
  Pallas kernels  11.1 us (14%)
  local copies, waits for them, and re-layouts  2.12 us (3%)
    all_to_all x3, starting transfers between devices, swap(): return lax.all_to_all(parts, axes, 0, 0, tiled=True)  23.9 us
    all_to_all x3, waiting for transfers between devices, swap(): return lax.all_to_all(parts, axes, 0, 0, tiled=True)  18 us
    pallas_call x8, Pallas kernels, call(): pl.pallas_call(body, in_specs=[anywhere if i in outside else smem if a.nd...  11.1 us
    all_to_all x1, blocking collectives, swap(): return lax.all_to_all(parts, axes, 0, 0, tiled=True)  8.06 us
    ppermute x1, waiting for transfers between devices, local(): outer = lax.ppermute(outer, supers, outward)  6.06 us
    all_gather x1, blocking collectives, local(): lax.all_gather(chip, 'c')  2.49 us
    all_gather x1, blocking collectives, local(): lax.all_gather(sums, 'c')  2.29 us
    unnamed x20, local copies, waits for them, and re-layouts  2.12 us
  transfers between devices with their start and end apart: 6, of which 4 were waited for; matrix products, arithmetic and copies ran while one was open for 0% of the time, Pallas kernels for 5%

profile of v4, /device:TPU:64, one launch (start us, length us, event | category | flops | bytes accessed | tf_op | source)
XLA Modules:
  0.0 80.3 jit_solution(735002942683435283)
XLA Ops:
  0.6 0.0 copy-start.2
  0.6 0.6 copy-done.2
  1.3 0.0 copy-start
  1.3 0.8 %copy-done = bf16[128,256]{1,0:T(8,128)(2,1)S(1)} copy-done((bf16[128,256]{1,0:T(8,128)(2,1)S(1)}, bf16[128,256]{1,0:T(8,128)(2,1)}, u32[]{:S(2)}) %copy-start) | copy-done | bytes 65560
  2.1 0.2 cluster_sums.1
  2.4 0.0 collective-permute-start
  2.4 1.7 %collective-permute-start.1 = (bf16[32,256]{1,0:T(8,128)(2,1)S(1)}, bf16[32,256]{1,0:T(8,128)(2,1)S(1)}, u32[]{:S(2)}, u32[]{:S(2)}) collective-permute-start(bf16[32,256]{1,0:T(8,128)(2,1)S(1)} %get-tuple-element.25), channel_id=1, source_target_pairs={{0,15},{1,0},{2,1},{3,2},{4,3},{5,4},{6,5},{7,6},{8,7},{9,8},{10,9... | collective-permute-start | bytes 49160 | tf_op jit(solution)/shard_map/ppermute | solution.py:385
  4.1 2.3 %all-gather = f32[144,256]{1,0:T(8,128)S(1)} all-gather(f32[72,256]{1,0:T(8,128)S(1)} %get-tuple-element.23), channel_id=2, replica_groups=mesh['x'=4,'y'=8,'z'=8,'c'=2] {'c'}, dimensions={0}, use_global_device_ids=true | all-gather | bytes 221184 | tf_op jit(solution)/shard_map/all_gather | solution.py:381
  6.4 0.0 copy-start.7
  6.4 0.0 copy-start.8
  6.4 0.7 chip_sums.1
  7.1 0.0 copy-start.1
  7.1 0.0 copy-start.3
  7.1 0.0 copy-start.4
  7.2 0.0 copy-start.5
  7.2 0.0 copy-start.6
  7.2 10.9 %all-to-all-start = ((bf16[8,72,256]{2,1,0:T(8,128)(2,1)}), bf16[8,72,256]{2,1,0:T(8,128)(2,1)S(1)}, u32[]{:S(2)}, u32[]{:S(2)}) async-start(bf16[8,72,256]{2,1,0:T(8,128)(2,1)} %chip_sums.1), calls=%async_computation | async-start | bytes 589824 | tf_op jit(solution)/shard_map/all_to_all | solution.py:360
  18.1 0.0 copy-start.9
  18.1 0.0 collective-permute-done.low_ref
  18.1 0.0 collective-permute-done.1.high_ref
  18.1 0.0 copy-done.7
  18.1 0.0 copy-done.8
  18.1 0.0 copy-done.1
  18.1 0.0 copy-done.3
  18.1 0.0 copy-done.4
  18.1 0.0 copy-done.5
  18.1 0.0 copy-done.6
  18.2 0.6 copy-done.9
  18.8 3.2 %near_attention.1 = (bf16[256,128]{1,0:T(8,128)(2,1)S(1)}, bf16[256,128]{1,0:T(8,128)(2,1)S(1)}, bf16[128,128]{1,0:T(8,128)(2,1)S(1)}, bf16[768,256]{1,0:T(8,128...) custom-call(bf16[32,256]{1,0:T(8,128)(2,1)S(1)} %collective-permute-, ...), custom_call_target="tpu_custom_call" | custom-call | flops 10737418240 | bytes 706564 | tf_op jit(solution)/shard_map/near_attention/pallas_call | solution.py:78
  22.0 2.5 %all-gather.1 = bf16[3712,128]{1,0:T(8,128)(2,1)S(1)} all-gather(bf16[1856,128]{1,0:T(8,128)(2,1)S(1)} %get-tuple-element.27), channel_id=3, replica_groups=mesh['x'=4,'y'=8,'z'=8,'c'=2] {'c'}, dimensions={0}, use_global_device_ids=true | all-gather | bytes 1425408 | tf_op jit(solution)/shard_map/all_gather | solution.py:414
  24.5 5.1 %all-to-all-done.parts_ref = bf16[8,72,256]{2,1,0:T(8,128)(2,1)S(1)} async-done(((bf16[8,72,256]{2,1,0:T(8,128)(2,1)}), bf16[8,72,256]{2,1,0:T(8,128)(2,1)S(1)}, u32[]{:S(2)}, u32[]{:S(2)}) %all-to-all-start) | async-done | bytes 294944 | tf_op jit(solution)/shard_map/all_to_all | solution.py:360
  29.5 5.2 %far_attention.1 = (bf16[32,24,256]{2,1,0:T(8,128)(2,1)}, bf16[256,128]{1,0:T(8,128)(2,1)S(1)}, bf16[32,256]{1,0:T(8,128)(2,1)S(1)}) custom-call(bf16[8,72,256]{2,1,0:T(8,128)(2,1)S(1)} %all-to-all-done.parts_ref, f32[64,64]{1,0:T(8,128)S(1)} %get-tuple-element.26.allowed_ref, bf16[2,1856,128]{2,1,0:T(8,128)(2,1)S(1)} %bitcast.7, ...), custom_call_target="tpu_custom_call" | custom-call | flops 10737418240 | bytes 2736132 | tf_op jit(solution)/shard_map/far_attention/pallas_call | solution.py:78
  34.7 5.9 %all-to-all-start.1 = ((bf16[32,24,256]{2,1,0:T(8,128)(2,1)}), bf16[32,24,256]{2,1,0:T(8,128)(2,1)S(1)}, u32[]{:S(2)}, u32[]{:S(2)}) async-start(bf16[32,24,256]{2,1,0:T(8,128)(2,1)} %get-tuple-element.35), calls=%async_computation.1 | async-start | bytes 786432 | tf_op jit(solution)/shard_map/all_to_all | solution.py:360
  40.6 1.9 %collective-permute-start.2 = (bf16[32,256]{1,0:T(8,128)(2,1)S(1)}, bf16[32,256]{1,0:T(8,128)(2,1)S(1)}, u32[]{:S(2)}, u32[]{:S(2)}) collective-permute-start(bf16[32,256]{1,0:T(8,128)(2,1)S(1)} %get-tuple-element.39), channel_id=1, source_target_pairs={{0,15},{2,1},{4,3},{6,5},{8,7},{10,9},{12,11},{14,13},{1,2},{3,4},... | collective-permute-start | bytes 49160 | tf_op jit(solution)/shard_map/ppermute | solution.py:404
  42.5 6.1 %collective-permute-done.2.outer_ref = bf16[32,256]{1,0:T(8,128)(2,1)S(1)} collective-permute-done((bf16[32,256]{1,0:T(8,128)(2,1)S(1)}, bf16[32,256]{1,0:T(8,128)(2,1)S(1)}, u32[]{:S(2)}, u32[]{:S(2)}) %collective-permute-start.2) | collective-permute-done | bytes 16416 | tf_op jit(solution)/shard_map/ppermute | solution.py:404
  48.6 0.2 own_nodes.1.own_ref
  48.8 6.4 %all-to-all-done.1.pieces_ref = bf16[32,24,256]{2,1,0:T(8,128)(2,1)S(1)} async-done(((bf16[32,24,256]{2,1,0:T(8,128)(2,1)}), bf16[32,24,256]{2,1,0:T(8,128)(2,1)S(1)}, u32[]{:S(2)}, u32[]{:S(2)}) %all-to-all-start.1) | async-done | bytes 393248 | tf_op jit(solution)/shard_map/all_to_all | solution.py:360
  55.2 0.7 weight_shares.1
  55.8 7.1 %all-to-all-start.2 = ((bf16[8,16,256]{2,1,0:T(8,128)(2,1)}), bf16[8,16,256]{2,1,0:T(8,128)(2,1)S(1)}, u32[]{:S(2)}, u32[]{:S(2)}) async-start(bf16[8,16,256]{2,1,0:T(8,128)(2,1)} %get-tuple-element.40), calls=%async_computation.2 | async-start | bytes 131072 | tf_op jit(solution)/shard_map/all_to_all | solution.py:360
  62.9 1.8 %all-gather.2 = bf16[64,256]{1,0:T(8,128)(2,1)S(1)} all-gather(bf16[32,256]{1,0:T(8,128)(2,1)S(1)} %get-tuple-element.41), channel_id=4, replica_groups=mesh['x'=4,'y'=8,'z'=8,'c'=2] {'c'}, dimensions={0}, use_global_device_ids=true | all-gather | bytes 49152 | tf_op jit(solution)/shard_map/all_gather | solution.py:437
  64.8 6.6 %all-to-all-done.2.parts_ref = bf16[8,16,256]{2,1,0:T(8,128)(2,1)S(1)} async-done(((bf16[8,16,256]{2,1,0:T(8,128)(2,1)}), bf16[8,16,256]{2,1,0:T(8,128)(2,1)S(1)}, u32[]{:S(2)}, u32[]{:S(2)}) %all-to-all-start.2) | async-done | bytes 65568 | tf_op jit(solution)/shard_map/all_to_all | solution.py:360
  71.3 8.1 %all_to_all.20.parts_ref = bf16[4,32,256]{2,1,0:T(8,128)(2,1)S(1)} all-to-all(bf16[4,32,256]{2,1,0:T(8,128)(2,1)S(1)} %weight_columns.1), channel_id=1, replica_groups=mesh['x'=4,'y'=8,'z'=8,'c'=2] {'x'}, dimensions={0} | all-to-all | bytes 131072 | tf_op jit(solution)/shard_map/all_to_all | solution.py:360
  79.4 0.9 %gradients.1 = (f32[4,16,256]{2,1,0:T(8,128)}, bf16[128,256]{1,0:T(8,128)(2,1)}) custom-call(bf16[4,32,256]{2,1,0:T(8,128)(2,1)S(1)} %all_to_all.20.parts_ref, f32[128,256]{1,0:T(8,128)S(1)} %own_nodes.1.own_ref, s32[1,128]{1,0:T(1,128)S(1)} %bitcast.11), custom_call_target="tpu_custom_call" | custom-call | flops 1048576 | bytes 197120 | tf_op jit(solution)/shard_map/gradients/pallas_call | solution.py:78
  (1 shorter events, 0.0 us)
Async XLA Ops:
  0.6 0.7 copy-start.2
  1.3 0.8 %copy-start = (bf16[128,256]{1,0:T(8,128)(2,1)S(1)}, bf16[128,256]{1,0:T(8,128)(2,1)}, u32[]{:S(2)}) copy-start(bf16[128,256]{1,0:T(8,128)(2,1)} %x_ref.1) | copy-start | bytes 196612
  2.4 15.7 %collective-permute-start = (bf16[32,256]{1,0:T(8,128)(2,1)S(1)}, bf16[32,256]{1,0:T(8,128)(2,1)S(1)}, u32[]{:S(2)}, u32[]{:S(2)}) collective-permute-start(bf16[32,256]{1,0:T(8,128)(2,1)S(1)} %get-tuple-element.24), channel_id=1, source_target_pairs={{0,1},{1,2},{2,3},{3,4},{4,5},{5,6},{6,7},{7,8},{8,9},{9,10},{10,1... | collective-permute-start | bytes 49160 | tf_op jit(solution)/shard_map/ppermute | solution.py:384
  2.4 15.7 %collective-permute-start.1 = (bf16[32,256]{1,0:T(8,128)(2,1)S(1)}, bf16[32,256]{1,0:T(8,128)(2,1)S(1)}, u32[]{:S(2)}, u32[]{:S(2)}) collective-permute-start(bf16[32,256]{1,0:T(8,128)(2,1)S(1)} %get-tuple-element.25), channel_id=1, source_target_pairs={{0,15},{1,0},{2,1},{3,2},{4,3},{5,4},{6,5},{7,6},{8,7},{9,8},{10,9... | collective-permute-start | bytes 49160 | tf_op jit(solution)/shard_map/ppermute | solution.py:385
  6.4 11.7 %copy-start.7 = (bf16[128,256]{1,0:T(8,128)(2,1)S(1)}, bf16[128,256]{1,0:T(8,128)(2,1)}, u32[]{:S(2)}) copy-start(bf16[128,256]{1,0:T(8,128)(2,1)} %grad_ref.3) | copy-start | bytes 196612
  6.4 11.7 %copy-start.8 = (s32[128,32]{0,1:T(8,128)S(1)}, s32[128,32]{0,1:T(8,128)}, u32[]{:S(2)}) copy-start(s32[128,32]{0,1:T(8,128)} %param.11) | copy-start | bytes 49156
  7.1 11.0 %copy-start.1 = (bf16[128,256]{1,0:T(8,128)(2,1)S(1)}, bf16[128,256]{1,0:T(8,128)(2,1)}, u32[]{:S(2)}) copy-start(bf16[128,256]{1,0:T(8,128)(2,1)} %x_ref.1) | copy-start | bytes 196612
  7.1 11.0 %copy-start.3 = (bf16[256,256]{1,0:T(8,128)(2,1)S(1)}, bf16[256,256]{1,0:T(8,128)(2,1)}, u32[]{:S(2)}) copy-start(bf16[256,256]{1,0:T(8,128)(2,1)} %wo_ref.1) | copy-start | bytes 393220
  7.1 11.0 %copy-start.4 = (bf16[256,256]{1,0:T(8,128)(2,1)S(1)}, bf16[256,256]{1,0:T(8,128)(2,1)}, u32[]{:S(2)}) copy-start(bf16[256,256]{1,0:T(8,128)(2,1)} %wk_ref.3) | copy-start | bytes 393220
  7.2 11.0 %copy-start.5 = (bf16[256,256]{1,0:T(8,128)(2,1)S(1)}, bf16[256,256]{1,0:T(8,128)(2,1)}, u32[]{:S(2)}) copy-start(bf16[256,256]{1,0:T(8,128)(2,1)} %wv_ref.3) | copy-start | bytes 393220
  7.2 11.0 %copy-start.6 = (bf16[256,256]{1,0:T(8,128)(2,1)S(1)}, bf16[256,256]{1,0:T(8,128)(2,1)}, u32[]{:S(2)}) copy-start(bf16[256,256]{1,0:T(8,128)(2,1)} %wq_ref.5) | copy-start | bytes 393220
  7.2 22.3 %all-to-all-start = ((bf16[8,72,256]{2,1,0:T(8,128)(2,1)}), bf16[8,72,256]{2,1,0:T(8,128)(2,1)S(1)}, u32[]{:S(2)}, u32[]{:S(2)}) async-start(bf16[8,72,256]{2,1,0:T(8,128)(2,1)} %chip_sums.1), calls=%async_computation | async-start | bytes 589824 | tf_op jit(solution)/shard_map/all_to_all | solution.py:360
  18.1 0.7 copy-start.9
  34.7 20.5 %all-to-all-start.1 = ((bf16[32,24,256]{2,1,0:T(8,128)(2,1)}), bf16[32,24,256]{2,1,0:T(8,128)(2,1)S(1)}, u32[]{:S(2)}, u32[]{:S(2)}) async-start(bf16[32,24,256]{2,1,0:T(8,128)(2,1)} %get-tuple-element.35), calls=%async_computation.1 | async-start | bytes 786432 | tf_op jit(solution)/shard_map/all_to_all | solution.py:360
  40.6 8.0 %collective-permute-start.2 = (bf16[32,256]{1,0:T(8,128)(2,1)S(1)}, bf16[32,256]{1,0:T(8,128)(2,1)S(1)}, u32[]{:S(2)}, u32[]{:S(2)}) collective-permute-start(bf16[32,256]{1,0:T(8,128)(2,1)S(1)} %get-tuple-element.39), channel_id=1, source_target_pairs={{0,15},{2,1},{4,3},{6,5},{8,7},{10,9},{12,11},{14,13},{1,2},{3,4},... | collective-permute-start | bytes 49160 | tf_op jit(solution)/shard_map/ppermute | solution.py:404
  55.8 15.5 %all-to-all-start.2 = ((bf16[8,16,256]{2,1,0:T(8,128)(2,1)}), bf16[8,16,256]{2,1,0:T(8,128)(2,1)S(1)}, u32[]{:S(2)}, u32[]{:S(2)}) async-start(bf16[8,16,256]{2,1,0:T(8,128)(2,1)} %get-tuple-element.40), calls=%async_computation.2 | async-start | bytes 131072 | tf_op jit(solution)/shard_map/all_to_all | solution.py:360

commit v5 on v4

--- a/solution.py
+++ b/solution.py
@@ -15,9 +15,9 @@
 HALO = 32
 EXT = NODES + 2 * HALO
 SUP = 64
+K_TOP = 8
 SUM_ROWS = SUP + 8
-STACK = HEADS * NODES
-CHIP_ROWS = (256, 256, 128, 128, 256, 256, 512, 64)
+CHIP_ROWS = (256, 256, 128, 128, 256, 256, 512)
 CHIP_AT = tuple(sum(CHIP_ROWS[:i]) for i in range(len(CHIP_ROWS) + 1))
 SCORE_SCALE = 1.0 / math.sqrt(HEAD_DIM)
 NEVER = -1e30
@@ -43,10 +43,6 @@
 
 def rows_of(h):
     return slice(h * HEAD_DIM, (h + 1) * HEAD_DIM)
-
-
-def lanes_of(h):
-    return slice(h * NODES, (h + 1) * NODES)
 
 
 def split_rows(m, core):
@@ -57,39 +53,38 @@
     return jnp.where(first, low, high).reshape(shape), jnp.where(first, high, low).reshape(shape)
 
 
-def stack_lanes(ref, flipped):
-    ref[...] = jnp.zeros(ref.shape, ref.dtype)
-    for h in range(HEADS):
-        ref[rows_of(h), lanes_of(h)] = flipped[rows_of(h)]
-
-
-def stack_rows(ref, rows):
-    head = lax.shift_right_logical(iota(rows.shape, 1), 5)
-    wide = rows.astype(F32)
-    for h in range(HEADS):
-        ref[lanes_of(h), :] = jnp.where(head == h, wide, 0.0).astype(rows.dtype)
-
-
-def call(body, name, outs, scratch, flops, *args, outside=()):
+def call(body, name, outs, scratch, flops, *args, outside=(), vmem=32):
     size = sum(a.size * a.dtype.itemsize for a in args)
-    vmem = pl.BlockSpec(memory_space=pltpu.VMEM)
+    inside = pl.BlockSpec(memory_space=pltpu.VMEM)
     smem = pl.BlockSpec(memory_space=pltpu.SMEM)
     anywhere = pl.BlockSpec(memory_space=pltpu.HBM)
     return pl.pallas_call(
         body,
-        in_specs=[anywhere if i in outside else smem if a.ndim == 1 else vmem for i, a in enumerate(args)],
+        in_specs=[anywhere if i in outside else smem if a.ndim == 1 else inside for i, a in enumerate(args)],
         name=name,
         out_shape=tuple(jax.ShapeDtypeStruct(s, d) for s, d in outs),
         scratch_shapes=[pltpu.VMEM(*s) if isinstance(s, tuple) else s for s in scratch],
-        compiler_params=pltpu.CompilerParams(vmem_limit_bytes=32 * 1024 * 1024),
+        compiler_params=pltpu.CompilerParams(vmem_limit_bytes=vmem * 1024 * 1024),
         cost_estimate=pl.CostEstimate(flops=flops, bytes_accessed=size, transcendentals=0),
     )(*args)
 
 
-def sums_body(x_any, cluster_any, out_ref, low_ref, high_ref, x_ref, cluster_ref, sems):
+def softmax_rows(scores):
+    e = jnp.exp(scores)
+    return e * (1.0 / jnp.sum(e, 0, keepdims=True))
+
+
+def score_grad(prob, g):
+    return (prob * (g - jnp.sum(prob * g, 0, keepdims=True)) * SCORE_SCALE).astype(BF)
+
+
+def sums_body(
+    x_any, cluster_any, links_any, out_ref, low_ref, high_ref, allowed_ref, x_ref, cluster_ref, links_ref, sems
+):
     copies = [
         pltpu.make_async_copy(cluster_any, cluster_ref, sems.at[0]),
         pltpu.make_async_copy(x_any, x_ref, sems.at[1]),
+        pltpu.make_async_copy(links_any, links_ref, sems.at[2]),
     ]
     for copy in copies:
         copy.start()
@@ -100,22 +95,24 @@
     counts = jnp.sum(member, 1, keepdims=True)
     diagonal = iota((SUP, WIDTH), 0) == iota((SUP, WIDTH), 1)
     count_row = jnp.sum(jnp.where(diagonal, counts, 0.0), 0, keepdims=True)
-    out_ref[:SUP] = sums
-    out_ref[SUP:] = jnp.broadcast_to(count_row, (SUM_ROWS - SUP, WIDTH))
+    count_rows = jnp.broadcast_to(count_row, (SUM_ROWS - SUP, WIDTH))
+    message = jnp.concatenate([sums, count_rows], 0).astype(BF)
+    for peer in range(out_ref.shape[0]):
+        out_ref[peer] = message
     low_ref[...] = x_ref[:HALO]
     high_ref[...] = x_ref[NODES - HALO :]
-
-
-def chip_sums_body(parts_ref, out_ref):
-    total = (parts_ref[0] + parts_ref[1]).astype(BF)
-    for peer in range(out_ref.shape[0]):
-        out_ref[peer] = total
+    links = links_ref[...]
+    target = iota((SUP, SUP), 0)
+    linked = links[:1] == target
+    for l in range(1, links.shape[0]):
+        linked = jnp.logical_or(linked, links[l : l + 1] == target)
+    allowed_ref[...] = jnp.where(linked, 0.0, NEVER)
 
 
 def near_body(
-    low_ref, x_ref, high_ref, grad_ref, slots_ref, links_ref, core_ref, wq_ref, wk_ref, wv_ref, wo_ref,
-    qt_ref, at_ref, xt_ref, wt_ref, out_t_ref, gq_t_ref, wkv_ref, base_ref, allowed_ref, chip_ref, outer_ref,
-    q_lanes, a_lanes, q_rows, a_rows, weight_all, score_all, near_t,
+    low_ref, x_ref, high_ref, grad_ref, slots_ref, core_ref, wq_ref, wk_ref, wv_ref, wo_ref,
+    qt_ref, at_ref, xt_ref, wt_ref, out_t_ref, gq_t_ref, wkv_ref, grad_kv_ref, chip_ref,
+    near_t,
 ):
     ext = jnp.concatenate([low_ref[...], x_ref[...], high_ref[...]], 0)
     wk = wk_ref[...]
@@ -130,30 +127,27 @@
     vals_t = flip(vals)
     qt_ref[...] = q_t
     at_ref[...] = a_t
-    stack_lanes(q_lanes, q_t)
-    stack_lanes(a_lanes, a_t)
-    stack_rows(q_rows, queries)
-    stack_rows(a_rows, grad_attn)
     slots = slots_ref[...]
     row = iota((EXT, NODES), 0)
     count = jnp.zeros((EXT, NODES), F32)
     for j in range(slots.shape[0]):
         count = count + jnp.where(slots[j : j + 1] == row, 1.0, 0.0)
     log_count = jnp.where(count > 0.0, jnp.log(jnp.maximum(count, 1.0)), NEVER)
+    gk_t = []
+    gv_t = []
     for h in range(HEADS):
-        score = mm(keys, q_lanes[:, lanes_of(h)])
-        e = jnp.exp(score * SCORE_SCALE + log_count)
-        prob = e * (1.0 / jnp.sum(e, 0, keepdims=True))
+        rows = rows_of(h)
+        prob = softmax_rows(mm(keys[:, rows], q_t[rows]) * SCORE_SCALE + log_count)
         weight = prob.astype(BF)
-        g = mm(vals, a_lanes[:, lanes_of(h)])
-        centre = jnp.sum(prob * g, 0, keepdims=True)
-        d_score = (prob * (g - centre) * SCORE_SCALE).astype(BF)
-        weight_all[:, lanes_of(h)] = weight
-        score_all[:, lanes_of(h)] = d_score
-        near_t[rows_of(h)] = mm(vals_t[rows_of(h)], weight)
-        gq_t_ref[rows_of(h)] = mm(keys_t[rows_of(h)], d_score)
-    grad_keys = mm(score_all[...], q_rows[...]).astype(BF)
-    grad_vals = mm(weight_all[...], a_rows[...]).astype(BF)
+        d_score = score_grad(prob, mm(vals[:, rows], a_t[rows]))
+        near_t[rows] = mm(vals_t[rows], weight)
+        gq_t_ref[rows] = mm(keys_t[rows], d_score)
+        gk_t.append(mm_nt(q_t[rows], d_score))
+        gv_t.append(mm_nt(a_t[rows], weight))
+    gk_t = jnp.concatenate(gk_t, 0).astype(BF)
+    gv_t = jnp.concatenate(gv_t, 0).astype(BF)
+    grad_kv_ref[:WIDTH] = gk_t
+    grad_kv_ref[WIDTH:] = gv_t
     core = core_ref[0]
     ext_t = ext.astype(F32).T
     wt_ref[:WIDTH] = flip(wq_ref[...])
@@ -164,8 +158,8 @@
     near_mine, near_other = split_rows(near_t[...], core)
     out_t_ref[...] = near_mine
     ext_t = ext_t.astype(BF)
-    key_mine, key_other = split_rows(mm(ext_t, grad_keys), core)
-    val_mine, val_other = split_rows(mm(ext_t, grad_vals), core)
+    key_mine, key_other = split_rows(mm_nt(ext_t, gk_t), core)
+    val_mine, val_other = split_rows(mm_nt(ext_t, gv_t), core)
     wkv_ref[0] = key_mine
     wkv_ref[1] = val_mine
     chip = [
@@ -176,35 +170,12 @@
     for part in chip:
         chip_ref[at : at + part.shape[0]] = part.astype(BF)
         at += part.shape[0]
-    back = mm_nt(grad_keys, wk) + mm_nt(grad_vals, wv)
-    base_ref[...] = grad_ref[...].astype(F32) + back[HALO : HALO + NODES]
-    below, above = back[:HALO], back[HALO + NODES :]
-    first = jnp.broadcast_to(core, below.shape) == 0
-    inner = jnp.where(first, above, below).astype(BF)
-    chip_ref[at : at + HALO] = inner[:, :NODES]
-    chip_ref[at + HALO :] = inner[:, NODES:]
-    outer_ref[...] = jnp.where(first, below, above).astype(BF)
-    links = links_ref[...]
-    target = iota((SUP, SUP), 0)
-    linked = links[:1] == target
-    for l in range(1, links.shape[0]):
-        linked = jnp.logical_or(linked, links[l : l + 1] == target)
-    allowed_ref[...] = jnp.where(linked, 0.0, NEVER)
-
-
-def softmax_rows(scores):
-    e = jnp.exp(scores)
-    return e * (1.0 / jnp.sum(e, 0, keepdims=True))
-
-
-def score_grad(prob, g):
-    return (prob * (g - jnp.sum(prob * g, 0, keepdims=True)) * SCORE_SCALE).astype(BF)
 
 
 def far_body(
     parts_ref, allowed_ref, both_ref, grad_ref, wq_ref, wk_ref, wv_ref, wt_ref,
     qt_ref, at_ref, xt_ref, near_t_ref, near_gq_ref, wkv_ref, core_ref,
-    message_ref, gq_t_ref, inner_ref,
+    message_ref, gq_t_ref,
 ):
     core = core_ref[0]
     sibling = both_ref.at[1 - core]
@@ -295,7 +266,6 @@
     rows = near_kv.shape[0] // 4
     near_k = wkv_ref[0] + jnp.concatenate([near_kv[:rows], near_kv[rows : 2 * rows]], 1)
     near_v = wkv_ref[1] + jnp.concatenate([near_kv[2 * rows : 3 * rows], near_kv[3 * rows :]], 1)
-    inner_ref[...] = folded(7)
     grads = [
         mm_nt(jnp.concatenate([x_t, low_rank[:, :SUP]], 1), jnp.concatenate([gq_t, gsq_t], 1)),
         near_k + mm_nt(low_rank, jnp.concatenate([gsk_t, gck_t], 1)),
@@ -316,13 +286,19 @@
             message_ref[w * n_z + z] = jnp.concatenate([rows, piece], 0).astype(BF)
 
 
-def own_body(base_ref, gq_t_ref, wq_ref, inner_ref, outer_ref, core_ref, out_ref):
+def back_body(grad_kv_ref, grad_ref, wk_ref, wv_ref, base_ref, below_ref, above_ref):
+    grad_kv = flip(grad_kv_ref[...])
+    back = mm_nt(grad_kv[:, :WIDTH], wk_ref[...]) + mm_nt(grad_kv[:, WIDTH:], wv_ref[...])
+    base_ref[...] = grad_ref[...].astype(F32) + back[HALO : HALO + NODES]
+    below_ref[...] = back[:HALO].astype(BF)
+    above_ref[...] = back[HALO + NODES :].astype(BF)
+
+
+def own_body(base_ref, gq_t_ref, wq_ref, below_ref, above_ref, out_ref):
     own = base_ref[...] + mm_nt(flip(gq_t_ref[...]), wq_ref[...])
-    inner, outer = inner_ref[...].astype(F32), outer_ref[...].astype(F32)
-    first = jnp.broadcast_to(core_ref[0], inner.shape) == 0
-    out_ref[:HALO] = own[:HALO] + jnp.where(first, outer, inner)
+    out_ref[:HALO] = own[:HALO] + below_ref[...].astype(F32)
     out_ref[HALO : NODES - HALO] = own[HALO : NODES - HALO]
-    out_ref[NODES - HALO :] = own[NODES - HALO :] + jnp.where(first, inner, outer)
+    out_ref[NODES - HALO :] = own[NODES - HALO :] + above_ref[...].astype(F32)
 
 
 def shares_body(n_w, pieces_ref, own_ref, out_ref, pooled_ref):
@@ -368,47 +344,56 @@
     up = [(i, (i + 1) % n_super) for i in range(n_super)]
     down = [(i, (i + n_super - 1) % n_super) for i in range(n_super)]
     cluster_row = cluster.reshape(1, NODES)
-    sums, first_rows, last_rows = call(
+    sums, first_rows, last_rows, allowed = call(
         sums_body,
         "cluster_sums",
-        [((SUM_ROWS, WIDTH), F32), ((HALO, WIDTH), BF), ((HALO, WIDTH), BF)],
-        [((NODES, WIDTH), BF), ((1, NODES), jnp.int32), pltpu.SemaphoreType.DMA((2,))],
+        [((n_z, SUM_ROWS, WIDTH), BF), ((HALO, WIDTH), BF), ((HALO, WIDTH), BF), ((SUP, SUP), F32)],
+        [
+            ((NODES, WIDTH), BF), ((1, NODES), jnp.int32), ((K_TOP, SUP), jnp.int32),
+            pltpu.SemaphoreType.DMA((3,)),
+        ],
         1 << 22,
-        node_feats, cluster_row,
-        outside=(0, 1),
-    )
-    (sums,) = call(
-        chip_sums_body, "chip_sums", [((n_z, SUM_ROWS, WIDTH), BF)], [], 1 << 20, lax.all_gather(sums, "c")
+        node_feats, cluster_row, super_links.T,
+        outside=(0, 1, 2),
+        vmem=60,
     )
     core = lax.axis_index("c").reshape(1)
     low = lax.ppermute(last_rows, supers, up)
     high = lax.ppermute(first_rows, supers, down)
-    parts = swap(sums, "z")
-    q_t, a_t, x_t, w_t, near_t, near_gq, wkv, base, allowed, chip, outer = call(
+    order = [[z // 2 if z % 2 == 0 else n_z - 1 - z // 2 for z in range(n_z)]]
+    parts = lax.all_to_all(sums, "z", 0, 0, axis_index_groups=order, tiled=True)
+    parts = lax.all_gather(parts, "c", tiled=True)
+    q_t, a_t, x_t, w_t, near_t, near_gq, wkv, grad_kv, chip = call(
         near_body,
         "near_attention",
         [
             ((WIDTH, NODES), BF), ((WIDTH, NODES), BF), ((WIDTH // 2, NODES), BF), ((3 * WIDTH, WIDTH), BF),
-            ((WIDTH // 2, NODES), F32), ((WIDTH, NODES), F32), ((2, WIDTH // 2, WIDTH), F32), ((NODES, WIDTH), F32),
-            ((SUP, SUP), F32), ((CHIP_AT[-1], NODES), BF), ((HALO, WIDTH), BF),
+            ((WIDTH // 2, NODES), F32), ((WIDTH, NODES), F32), ((2, WIDTH // 2, WIDTH), F32), ((2 * WIDTH, EXT), BF),
+            ((CHIP_AT[-1], NODES), BF),
         ],
         [
-            ((WIDTH, STACK), BF), ((WIDTH, STACK), BF), ((STACK, WIDTH), BF), ((STACK, WIDTH), BF),
-            ((EXT, STACK), BF), ((EXT, STACK), BF), ((WIDTH, NODES), F32),
+            ((WIDTH, NODES), F32),
         ],
         10 << 30,
-        low, node_feats, high, grad_out, neighbours.T, super_links.T, core, w_query, w_key, w_value, w_out,
-    )
-    outward = [(2 * z, (2 * z - 1) % n_super) for z in range(n_z)]
-    outward += [(2 * z + 1, (2 * z + 2) % n_super) for z in range(n_z)]
-    outer = lax.ppermute(outer, supers, outward)
+        low, node_feats, high, grad_out, neighbours.T, core, w_query, w_key, w_value, w_out,
+    )
+    base, below, above = call(
+        back_body,
+        "halo_returns",
+        [((NODES, WIDTH), F32), ((HALO, WIDTH), BF), ((HALO, WIDTH), BF)],
+        [],
+        1 << 28,
+        grad_kv, grad_out, w_key, w_value,
+    )
+    from_above = lax.ppermute(below, supers, down)
+    from_below = lax.ppermute(above, supers, up)
     share_rows = WIDTH // n_super
     half = (SUP // 2, WIDTH)
     message_rows = share_rows + SUP // 2 // n_x
-    pieces, gq_t, inner = call(
+    pieces, gq_t = call(
         far_body,
         "far_attention",
-        [((n_x * n_z, message_rows, WIDTH), BF), ((WIDTH, NODES), BF), ((HALO, WIDTH), BF)],
+        [((n_x * n_z, message_rows, WIDTH), BF), ((WIDTH, NODES), BF)],
         [],
         10 << 30,
         parts, allowed, lax.all_gather(chip, "c"), grad_out, w_query, w_key, w_value, w_t,
@@ -416,7 +401,7 @@
     )
     pieces = swap(pieces, ("x", "z"))
     (own,) = call(
-        own_body, "own_nodes", [((NODES, WIDTH), F32)], [], 1 << 28, base, gq_t, w_query, inner, outer, core
+        own_body, "own_nodes", [((NODES, WIDTH), F32)], [], 1 << 28, base, gq_t, w_query, from_below, from_above
     )
     shares, pooled = call(
         functools.partial(shares_body, n_x),

time: 80.8 us -> 79.7 us (0.986)
  local copies, waits for them, and re-layouts: 2.12 us -> 0.04 us
  starting transfers between devices: 27.6 us -> 28.6 us
    all_to_all x0 -> x1, starting transfers between devices: none -> 11.3 us  [local(): parts = lax.all_to_all(sums, 'z', 0, 0, axis_index_groups=order, tiled=True)]
    all_to_all x3 -> x2, starting transfers between devices: 23.9 us -> 13.8 us  [swap(): return lax.all_to_all(parts, axes, 0, 0, tiled=True)]
    all_to_all x3 -> x2, waiting for transfers between devices: 18 us -> 12.9 us  [swap(): return lax.all_to_all(parts, axes, 0, 0, tiled=True)]
    all_to_all x0 -> x1, waiting for transfers between devices: none -> 3.65 us  [local(): parts = lax.all_to_all(sums, 'z', 0, 0, axis_index_groups=order, tiled=True)]
    unnamed x20 -> x18, local copies, waits for them, and re-layouts: 2.12 us -> 0.04 us
    pallas_call x8, Pallas kernels: 11.1 us -> 11.9 us  [call(): pl.pallas_call(body, in_specs=[anywhere if i in outside else smem if a.nd...]
    ppermute x1 -> x2, waiting for transfers between devices: 6.06 us -> 6.67 us  [the longest x1 5.15 us: local(): from_below = lax.ppermute(above, supers, up)]
    ppermute x1 -> x2, starting transfers between devices: 1.92 us -> 1.75 us  [the longest x1 1.73 us: local(): from_above = lax.ppermute(below, supers, down)]
  transfers between devices with their start and end apart: 6 -> 7, of which waited for: 4 -> 5; matrix products, arithmetic and copies ran while one was open for 0% -> 0% of each run, Pallas kernels for 5% -> 4%
where the time goes in v5:
time: 79.7 us; the launch traced here: 79.2 us
  starting transfers between devices  28.6 us (36%)
  waiting for transfers between devices  23.3 us (29%)
  blocking collectives  14.6 us (18%)
  Pallas kernels  11.9 us (15%)
    all_to_all x2, starting transfers between devices, swap(): return lax.all_to_all(parts, axes, 0, 0, tiled=True)  13.8 us
    all_to_all x2, waiting for transfers between devices, swap(): return lax.all_to_all(parts, axes, 0, 0, tiled=True)  12.9 us
    pallas_call x8, Pallas kernels, call(): pl.pallas_call(body, in_specs=[anywhere if i in outside else smem if a.nd...  11.9 us
    all_to_all x1, starting transfers between devices, local(): parts = lax.all_to_all(sums, 'z', 0, 0, axis_index_groups=order, tiled=True)  11.3 us
    all_to_all x1, blocking collectives, swap(): return lax.all_to_all(parts, axes, 0, 0, tiled=True)  8.06 us
    ppermute x1, waiting for transfers between devices, local(): from_below = lax.ppermute(above, supers, up)  5.15 us
    all_to_all x1, waiting for transfers between devices, local(): parts = lax.all_to_all(sums, 'z', 0, 0, axis_index_groups=order, tiled=True)  3.65 us
    all_gather x1, blocking collectives, local(): lax.all_gather(chip, 'c')  2.46 us
  transfers between devices with their start and end apart: 7, of which 5 were waited for; matrix products, arithmetic and copies ran while one was open for 0% of the time, Pallas kernels for 4%

profile of v5, /device:TPU:64, one launch (start us, length us, event | category | flops | bytes accessed | tf_op | source)
XLA Modules:
  0.0 79.2 jit_solution(1787847272404002702)
XLA Ops:
  0.6 0.0 copy-start.6
  0.6 0.0 copy-start.8
  0.7 1.8 %cluster_sums.1 = (bf16[8,72,256]{2,1,0:T(8,128)(2,1)}, bf16[32,256]{1,0:T(8,128)(2,1)}, bf16[32,256]{1,0:T(8,128)(2,1)}, f32[64,64]{1,0:T(8,128)}) custom-call(bf16[128,256]{1,0:T(8,128)(2,1)} %x_ref.1, s32[1,128]{1,0:T(1,128)} %bitcast.8, s32[8,64]{1,0:T(8,128)} %bitcast.11), custom_call_target="tpu_custom_call" | custom-call | flops 4194304 | bytes 68096 | tf_op jit(solution)/shard_map/cluster_sums/pallas_call | solution.py:61
  2.4 0.0 collective-permute-start
  2.5 1.7 %collective-permute-start.1 = (bf16[32,256]{1,0:T(8,128)(2,1)}, bf16[32,256]{1,0:T(8,128)(2,1)S(1)}, u32[]{:S(2)}, u32[]{:S(2)}) collective-permute-start(bf16[32,256]{1,0:T(8,128)(2,1)} %get-tuple-element.27), channel_id=1, source_target_pairs={{0,15},{1,0},{2,1},{3,2},{4,3},{5,4},{6,5},{7,6},{8,7},{9,8},{10,9... | collective-permute-start | bytes 49160 | tf_op jit(solution)/shard_map/ppermute | solution.py:362
  4.2 0.0 copy-start
  4.2 0.0 copy-start.2
  4.2 0.0 copy-start.3
  4.2 0.0 copy-start.4
  4.2 0.0 copy-start.5
  4.2 11.3 %all-to-all-start = ((bf16[8,72,256]{2,1,0:T(8,128)(2,1)}), bf16[8,72,256]{2,1,0:T(8,128)(2,1)S(1)}, u32[]{:S(2)}, u32[]{:S(2)}) async-start(bf16[8,72,256]{2,1,0:T(8,128)(2,1)} %get-tuple-element.24), calls=%async_computation | async-start | bytes 589824 | tf_op jit(solution)/shard_map/all_to_all | solution.py:364
  15.5 0.0 collective-permute-done.low_ref
  15.5 0.0 collective-permute-done.1.high_ref
  15.5 0.0 copy-done.6
  15.5 0.0 copy-done.8
  15.5 0.0 copy-done
  15.6 0.0 copy-done.2
  15.6 0.0 copy-done.3
  15.6 0.0 copy-done.4
  15.6 0.0 copy-done.5
  15.6 3.0 %near_attention.1 = (bf16[256,128]{1,0:T(8,128)(2,1)S(1)}, bf16[256,128]{1,0:T(8,128)(2,1)S(1)}, bf16[128,128]{1,0:T(8,128)(2,1)S(1)}, bf16[768,256]{1,0:T(8,128...) custom-call(bf16[32,256]{1,0:T(8,128)(2,1)S(1)} %collective-permute-, ...), custom_call_target="tpu_custom_call" | custom-call | flops 10737418240 | bytes 704516 | tf_op jit(solution)/shard_map/near_attention/pallas_call | solution.py:61
  18.6 2.5 %all-gather = bf16[3584,128]{1,0:T(8,128)(2,1)S(1)} all-gather(bf16[1792,128]{1,0:T(8,128)(2,1)S(1)} %get-tuple-element.28), channel_id=2, replica_groups=mesh['x'=4,'y'=8,'z'=8,'c'=2] {'c'}, dimensions={0}, use_global_device_ids=true | all-gather | bytes 1376256 | tf_op jit(solution)/shard_map/all_gather | solution.py:399
  21.0 0.0 copy-start.7
  21.0 3.6 %all-to-all-done = bf16[8,72,256]{2,1,0:T(8,128)(2,1)S(1)} async-done(((bf16[8,72,256]{2,1,0:T(8,128)(2,1)}), bf16[8,72,256]{2,1,0:T(8,128)(2,1)S(1)}, u32[]{:S(2)}, u32[]{:S(2)}) %all-to-all-start) | async-done | bytes 294944 | tf_op jit(solution)/shard_map/all_to_all | solution.py:364
  24.7 2.2 %all_gather.15.parts_ref = bf16[16,72,256]{2,1,0:T(8,128)(2,1)S(1)} all-gather(bf16[8,72,256]{2,1,0:T(8,128)(2,1)S(1)} %all-to-all-done), channel_id=1, replica_groups=mesh['x'=4,'y'=8,'z'=8,'c'=2] {'c'}, dimensions={0}, use_global_device_ids=true | all-gather | bytes 884736 | tf_op jit(solution)/shard_map/all_gather | solution.py:365
  26.9 0.0 copy-done.7
  26.9 5.2 %far_attention.1 = (bf16[32,24,256]{2,1,0:T(8,128)(2,1)}, bf16[256,128]{1,0:T(8,128)(2,1)S(1)}) custom-call(bf16[16,72,256]{2,1,0:T(8,128)(2,1)S(1)} %all_gather.15.parts_ref, f32[64,64]{1,0:T(8,128)S(1)} %copy-done.7, bf16[2,1792,128]{2,1,0:T(8,128)(2,1)S(1)} %bitcast.6, bf16[128,256]{1,0:T(8,128)(2,1)S(1)} %copy-done.6, bf16[256,256]{1,0:T(8,128)(2,1)S(1)} %copy-done.5, ...), custom_call_target="tpu_custom_call" | custom-call | flops 10737418240 | bytes 2998276 | tf_op jit(solution)/shard_map/far_attention/pallas_call | solution.py:61
  32.1 6.7 %all-to-all-start.1 = ((bf16[32,24,256]{2,1,0:T(8,128)(2,1)}), bf16[32,24,256]{2,1,0:T(8,128)(2,1)S(1)}, u32[]{:S(2)}, u32[]{:S(2)}) async-start(bf16[32,24,256]{2,1,0:T(8,128)(2,1)} %get-tuple-element.36), calls=%async_computation.1 | async-start | bytes 786432 | tf_op jit(solution)/shard_map/all_to_all | solution.py:336
  38.8 0.3 halo_returns.1
  39.0 0.0 collective-permute-start.2
  39.1 1.7 %collective-permute-start.3 = (bf16[32,256]{1,0:T(8,128)(2,1)S(1)}, bf16[32,256]{1,0:T(8,128)(2,1)S(1)}, u32[]{:S(2)}, u32[]{:S(2)}) collective-permute-start(bf16[32,256]{1,0:T(8,128)(2,1)S(1)} %get-tuple-element.41), channel_id=1, source_target_pairs={{0,15},{1,0},{2,1},{3,2},{4,3},{5,4},{6,5},{7,6},{8,7},{9,8},{10,9... | collective-permute-start | bytes 49160 | tf_op jit(solution)/shard_map/ppermute | solution.py:388
  40.8 5.1 %collective-permute-done.2.below_ref = bf16[32,256]{1,0:T(8,128)(2,1)S(1)} collective-permute-done((bf16[32,256]{1,0:T(8,128)(2,1)S(1)}, bf16[32,256]{1,0:T(8,128)(2,1)S(1)}, u32[]{:S(2)}, u32[]{:S(2)}) %collective-permute-start.2) | collective-permute-done | bytes 16416 | tf_op jit(solution)/shard_map/ppermute | solution.py:389
  45.9 1.5 %collective-permute-done.3.above_ref = bf16[32,256]{1,0:T(8,128)(2,1)S(1)} collective-permute-done((bf16[32,256]{1,0:T(8,128)(2,1)S(1)}, bf16[32,256]{1,0:T(8,128)(2,1)S(1)}, u32[]{:S(2)}, u32[]{:S(2)}) %collective-permute-start.3) | collective-permute-done | bytes 16416 | tf_op jit(solution)/shard_map/ppermute | solution.py:388
  47.5 0.2 own_nodes.1.own_ref
  47.7 6.4 %all-to-all-done.1.pieces_ref = bf16[32,24,256]{2,1,0:T(8,128)(2,1)S(1)} async-done(((bf16[32,24,256]{2,1,0:T(8,128)(2,1)}), bf16[32,24,256]{2,1,0:T(8,128)(2,1)S(1)}, u32[]{:S(2)}, u32[]{:S(2)}) %all-to-all-start.1) | async-done | bytes 393248 | tf_op jit(solution)/shard_map/all_to_all | solution.py:336
  54.1 0.7 weight_shares.1
  54.8 7.1 %all-to-all-start.2 = ((bf16[8,16,256]{2,1,0:T(8,128)(2,1)}), bf16[8,16,256]{2,1,0:T(8,128)(2,1)S(1)}, u32[]{:S(2)}, u32[]{:S(2)}) async-start(bf16[8,16,256]{2,1,0:T(8,128)(2,1)} %get-tuple-element.42), calls=%async_computation.2 | async-start | bytes 131072 | tf_op jit(solution)/shard_map/all_to_all | solution.py:336
  61.8 1.8 %all-gather.1 = bf16[64,256]{1,0:T(8,128)(2,1)S(1)} all-gather(bf16[32,256]{1,0:T(8,128)(2,1)S(1)} %get-tuple-element.43), channel_id=3, replica_groups=mesh['x'=4,'y'=8,'z'=8,'c'=2] {'c'}, dimensions={0}, use_global_device_ids=true | all-gather | bytes 49152 | tf_op jit(solution)/shard_map/all_gather | solution.py:422
  63.7 6.6 %all-to-all-done.2.parts_ref = bf16[8,16,256]{2,1,0:T(8,128)(2,1)S(1)} async-done(((bf16[8,16,256]{2,1,0:T(8,128)(2,1)}), bf16[8,16,256]{2,1,0:T(8,128)(2,1)S(1)}, u32[]{:S(2)}, u32[]{:S(2)}) %all-to-all-start.2) | async-done | bytes 65568 | tf_op jit(solution)/shard_map/all_to_all | solution.py:336
  70.2 0.0 copy-start.1
  70.3 8.1 %all_to_all.20.parts_ref = bf16[4,32,256]{2,1,0:T(8,128)(2,1)S(1)} all-to-all(bf16[4,32,256]{2,1,0:T(8,128)(2,1)S(1)} %weight_columns.1), channel_id=1, replica_groups=mesh['x'=4,'y'=8,'z'=8,'c'=2] {'x'}, dimensions={0} | all-to-all | bytes 131072 | tf_op jit(solution)/shard_map/all_to_all | solution.py:336
  78.3 0.0 copy-done.1
  78.3 0.9 %gradients.1 = (f32[4,16,256]{2,1,0:T(8,128)}, bf16[128,256]{1,0:T(8,128)(2,1)}) custom-call(bf16[4,32,256]{2,1,0:T(8,128)(2,1)S(1)} %all_to_all.20.parts_ref, f32[128,256]{1,0:T(8,128)S(1)} %own_nodes.1.own_ref, s32[1,128]{1,0:T(1,128)S(1)} %bitcast.9), custom_call_target="tpu_custom_call" | custom-call | flops 1048576 | bytes 197120 | tf_op jit(solution)/shard_map/gradients/pallas_call | solution.py:61
  (1 shorter events, 0.0 us)
Async XLA Ops:
  0.6 14.9 %copy-start.6 = (bf16[128,256]{1,0:T(8,128)(2,1)S(1)}, bf16[128,256]{1,0:T(8,128)(2,1)}, u32[]{:S(2)}) copy-start(bf16[128,256]{1,0:T(8,128)(2,1)} %grad_ref.5) | copy-start | bytes 196612
  0.6 14.9 %copy-start.8 = (s32[128,32]{0,1:T(8,128)S(1)}, s32[128,32]{0,1:T(8,128)}, u32[]{:S(2)}) copy-start(s32[128,32]{0,1:T(8,128)} %param.11) | copy-start | bytes 49156
  2.4 13.1 %collective-permute-start = (bf16[32,256]{1,0:T(8,128)(2,1)}, bf16[32,256]{1,0:T(8,128)(2,1)S(1)}, u32[]{:S(2)}, u32[]{:S(2)}) collective-permute-start(bf16[32,256]{1,0:T(8,128)(2,1)} %get-tuple-element.26), channel_id=1, source_target_pairs={{0,1},{1,2},{2,3},{3,4},{4,5},{5,6},{6,7},{7,8},{8,9},{9,10},{10,1... | collective-permute-start | bytes 49160 | tf_op jit(solution)/shard_map/ppermute | solution.py:361
  2.5 13.1 %collective-permute-start.1 = (bf16[32,256]{1,0:T(8,128)(2,1)}, bf16[32,256]{1,0:T(8,128)(2,1)S(1)}, u32[]{:S(2)}, u32[]{:S(2)}) collective-permute-start(bf16[32,256]{1,0:T(8,128)(2,1)} %get-tuple-element.27), channel_id=1, source_target_pairs={{0,15},{1,0},{2,1},{3,2},{4,3},{5,4},{6,5},{7,6},{8,7},{9,8},{10,9... | collective-permute-start | bytes 49160 | tf_op jit(solution)/shard_map/ppermute | solution.py:362
  4.2 11.3 %copy-start = (bf16[128,256]{1,0:T(8,128)(2,1)S(1)}, bf16[128,256]{1,0:T(8,128)(2,1)}, u32[]{:S(2)}) copy-start(bf16[128,256]{1,0:T(8,128)(2,1)} %x_ref.1) | copy-start | bytes 196612
  4.2 11.4 %copy-start.2 = (bf16[256,256]{1,0:T(8,128)(2,1)S(1)}, bf16[256,256]{1,0:T(8,128)(2,1)}, u32[]{:S(2)}) copy-start(bf16[256,256]{1,0:T(8,128)(2,1)} %wo_ref.1) | copy-start | bytes 393220
  4.2 11.4 %copy-start.3 = (bf16[256,256]{1,0:T(8,128)(2,1)S(1)}, bf16[256,256]{1,0:T(8,128)(2,1)}, u32[]{:S(2)}) copy-start(bf16[256,256]{1,0:T(8,128)(2,1)} %wk_ref.5) | copy-start | bytes 393220
  4.2 11.4 %copy-start.4 = (bf16[256,256]{1,0:T(8,128)(2,1)S(1)}, bf16[256,256]{1,0:T(8,128)(2,1)}, u32[]{:S(2)}) copy-start(bf16[256,256]{1,0:T(8,128)(2,1)} %wv_ref.5) | copy-start | bytes 393220
  4.2 11.4 %copy-start.5 = (bf16[256,256]{1,0:T(8,128)(2,1)S(1)}, bf16[256,256]{1,0:T(8,128)(2,1)}, u32[]{:S(2)}) copy-start(bf16[256,256]{1,0:T(8,128)(2,1)} %wq_ref.5) | copy-start | bytes 393220
  4.2 20.5 %all-to-all-start = ((bf16[8,72,256]{2,1,0:T(8,128)(2,1)}), bf16[8,72,256]{2,1,0:T(8,128)(2,1)S(1)}, u32[]{:S(2)}, u32[]{:S(2)}) async-start(bf16[8,72,256]{2,1,0:T(8,128)(2,1)} %get-tuple-element.24), calls=%async_computation | async-start | bytes 589824 | tf_op jit(solution)/shard_map/all_to_all | solution.py:364
  21.0 5.9 %copy-start.7 = (f32[64,64]{1,0:T(8,128)S(1)}, f32[64,64]{1,0:T(8,128)}, u32[]{:S(2)}) copy-start(f32[64,64]{1,0:T(8,128)} %get-tuple-element.25.allowed_ref) | copy-start | bytes 49156
  32.1 22.0 %all-to-all-start.1 = ((bf16[32,24,256]{2,1,0:T(8,128)(2,1)}), bf16[32,24,256]{2,1,0:T(8,128)(2,1)S(1)}, u32[]{:S(2)}, u32[]{:S(2)}) async-start(bf16[32,24,256]{2,1,0:T(8,128)(2,1)} %get-tuple-element.36), calls=%async_computation.1 | async-start | bytes 786432 | tf_op jit(solution)/shard_map/all_to_all | solution.py:336
  39.0 6.9 %collective-permute-start.2 = (bf16[32,256]{1,0:T(8,128)(2,1)S(1)}, bf16[32,256]{1,0:T(8,128)(2,1)S(1)}, u32[]{:S(2)}, u32[]{:S(2)}) collective-permute-start(bf16[32,256]{1,0:T(8,128)(2,1)S(1)} %get-tuple-element.40), channel_id=1, source_target_pairs={{0,1},{1,2},{2,3},{3,4},{4,5},{5,6},{6,7},{7,8},{8,9},{9,10},{10,1... | collective-permute-start | bytes 49160 | tf_op jit(solution)/shard_map/ppermute | solution.py:389
  39.1 8.4 %collective-permute-start.3 = (bf16[32,256]{1,0:T(8,128)(2,1)S(1)}, bf16[32,256]{1,0:T(8,128)(2,1)S(1)}, u32[]{:S(2)}, u32[]{:S(2)}) collective-permute-start(bf16[32,256]{1,0:T(8,128)(2,1)S(1)} %get-tuple-element.41), channel_id=1, source_target_pairs={{0,15},{1,0},{2,1},{3,2},{4,3},{5,4},{6,5},{7,6},{8,7},{9,8},{10,9... | collective-permute-start | bytes 49160 | tf_op jit(solution)/shard_map/ppermute | solution.py:388
  54.8 15.5 %all-to-all-start.2 = ((bf16[8,16,256]{2,1,0:T(8,128)(2,1)}), bf16[8,16,256]{2,1,0:T(8,128)(2,1)S(1)}, u32[]{:S(2)}, u32[]{:S(2)}) async-start(bf16[8,16,256]{2,1,0:T(8,128)(2,1)} %get-tuple-element.42), calls=%async_computation.2 | async-start | bytes 131072 | tf_op jit(solution)/shard_map/all_to_all | solution.py:336
  70.2 8.1 %copy-start.1 = (s32[128]{0:T(128)S(1)}, s32[128]{0:T(128)}, u32[]{:S(2)}) copy-start(s32[128]{0:T(128)} %param.12) | copy-start | bytes 1540

commit v6 on v5

--- a/solution.py
+++ b/solution.py
@@ -71,7 +71,7 @@
 
 def softmax_rows(scores):
     e = jnp.exp(scores)
-    return e * (1.0 / jnp.sum(e, 0, keepdims=True))
+    return e / jnp.sum(e, 0, keepdims=True)
 
 
 def score_grad(prob, g):

time: 79.7 us -> 79.7 us (level)
  no operation moved by 1% of the time
where the time goes in v6:
time: 79.7 us; the launch traced here: 79.2 us
  starting transfers between devices  28.6 us (36%)
  waiting for transfers between devices  23.3 us (29%)
  blocking collectives  14.6 us (18%)
  Pallas kernels  11.9 us (15%)
    all_to_all x2, starting transfers between devices, swap(): return lax.all_to_all(parts, axes, 0, 0, tiled=True)  13.8 us
    all_to_all x2, waiting for transfers between devices, swap(): return lax.all_to_all(parts, axes, 0, 0, tiled=True)  12.9 us
    pallas_call x8, Pallas kernels, call(): pl.pallas_call(body, in_specs=[anywhere if i in outside else smem if a.nd...  11.9 us
    all_to_all x1, starting transfers between devices, local(): parts = lax.all_to_all(sums, 'z', 0, 0, axis_index_groups=order, tiled=True)  11.3 us
    all_to_all x1, blocking collectives, swap(): return lax.all_to_all(parts, axes, 0, 0, tiled=True)  8.06 us
    ppermute x1, waiting for transfers between devices, local(): from_below = lax.ppermute(above, supers, up)  5.15 us
    all_to_all x1, waiting for transfers between devices, local(): parts = lax.all_to_all(sums, 'z', 0, 0, axis_index_groups=order, tiled=True)  3.65 us
    all_gather x1, blocking collectives, local(): lax.all_gather(chip, 'c')  2.46 us
  transfers between devices with their start and end apart: 7, of which 5 were waited for; matrix products, arithmetic and copies ran while one was open for 0% of the time, Pallas kernels for 4%

profile of v6, /device:TPU:64, one launch (start us, length us, event | category | flops | bytes accessed | tf_op | source)
XLA Modules:
  0.0 79.2 jit_solution(1787847272404002702)
XLA Ops:
  0.6 0.0 copy-start.6
  0.6 0.0 copy-start.8
  0.7 1.8 %cluster_sums.1 = (bf16[8,72,256]{2,1,0:T(8,128)(2,1)}, bf16[32,256]{1,0:T(8,128)(2,1)}, bf16[32,256]{1,0:T(8,128)(2,1)}, f32[64,64]{1,0:T(8,128)}) custom-call(bf16[128,256]{1,0:T(8,128)(2,1)} %x_ref.1, s32[1,128]{1,0:T(1,128)} %bitcast.8, s32[8,64]{1,0:T(8,128)} %bitcast.11), custom_call_target="tpu_custom_call" | custom-call | flops 4194304 | bytes 68096 | tf_op jit(solution)/shard_map/cluster_sums/pallas_call | solution.py:61
  2.4 0.0 collective-permute-start
  2.5 1.7 %collective-permute-start.1 = (bf16[32,256]{1,0:T(8,128)(2,1)}, bf16[32,256]{1,0:T(8,128)(2,1)S(1)}, u32[]{:S(2)}, u32[]{:S(2)}) collective-permute-start(bf16[32,256]{1,0:T(8,128)(2,1)} %get-tuple-element.27), channel_id=1, source_target_pairs={{0,15},{1,0},{2,1},{3,2},{4,3},{5,4},{6,5},{7,6},{8,7},{9,8},{10,9... | collective-permute-start | bytes 49160 | tf_op jit(solution)/shard_map/ppermute | solution.py:362
  4.2 0.0 copy-start
  4.2 0.0 copy-start.2
  4.2 0.0 copy-start.3
  4.2 0.0 copy-start.4
  4.2 0.0 copy-start.5
  4.2 11.3 %all-to-all-start = ((bf16[8,72,256]{2,1,0:T(8,128)(2,1)}), bf16[8,72,256]{2,1,0:T(8,128)(2,1)S(1)}, u32[]{:S(2)}, u32[]{:S(2)}) async-start(bf16[8,72,256]{2,1,0:T(8,128)(2,1)} %get-tuple-element.24), calls=%async_computation | async-start | bytes 589824 | tf_op jit(solution)/shard_map/all_to_all | solution.py:364
  15.5 0.0 collective-permute-done.low_ref
  15.5 0.0 collective-permute-done.1.high_ref
  15.5 0.0 copy-done.6
  15.5 0.0 copy-done.8
  15.5 0.0 copy-done
  15.6 0.0 copy-done.2
  15.6 0.0 copy-done.3
  15.6 0.0 copy-done.4
  15.6 0.0 copy-done.5
  15.6 3.0 %near_attention.1 = (bf16[256,128]{1,0:T(8,128)(2,1)S(1)}, bf16[256,128]{1,0:T(8,128)(2,1)S(1)}, bf16[128,128]{1,0:T(8,128)(2,1)S(1)}, bf16[768,256]{1,0:T(8,128...) custom-call(bf16[32,256]{1,0:T(8,128)(2,1)S(1)} %collective-permute-, ...), custom_call_target="tpu_custom_call" | custom-call | flops 10737418240 | bytes 704516 | tf_op jit(solution)/shard_map/near_attention/pallas_call | solution.py:61
  18.6 2.5 %all-gather = bf16[3584,128]{1,0:T(8,128)(2,1)S(1)} all-gather(bf16[1792,128]{1,0:T(8,128)(2,1)S(1)} %get-tuple-element.28), channel_id=2, replica_groups=mesh['x'=4,'y'=8,'z'=8,'c'=2] {'c'}, dimensions={0}, use_global_device_ids=true | all-gather | bytes 1376256 | tf_op jit(solution)/shard_map/all_gather | solution.py:399
  21.0 0.0 copy-start.7
  21.0 3.6 %all-to-all-done = bf16[8,72,256]{2,1,0:T(8,128)(2,1)S(1)} async-done(((bf16[8,72,256]{2,1,0:T(8,128)(2,1)}), bf16[8,72,256]{2,1,0:T(8,128)(2,1)S(1)}, u32[]{:S(2)}, u32[]{:S(2)}) %all-to-all-start) | async-done | bytes 294944 | tf_op jit(solution)/shard_map/all_to_all | solution.py:364
  24.7 2.2 %all_gather.15.parts_ref = bf16[16,72,256]{2,1,0:T(8,128)(2,1)S(1)} all-gather(bf16[8,72,256]{2,1,0:T(8,128)(2,1)S(1)} %all-to-all-done), channel_id=1, replica_groups=mesh['x'=4,'y'=8,'z'=8,'c'=2] {'c'}, dimensions={0}, use_global_device_ids=true | all-gather | bytes 884736 | tf_op jit(solution)/shard_map/all_gather | solution.py:365
  26.9 0.0 copy-done.7
  26.9 5.2 %far_attention.1 = (bf16[32,24,256]{2,1,0:T(8,128)(2,1)}, bf16[256,128]{1,0:T(8,128)(2,1)S(1)}) custom-call(bf16[16,72,256]{2,1,0:T(8,128)(2,1)S(1)} %all_gather.15.parts_ref, f32[64,64]{1,0:T(8,128)S(1)} %copy-done.7, bf16[2,1792,128]{2,1,0:T(8,128)(2,1)S(1)} %bitcast.6, bf16[128,256]{1,0:T(8,128)(2,1)S(1)} %copy-done.6, bf16[256,256]{1,0:T(8,128)(2,1)S(1)} %copy-done.5, ...), custom_call_target="tpu_custom_call" | custom-call | flops 10737418240 | bytes 2998276 | tf_op jit(solution)/shard_map/far_attention/pallas_call | solution.py:61
  32.1 6.7 %all-to-all-start.1 = ((bf16[32,24,256]{2,1,0:T(8,128)(2,1)}), bf16[32,24,256]{2,1,0:T(8,128)(2,1)S(1)}, u32[]{:S(2)}, u32[]{:S(2)}) async-start(bf16[32,24,256]{2,1,0:T(8,128)(2,1)} %get-tuple-element.36), calls=%async_computation.1 | async-start | bytes 786432 | tf_op jit(solution)/shard_map/all_to_all | solution.py:336
  38.8 0.3 halo_returns.1
  39.0 0.0 collective-permute-start.2
  39.1 1.7 %collective-permute-start.3 = (bf16[32,256]{1,0:T(8,128)(2,1)S(1)}, bf16[32,256]{1,0:T(8,128)(2,1)S(1)}, u32[]{:S(2)}, u32[]{:S(2)}) collective-permute-start(bf16[32,256]{1,0:T(8,128)(2,1)S(1)} %get-tuple-element.41), channel_id=1, source_target_pairs={{0,15},{1,0},{2,1},{3,2},{4,3},{5,4},{6,5},{7,6},{8,7},{9,8},{10,9... | collective-permute-start | bytes 49160 | tf_op jit(solution)/shard_map/ppermute | solution.py:388
  40.8 5.1 %collective-permute-done.2.below_ref = bf16[32,256]{1,0:T(8,128)(2,1)S(1)} collective-permute-done((bf16[32,256]{1,0:T(8,128)(2,1)S(1)}, bf16[32,256]{1,0:T(8,128)(2,1)S(1)}, u32[]{:S(2)}, u32[]{:S(2)}) %collective-permute-start.2) | collective-permute-done | bytes 16416 | tf_op jit(solution)/shard_map/ppermute | solution.py:389
  45.9 1.5 %collective-permute-done.3.above_ref = bf16[32,256]{1,0:T(8,128)(2,1)S(1)} collective-permute-done((bf16[32,256]{1,0:T(8,128)(2,1)S(1)}, bf16[32,256]{1,0:T(8,128)(2,1)S(1)}, u32[]{:S(2)}, u32[]{:S(2)}) %collective-permute-start.3) | collective-permute-done | bytes 16416 | tf_op jit(solution)/shard_map/ppermute | solution.py:388
  47.5 0.2 own_nodes.1.own_ref
  47.7 6.4 %all-to-all-done.1.pieces_ref = bf16[32,24,256]{2,1,0:T(8,128)(2,1)S(1)} async-done(((bf16[32,24,256]{2,1,0:T(8,128)(2,1)}), bf16[32,24,256]{2,1,0:T(8,128)(2,1)S(1)}, u32[]{:S(2)}, u32[]{:S(2)}) %all-to-all-start.1) | async-done | bytes 393248 | tf_op jit(solution)/shard_map/all_to_all | solution.py:336
  54.1 0.7 weight_shares.1
  54.8 7.1 %all-to-all-start.2 = ((bf16[8,16,256]{2,1,0:T(8,128)(2,1)}), bf16[8,16,256]{2,1,0:T(8,128)(2,1)S(1)}, u32[]{:S(2)}, u32[]{:S(2)}) async-start(bf16[8,16,256]{2,1,0:T(8,128)(2,1)} %get-tuple-element.42), calls=%async_computation.2 | async-start | bytes 131072 | tf_op jit(solution)/shard_map/all_to_all | solution.py:336
  61.8 1.8 %all-gather.1 = bf16[64,256]{1,0:T(8,128)(2,1)S(1)} all-gather(bf16[32,256]{1,0:T(8,128)(2,1)S(1)} %get-tuple-element.43), channel_id=3, replica_groups=mesh['x'=4,'y'=8,'z'=8,'c'=2] {'c'}, dimensions={0}, use_global_device_ids=true | all-gather | bytes 49152 | tf_op jit(solution)/shard_map/all_gather | solution.py:422
  63.7 6.6 %all-to-all-done.2.parts_ref = bf16[8,16,256]{2,1,0:T(8,128)(2,1)S(1)} async-done(((bf16[8,16,256]{2,1,0:T(8,128)(2,1)}), bf16[8,16,256]{2,1,0:T(8,128)(2,1)S(1)}, u32[]{:S(2)}, u32[]{:S(2)}) %all-to-all-start.2) | async-done | bytes 65568 | tf_op jit(solution)/shard_map/all_to_all | solution.py:336
  70.2 0.0 copy-start.1
  70.3 8.1 %all_to_all.20.parts_ref = bf16[4,32,256]{2,1,0:T(8,128)(2,1)S(1)} all-to-all(bf16[4,32,256]{2,1,0:T(8,128)(2,1)S(1)} %weight_columns.1), channel_id=1, replica_groups=mesh['x'=4,'y'=8,'z'=8,'c'=2] {'x'}, dimensions={0} | all-to-all | bytes 131072 | tf_op jit(solution)/shard_map/all_to_all | solution.py:336
  78.3 0.0 copy-done.1
  78.3 0.9 %gradients.1 = (f32[4,16,256]{2,1,0:T(8,128)}, bf16[128,256]{1,0:T(8,128)(2,1)}) custom-call(bf16[4,32,256]{2,1,0:T(8,128)(2,1)S(1)} %all_to_all.20.parts_ref, f32[128,256]{1,0:T(8,128)S(1)} %own_nodes.1.own_ref, s32[1,128]{1,0:T(1,128)S(1)} %bitcast.9), custom_call_target="tpu_custom_call" | custom-call | flops 1048576 | bytes 197120 | tf_op jit(solution)/shard_map/gradients/pallas_call | solution.py:61
  (1 shorter events, 0.0 us)
Async XLA Ops:
  0.6 14.9 %copy-start.6 = (bf16[128,256]{1,0:T(8,128)(2,1)S(1)}, bf16[128,256]{1,0:T(8,128)(2,1)}, u32[]{:S(2)}) copy-start(bf16[128,256]{1,0:T(8,128)(2,1)} %grad_ref.5) | copy-start | bytes 196612
  0.6 14.9 %copy-start.8 = (s32[128,32]{0,1:T(8,128)S(1)}, s32[128,32]{0,1:T(8,128)}, u32[]{:S(2)}) copy-start(s32[128,32]{0,1:T(8,128)} %param.11) | copy-start | bytes 49156
  2.4 13.1 %collective-permute-start = (bf16[32,256]{1,0:T(8,128)(2,1)}, bf16[32,256]{1,0:T(8,128)(2,1)S(1)}, u32[]{:S(2)}, u32[]{:S(2)}) collective-permute-start(bf16[32,256]{1,0:T(8,128)(2,1)} %get-tuple-element.26), channel_id=1, source_target_pairs={{0,1},{1,2},{2,3},{3,4},{4,5},{5,6},{6,7},{7,8},{8,9},{9,10},{10,1... | collective-permute-start | bytes 49160 | tf_op jit(solution)/shard_map/ppermute | solution.py:361
  2.5 13.1 %collective-permute-start.1 = (bf16[32,256]{1,0:T(8,128)(2,1)}, bf16[32,256]{1,0:T(8,128)(2,1)S(1)}, u32[]{:S(2)}, u32[]{:S(2)}) collective-permute-start(bf16[32,256]{1,0:T(8,128)(2,1)} %get-tuple-element.27), channel_id=1, source_target_pairs={{0,15},{1,0},{2,1},{3,2},{4,3},{5,4},{6,5},{7,6},{8,7},{9,8},{10,9... | collective-permute-start | bytes 49160 | tf_op jit(solution)/shard_map/ppermute | solution.py:362
  4.2 11.3 %copy-start = (bf16[128,256]{1,0:T(8,128)(2,1)S(1)}, bf16[128,256]{1,0:T(8,128)(2,1)}, u32[]{:S(2)}) copy-start(bf16[128,256]{1,0:T(8,128)(2,1)} %x_ref.1) | copy-start | bytes 196612
  4.2 11.4 %copy-start.2 = (bf16[256,256]{1,0:T(8,128)(2,1)S(1)}, bf16[256,256]{1,0:T(8,128)(2,1)}, u32[]{:S(2)}) copy-start(bf16[256,256]{1,0:T(8,128)(2,1)} %wo_ref.1) | copy-start | bytes 393220
  4.2 11.4 %copy-start.3 = (bf16[256,256]{1,0:T(8,128)(2,1)S(1)}, bf16[256,256]{1,0:T(8,128)(2,1)}, u32[]{:S(2)}) copy-start(bf16[256,256]{1,0:T(8,128)(2,1)} %wk_ref.5) | copy-start | bytes 393220
  4.2 11.4 %copy-start.4 = (bf16[256,256]{1,0:T(8,128)(2,1)S(1)}, bf16[256,256]{1,0:T(8,128)(2,1)}, u32[]{:S(2)}) copy-start(bf16[256,256]{1,0:T(8,128)(2,1)} %wv_ref.5) | copy-start | bytes 393220
  4.2 11.4 %copy-start.5 = (bf16[256,256]{1,0:T(8,128)(2,1)S(1)}, bf16[256,256]{1,0:T(8,128)(2,1)}, u32[]{:S(2)}) copy-start(bf16[256,256]{1,0:T(8,128)(2,1)} %wq_ref.5) | copy-start | bytes 393220
  4.2 20.5 %all-to-all-start = ((bf16[8,72,256]{2,1,0:T(8,128)(2,1)}), bf16[8,72,256]{2,1,0:T(8,128)(2,1)S(1)}, u32[]{:S(2)}, u32[]{:S(2)}) async-start(bf16[8,72,256]{2,1,0:T(8,128)(2,1)} %get-tuple-element.24), calls=%async_computation | async-start | bytes 589824 | tf_op jit(solution)/shard_map/all_to_all | solution.py:364
  21.0 5.9 %copy-start.7 = (f32[64,64]{1,0:T(8,128)S(1)}, f32[64,64]{1,0:T(8,128)}, u32[]{:S(2)}) copy-start(f32[64,64]{1,0:T(8,128)} %get-tuple-element.25.allowed_ref) | copy-start | bytes 49156
  32.1 22.0 %all-to-all-start.1 = ((bf16[32,24,256]{2,1,0:T(8,128)(2,1)}), bf16[32,24,256]{2,1,0:T(8,128)(2,1)S(1)}, u32[]{:S(2)}, u32[]{:S(2)}) async-start(bf16[32,24,256]{2,1,0:T(8,128)(2,1)} %get-tuple-element.36), calls=%async_computation.1 | async-start | bytes 786432 | tf_op jit(solution)/shard_map/all_to_all | solution.py:336
  39.0 6.9 %collective-permute-start.2 = (bf16[32,256]{1,0:T(8,128)(2,1)S(1)}, bf16[32,256]{1,0:T(8,128)(2,1)S(1)}, u32[]{:S(2)}, u32[]{:S(2)}) collective-permute-start(bf16[32,256]{1,0:T(8,128)(2,1)S(1)} %get-tuple-element.40), channel_id=1, source_target_pairs={{0,1},{1,2},{2,3},{3,4},{4,5},{5,6},{6,7},{7,8},{8,9},{9,10},{10,1... | collective-permute-start | bytes 49160 | tf_op jit(solution)/shard_map/ppermute | solution.py:389
  39.1 8.4 %collective-permute-start.3 = (bf16[32,256]{1,0:T(8,128)(2,1)S(1)}, bf16[32,256]{1,0:T(8,128)(2,1)S(1)}, u32[]{:S(2)}, u32[]{:S(2)}) collective-permute-start(bf16[32,256]{1,0:T(8,128)(2,1)S(1)} %get-tuple-element.41), channel_id=1, source_target_pairs={{0,15},{1,0},{2,1},{3,2},{4,3},{5,4},{6,5},{7,6},{8,7},{9,8},{10,9... | collective-permute-start | bytes 49160 | tf_op jit(solution)/shard_map/ppermute | solution.py:388
  54.8 15.5 %all-to-all-start.2 = ((bf16[8,16,256]{2,1,0:T(8,128)(2,1)}), bf16[8,16,256]{2,1,0:T(8,128)(2,1)S(1)}, u32[]{:S(2)}, u32[]{:S(2)}) async-start(bf16[8,16,256]{2,1,0:T(8,128)(2,1)} %get-tuple-element.42), calls=%async_computation.2 | async-start | bytes 131072 | tf_op jit(solution)/shard_map/all_to_all | solution.py:336
  70.2 8.1 %copy-start.1 = (s32[128]{0:T(128)S(1)}, s32[128]{0:T(128)}, u32[]{:S(2)}) copy-start(s32[128]{0:T(128)} %param.12) | copy-start | bytes 1540

commit v7 on v6

--- a/solution.py
+++ b/solution.py
@@ -336,6 +336,11 @@
     return lax.all_to_all(parts, axes, 0, 0, tiled=True)
 
 
+def swap_back(parts, axes, count):
+    order = [list(range(count))[::-1]]
+    return lax.all_to_all(parts, axes, 0, 0, axis_index_groups=order, tiled=True)
+
+
 def local(sizes, node_feats, grad_out, neighbours, cluster, super_links, w_query, w_key, w_value, w_out):
     n_x, n_y, n_z, n_c = sizes
     n_super = n_z * n_c
@@ -412,7 +417,7 @@
         pieces, own,
         outside=(1,),
     )
-    shares = swap(shares, "y")
+    shares = swap_back(shares, "y", n_y)
     (columns,) = call(
         columns_body,
         "weight_columns",

time: 79.7 us -> 77.4 us (0.971)
  waiting for transfers between devices: 23.3 us -> 20.2 us
    all_to_all x0 -> x1, starting transfers between devices: none -> 7.66 us  [swap_back(): lax.all_to_all(parts, axes, 0, 0, axis_index_groups=order, tiled=True)]
    all_to_all x2 -> x1, starting transfers between devices: 13.8 us -> 6.71 us  [swap(): return lax.all_to_all(parts, axes, 0, 0, tiled=True)]
    all_to_all x2 -> x1, waiting for transfers between devices: 12.9 us -> 6.38 us  [swap(): return lax.all_to_all(parts, axes, 0, 0, tiled=True)]
    all_to_all x0 -> x1, waiting for transfers between devices: none -> 3.54 us  [swap_back(): lax.all_to_all(parts, axes, 0, 0, axis_index_groups=order, tiled=True)]
where the time goes in v7:
time: 77.4 us; the launch traced here: 76.9 us
  starting transfers between devices  29.2 us (38%)
  waiting for transfers between devices  20.2 us (26%)
  blocking collectives  14.7 us (19%)
  Pallas kernels  11.9 us (15%)
  between operations  0.79 us (1%)
    pallas_call x8, Pallas kernels, call(): pl.pallas_call(body, in_specs=[anywhere if i in outside else smem if a.nd...  11.9 us
    all_to_all x1, starting transfers between devices, local(): parts = lax.all_to_all(sums, 'z', 0, 0, axis_index_groups=order, tiled=True)  11.3 us
    all_to_all x1, blocking collectives, swap(): return lax.all_to_all(parts, axes, 0, 0, tiled=True)  8.24 us
    all_to_all x1, starting transfers between devices, swap_back(): lax.all_to_all(parts, axes, 0, 0, axis_index_groups=order, tiled=True)  7.66 us
    all_to_all x1, starting transfers between devices, swap(): return lax.all_to_all(parts, axes, 0, 0, tiled=True)  6.71 us
    all_to_all x1, waiting for transfers between devices, swap(): return lax.all_to_all(parts, axes, 0, 0, tiled=True)  6.38 us
    ppermute x1, waiting for transfers between devices, local(): from_below = lax.ppermute(above, supers, up)  5.15 us
    all_to_all x1, waiting for transfers between devices, local(): parts = lax.all_to_all(sums, 'z', 0, 0, axis_index_groups=order, tiled=True)  3.65 us
  transfers between devices with their start and end apart: 7, of which 5 were waited for; matrix products, arithmetic and copies ran while one was open for 0% of the time, Pallas kernels for 4%

profile of v7, /device:TPU:64, one launch (start us, length us, event | category | flops | bytes accessed | tf_op | source)
XLA Modules:
  0.0 76.9 jit_solution(14543429038558594139)
XLA Ops:
  0.6 0.0 copy-start.6
  0.6 0.0 copy-start.8
  0.7 1.8 %cluster_sums.1 = (bf16[8,72,256]{2,1,0:T(8,128)(2,1)}, bf16[32,256]{1,0:T(8,128)(2,1)}, bf16[32,256]{1,0:T(8,128)(2,1)}, f32[64,64]{1,0:T(8,128)}) custom-call(bf16[128,256]{1,0:T(8,128)(2,1)} %x_ref.1, s32[1,128]{1,0:T(1,128)} %bitcast.8, s32[8,64]{1,0:T(8,128)} %bitcast.11), custom_call_target="tpu_custom_call" | custom-call | flops 4194304 | bytes 68096 | tf_op jit(solution)/shard_map/cluster_sums/pallas_call | solution.py:61
  2.4 0.0 collective-permute-start
  2.5 1.7 %collective-permute-start.1 = (bf16[32,256]{1,0:T(8,128)(2,1)}, bf16[32,256]{1,0:T(8,128)(2,1)S(1)}, u32[]{:S(2)}, u32[]{:S(2)}) collective-permute-start(bf16[32,256]{1,0:T(8,128)(2,1)} %get-tuple-element.27), channel_id=1, source_target_pairs={{0,15},{1,0},{2,1},{3,2},{4,3},{5,4},{6,5},{7,6},{8,7},{9,8},{10,9... | collective-permute-start | bytes 49160 | tf_op jit(solution)/shard_map/ppermute | solution.py:367
  4.2 0.0 copy-start
  4.2 0.0 copy-start.2
  4.2 0.0 copy-start.3
  4.2 0.0 copy-start.4
  4.2 0.0 copy-start.5
  4.2 11.3 %all-to-all-start = ((bf16[8,72,256]{2,1,0:T(8,128)(2,1)}), bf16[8,72,256]{2,1,0:T(8,128)(2,1)S(1)}, u32[]{:S(2)}, u32[]{:S(2)}) async-start(bf16[8,72,256]{2,1,0:T(8,128)(2,1)} %get-tuple-element.24), calls=%async_computation | async-start | bytes 589824 | tf_op jit(solution)/shard_map/all_to_all | solution.py:369
  15.5 0.0 collective-permute-done.low_ref
  15.5 0.0 collective-permute-done.1.high_ref
  15.5 0.0 copy-done.6
  15.5 0.0 copy-done.8
  15.5 0.0 copy-done
  15.6 0.0 copy-done.2
  15.6 0.0 copy-done.3
  15.6 0.0 copy-done.4
  15.6 0.0 copy-done.5
  15.6 3.0 %near_attention.1 = (bf16[256,128]{1,0:T(8,128)(2,1)S(1)}, bf16[256,128]{1,0:T(8,128)(2,1)S(1)}, bf16[128,128]{1,0:T(8,128)(2,1)S(1)}, bf16[768,256]{1,0:T(8,128...) custom-call(bf16[32,256]{1,0:T(8,128)(2,1)S(1)} %collective-permute-, ...), custom_call_target="tpu_custom_call" | custom-call | flops 10737418240 | bytes 704516 | tf_op jit(solution)/shard_map/near_attention/pallas_call | solution.py:61
  18.6 2.5 %all-gather = bf16[3584,128]{1,0:T(8,128)(2,1)S(1)} all-gather(bf16[1792,128]{1,0:T(8,128)(2,1)S(1)} %get-tuple-element.28), channel_id=2, replica_groups=mesh['x'=4,'y'=8,'z'=8,'c'=2] {'c'}, dimensions={0}, use_global_device_ids=true | all-gather | bytes 1376256 | tf_op jit(solution)/shard_map/all_gather | solution.py:404
  21.0 0.0 copy-start.7
  21.0 3.6 %all-to-all-done = bf16[8,72,256]{2,1,0:T(8,128)(2,1)S(1)} async-done(((bf16[8,72,256]{2,1,0:T(8,128)(2,1)}), bf16[8,72,256]{2,1,0:T(8,128)(2,1)S(1)}, u32[]{:S(2)}, u32[]{:S(2)}) %all-to-all-start) | async-done | bytes 294944 | tf_op jit(solution)/shard_map/all_to_all | solution.py:369
  24.7 2.2 %all_gather.15.parts_ref = bf16[16,72,256]{2,1,0:T(8,128)(2,1)S(1)} all-gather(bf16[8,72,256]{2,1,0:T(8,128)(2,1)S(1)} %all-to-all-done), channel_id=1, replica_groups=mesh['x'=4,'y'=8,'z'=8,'c'=2] {'c'}, dimensions={0}, use_global_device_ids=true | all-gather | bytes 884736 | tf_op jit(solution)/shard_map/all_gather | solution.py:370
  26.9 0.0 copy-done.7
  26.9 5.2 %far_attention.1 = (bf16[32,24,256]{2,1,0:T(8,128)(2,1)}, bf16[256,128]{1,0:T(8,128)(2,1)S(1)}) custom-call(bf16[16,72,256]{2,1,0:T(8,128)(2,1)S(1)} %all_gather.15.parts_ref, f32[64,64]{1,0:T(8,128)S(1)} %copy-done.7, bf16[2,1792,128]{2,1,0:T(8,128)(2,1)S(1)} %bitcast.6, bf16[128,256]{1,0:T(8,128)(2,1)S(1)} %copy-done.6, bf16[256,256]{1,0:T(8,128)(2,1)S(1)} %copy-done.5, ...), custom_call_target="tpu_custom_call" | custom-call | flops 10737418240 | bytes 2998276 | tf_op jit(solution)/shard_map/far_attention/pallas_call | solution.py:61
  32.1 6.7 %all-to-all-start.1 = ((bf16[32,24,256]{2,1,0:T(8,128)(2,1)}), bf16[32,24,256]{2,1,0:T(8,128)(2,1)S(1)}, u32[]{:S(2)}, u32[]{:S(2)}) async-start(bf16[32,24,256]{2,1,0:T(8,128)(2,1)} %get-tuple-element.36), calls=%async_computation.1 | async-start | bytes 786432 | tf_op jit(solution)/shard_map/all_to_all | solution.py:336
  38.8 0.3 halo_returns.1
  39.0 0.0 collective-permute-start.2
  39.1 1.7 %collective-permute-start.3 = (bf16[32,256]{1,0:T(8,128)(2,1)S(1)}, bf16[32,256]{1,0:T(8,128)(2,1)S(1)}, u32[]{:S(2)}, u32[]{:S(2)}) collective-permute-start(bf16[32,256]{1,0:T(8,128)(2,1)S(1)} %get-tuple-element.41), channel_id=1, source_target_pairs={{0,15},{1,0},{2,1},{3,2},{4,3},{5,4},{6,5},{7,6},{8,7},{9,8},{10,9... | collective-permute-start | bytes 49160 | tf_op jit(solution)/shard_map/ppermute | solution.py:393
  40.8 5.1 %collective-permute-done.2.below_ref = bf16[32,256]{1,0:T(8,128)(2,1)S(1)} collective-permute-done((bf16[32,256]{1,0:T(8,128)(2,1)S(1)}, bf16[32,256]{1,0:T(8,128)(2,1)S(1)}, u32[]{:S(2)}, u32[]{:S(2)}) %collective-permute-start.2) | collective-permute-done | bytes 16416 | tf_op jit(solution)/shard_map/ppermute | solution.py:394
  45.9 1.5 %collective-permute-done.3.above_ref = bf16[32,256]{1,0:T(8,128)(2,1)S(1)} collective-permute-done((bf16[32,256]{1,0:T(8,128)(2,1)S(1)}, bf16[32,256]{1,0:T(8,128)(2,1)S(1)}, u32[]{:S(2)}, u32[]{:S(2)}) %collective-permute-start.3) | collective-permute-done | bytes 16416 | tf_op jit(solution)/shard_map/ppermute | solution.py:393
  47.5 0.2 own_nodes.1.own_ref
  47.7 6.4 %all-to-all-done.1.pieces_ref = bf16[32,24,256]{2,1,0:T(8,128)(2,1)S(1)} async-done(((bf16[32,24,256]{2,1,0:T(8,128)(2,1)}), bf16[32,24,256]{2,1,0:T(8,128)(2,1)S(1)}, u32[]{:S(2)}, u32[]{:S(2)}) %all-to-all-start.1) | async-done | bytes 393248 | tf_op jit(solution)/shard_map/all_to_all | solution.py:336
  54.1 0.7 weight_shares.1
  54.8 7.7 %all-to-all-start.2 = ((bf16[8,16,256]{2,1,0:T(8,128)(2,1)}), bf16[8,16,256]{2,1,0:T(8,128)(2,1)S(1)}, u32[]{:S(2)}, u32[]{:S(2)}) async-start(bf16[8,16,256]{2,1,0:T(8,128)(2,1)} %get-tuple-element.42), calls=%async_computation.2 | async-start | bytes 131072 | tf_op jit(solution)/shard_map/all_to_all | solution.py:341
  62.4 1.8 %all-gather.1 = bf16[64,256]{1,0:T(8,128)(2,1)S(1)} all-gather(bf16[32,256]{1,0:T(8,128)(2,1)S(1)} %get-tuple-element.43), channel_id=3, replica_groups=mesh['x'=4,'y'=8,'z'=8,'c'=2] {'c'}, dimensions={0}, use_global_device_ids=true | all-gather | bytes 49152 | tf_op jit(solution)/shard_map/all_gather | solution.py:427
  64.2 3.5 %all-to-all-done.2.parts_ref = bf16[8,16,256]{2,1,0:T(8,128)(2,1)S(1)} async-done(((bf16[8,16,256]{2,1,0:T(8,128)(2,1)}), bf16[8,16,256]{2,1,0:T(8,128)(2,1)S(1)}, u32[]{:S(2)}, u32[]{:S(2)}) %all-to-all-start.2) | async-done | bytes 65568 | tf_op jit(solution)/shard_map/all_to_all | solution.py:341
  67.8 0.0 copy-start.1
  67.8 8.2 %all_to_all.20.parts_ref = bf16[4,32,256]{2,1,0:T(8,128)(2,1)S(1)} all-to-all(bf16[4,32,256]{2,1,0:T(8,128)(2,1)S(1)} %weight_columns.1), channel_id=1, replica_groups=mesh['x'=4,'y'=8,'z'=8,'c'=2] {'x'}, dimensions={0} | all-to-all | bytes 131072 | tf_op jit(solution)/shard_map/all_to_all | solution.py:336
  76.0 0.0 copy-done.1
  76.0 0.9 %gradients.1 = (f32[4,16,256]{2,1,0:T(8,128)}, bf16[128,256]{1,0:T(8,128)(2,1)}) custom-call(bf16[4,32,256]{2,1,0:T(8,128)(2,1)S(1)} %all_to_all.20.parts_ref, f32[128,256]{1,0:T(8,128)S(1)} %own_nodes.1.own_ref, s32[1,128]{1,0:T(1,128)S(1)} %bitcast.9), custom_call_target="tpu_custom_call" | custom-call | flops 1048576 | bytes 197120 | tf_op jit(solution)/shard_map/gradients/pallas_call | solution.py:61
  (1 shorter events, 0.0 us)
Async XLA Ops:
  0.6 14.9 %copy-start.6 = (bf16[128,256]{1,0:T(8,128)(2,1)S(1)}, bf16[128,256]{1,0:T(8,128)(2,1)}, u32[]{:S(2)}) copy-start(bf16[128,256]{1,0:T(8,128)(2,1)} %grad_ref.5) | copy-start | bytes 196612
  0.6 14.9 %copy-start.8 = (s32[128,32]{0,1:T(8,128)S(1)}, s32[128,32]{0,1:T(8,128)}, u32[]{:S(2)}) copy-start(s32[128,32]{0,1:T(8,128)} %param.11) | copy-start | bytes 49156
  2.4 13.1 %collective-permute-start = (bf16[32,256]{1,0:T(8,128)(2,1)}, bf16[32,256]{1,0:T(8,128)(2,1)S(1)}, u32[]{:S(2)}, u32[]{:S(2)}) collective-permute-start(bf16[32,256]{1,0:T(8,128)(2,1)} %get-tuple-element.26), channel_id=1, source_target_pairs={{0,1},{1,2},{2,3},{3,4},{4,5},{5,6},{6,7},{7,8},{8,9},{9,10},{10,1... | collective-permute-start | bytes 49160 | tf_op jit(solution)/shard_map/ppermute | solution.py:366
  2.5 13.1 %collective-permute-start.1 = (bf16[32,256]{1,0:T(8,128)(2,1)}, bf16[32,256]{1,0:T(8,128)(2,1)S(1)}, u32[]{:S(2)}, u32[]{:S(2)}) collective-permute-start(bf16[32,256]{1,0:T(8,128)(2,1)} %get-tuple-element.27), channel_id=1, source_target_pairs={{0,15},{1,0},{2,1},{3,2},{4,3},{5,4},{6,5},{7,6},{8,7},{9,8},{10,9... | collective-permute-start | bytes 49160 | tf_op jit(solution)/shard_map/ppermute | solution.py:367
  4.2 11.3 %copy-start = (bf16[128,256]{1,0:T(8,128)(2,1)S(1)}, bf16[128,256]{1,0:T(8,128)(2,1)}, u32[]{:S(2)}) copy-start(bf16[128,256]{1,0:T(8,128)(2,1)} %x_ref.1) | copy-start | bytes 196612
  4.2 11.4 %copy-start.2 = (bf16[256,256]{1,0:T(8,128)(2,1)S(1)}, bf16[256,256]{1,0:T(8,128)(2,1)}, u32[]{:S(2)}) copy-start(bf16[256,256]{1,0:T(8,128)(2,1)} %wo_ref.1) | copy-start | bytes 393220
  4.2 11.4 %copy-start.3 = (bf16[256,256]{1,0:T(8,128)(2,1)S(1)}, bf16[256,256]{1,0:T(8,128)(2,1)}, u32[]{:S(2)}) copy-start(bf16[256,256]{1,0:T(8,128)(2,1)} %wk_ref.5) | copy-start | bytes 393220
  4.2 11.4 %copy-start.4 = (bf16[256,256]{1,0:T(8,128)(2,1)S(1)}, bf16[256,256]{1,0:T(8,128)(2,1)}, u32[]{:S(2)}) copy-start(bf16[256,256]{1,0:T(8,128)(2,1)} %wv_ref.5) | copy-start | bytes 393220
  4.2 11.4 %copy-start.5 = (bf16[256,256]{1,0:T(8,128)(2,1)S(1)}, bf16[256,256]{1,0:T(8,128)(2,1)}, u32[]{:S(2)}) copy-start(bf16[256,256]{1,0:T(8,128)(2,1)} %wq_ref.5) | copy-start | bytes 393220
  4.2 20.5 %all-to-all-start = ((bf16[8,72,256]{2,1,0:T(8,128)(2,1)}), bf16[8,72,256]{2,1,0:T(8,128)(2,1)S(1)}, u32[]{:S(2)}, u32[]{:S(2)}) async-start(bf16[8,72,256]{2,1,0:T(8,128)(2,1)} %get-tuple-element.24), calls=%async_computation | async-start | bytes 589824 | tf_op jit(solution)/shard_map/all_to_all | solution.py:369
  21.0 5.9 %copy-start.7 = (f32[64,64]{1,0:T(8,128)S(1)}, f32[64,64]{1,0:T(8,128)}, u32[]{:S(2)}) copy-start(f32[64,64]{1,0:T(8,128)} %get-tuple-element.25.allowed_ref) | copy-start | bytes 49156
  32.1 22.0 %all-to-all-start.1 = ((bf16[32,24,256]{2,1,0:T(8,128)(2,1)}), bf16[32,24,256]{2,1,0:T(8,128)(2,1)S(1)}, u32[]{:S(2)}, u32[]{:S(2)}) async-start(bf16[32,24,256]{2,1,0:T(8,128)(2,1)} %get-tuple-element.36), calls=%async_computation.1 | async-start | bytes 786432 | tf_op jit(solution)/shard_map/all_to_all | solution.py:336
  39.0 6.9 %collective-permute-start.2 = (bf16[32,256]{1,0:T(8,128)(2,1)S(1)}, bf16[32,256]{1,0:T(8,128)(2,1)S(1)}, u32[]{:S(2)}, u32[]{:S(2)}) collective-permute-start(bf16[32,256]{1,0:T(8,128)(2,1)S(1)} %get-tuple-element.40), channel_id=1, source_target_pairs={{0,1},{1,2},{2,3},{3,4},{4,5},{5,6},{6,7},{7,8},{8,9},{9,10},{10,1... | collective-permute-start | bytes 49160 | tf_op jit(solution)/shard_map/ppermute | solution.py:394
  39.1 8.4 %collective-permute-start.3 = (bf16[32,256]{1,0:T(8,128)(2,1)S(1)}, bf16[32,256]{1,0:T(8,128)(2,1)S(1)}, u32[]{:S(2)}, u32[]{:S(2)}) collective-permute-start(bf16[32,256]{1,0:T(8,128)(2,1)S(1)} %get-tuple-element.41), channel_id=1, source_target_pairs={{0,15},{1,0},{2,1},{3,2},{4,3},{5,4},{6,5},{7,6},{8,7},{9,8},{10,9... | collective-permute-start | bytes 49160 | tf_op jit(solution)/shard_map/ppermute | solution.py:393
  54.8 13.0 %all-to-all-start.2 = ((bf16[8,16,256]{2,1,0:T(8,128)(2,1)}), bf16[8,16,256]{2,1,0:T(8,128)(2,1)S(1)}, u32[]{:S(2)}, u32[]{:S(2)}) async-start(bf16[8,16,256]{2,1,0:T(8,128)(2,1)} %get-tuple-element.42), calls=%async_computation.2 | async-start | bytes 131072 | tf_op jit(solution)/shard_map/all_to_all | solution.py:341
  67.8 8.3 %copy-start.1 = (s32[128]{0:T(128)S(1)}, s32[128]{0:T(128)}, u32[]{:S(2)}) copy-start(s32[128]{0:T(128)} %param.12) | copy-start | bytes 1540

commit v8 on v7

--- a/solution.py
+++ b/solution.py
@@ -337,7 +337,7 @@
 
 
 def swap_back(parts, axes, count):
-    order = [list(range(count))[::-1]]
+    order = [list(range(count // 2, count)) + list(range(count // 2))[::-1]]
     return lax.all_to_all(parts, axes, 0, 0, axis_index_groups=order, tiled=True)
 
 

time: 77.4 us -> 76.6 us (0.990)
  the two profiles are of different devices: /device:TPU:64 before, /device:TPU:8 now
where the time goes in v8:
time: 76.6 us; the launch traced here: 76.1 us
  starting transfers between devices  29.9 us (39%)
  waiting for transfers between devices  18.1 us (24%)
  blocking collectives  15.3 us (20%)
  Pallas kernels  11.9 us (16%)
  between operations  0.8 us (1%)
    pallas_call x8, Pallas kernels, call(): pl.pallas_call(body, in_specs=[anywhere if i in outside else smem if a.nd...  11.9 us
    all_to_all x1, blocking collectives, swap(): return lax.all_to_all(parts, axes, 0, 0, tiled=True)  8.77 us
    ppermute x1, starting transfers between devices, local(): high = lax.ppermute(first_rows, supers, down)  8.49 us
    all_to_all x1, starting transfers between devices, swap_back(): lax.all_to_all(parts, axes, 0, 0, axis_index_groups=order, tiled=True)  8.1 us
    all_to_all x1, waiting for transfers between devices, swap(): return lax.all_to_all(parts, axes, 0, 0, tiled=True)  6.36 us
    all_to_all x1, starting transfers between devices, swap(): return lax.all_to_all(parts, axes, 0, 0, tiled=True)  5.48 us
    all_to_all x1, waiting for transfers between devices, local(): parts = lax.all_to_all(sums, 'z', 0, 0, axis_index_groups=order, tiled=True)  5.1 us
    all_to_all x1, starting transfers between devices, local(): parts = lax.all_to_all(sums, 'z', 0, 0, axis_index_groups=order, tiled=True)  4.88 us
  transfers between devices with their start and end apart: 7, of which 4 were waited for; matrix products, arithmetic and copies ran while one was open for 0% of the time, Pallas kernels for 5%

profile of v8, /device:TPU:8, one launch (start us, length us, event | category | flops | bytes accessed | tf_op | source)
XLA Modules:
  0.0 76.1 jit_solution(7881988584848061187)
XLA Ops:
  0.6 0.0 copy-start.6
  0.6 0.0 copy-start.8
  0.7 1.8 %cluster_sums.1 = (bf16[8,72,256]{2,1,0:T(8,128)(2,1)}, bf16[32,256]{1,0:T(8,128)(2,1)}, bf16[32,256]{1,0:T(8,128)(2,1)}, f32[64,64]{1,0:T(8,128)}) custom-call(bf16[128,256]{1,0:T(8,128)(2,1)} %x_ref.1, s32[1,128]{1,0:T(1,128)} %bitcast.8, s32[8,64]{1,0:T(8,128)} %bitcast.11), custom_call_target="tpu_custom_call" | custom-call | flops 4194304 | bytes 68096 | tf_op jit(solution)/shard_map/cluster_sums/pallas_call | solution.py:61
  2.4 0.0 collective-permute-start
  2.5 8.5 %collective-permute-start.1 = (bf16[32,256]{1,0:T(8,128)(2,1)}, bf16[32,256]{1,0:T(8,128)(2,1)S(1)}, u32[]{:S(2)}, u32[]{:S(2)}) collective-permute-start(bf16[32,256]{1,0:T(8,128)(2,1)} %get-tuple-element.27), channel_id=1, source_target_pairs={{0,15},{1,0},{2,1},{3,2},{4,3},{5,4},{6,5},{7,6},{8,7},{9,8},{10,9... | collective-permute-start | bytes 49160 | tf_op jit(solution)/shard_map/ppermute | solution.py:367
  11.0 0.0 copy-start
  11.0 0.0 copy-start.2
  11.0 0.0 copy-start.3
  11.0 0.0 copy-start.4
  11.0 0.0 copy-start.5
  11.0 4.9 %all-to-all-start = ((bf16[8,72,256]{2,1,0:T(8,128)(2,1)}), bf16[8,72,256]{2,1,0:T(8,128)(2,1)S(1)}, u32[]{:S(2)}, u32[]{:S(2)}) async-start(bf16[8,72,256]{2,1,0:T(8,128)(2,1)} %get-tuple-element.24), calls=%async_computation | async-start | bytes 589824 | tf_op jit(solution)/shard_map/all_to_all | solution.py:369
  15.9 0.0 collective-permute-done.low_ref
  15.9 0.0 collective-permute-done.1.high_ref
  15.9 0.0 copy-done.6
  15.9 0.0 copy-done.8
  15.9 0.0 copy-done
  15.9 0.0 copy-done.2
  15.9 0.0 copy-done.3
  15.9 0.0 copy-done.4
  15.9 0.0 copy-done.5
  15.9 3.0 %near_attention.1 = (bf16[256,128]{1,0:T(8,128)(2,1)S(1)}, bf16[256,128]{1,0:T(8,128)(2,1)S(1)}, bf16[128,128]{1,0:T(8,128)(2,1)S(1)}, bf16[768,256]{1,0:T(8,128...) custom-call(bf16[32,256]{1,0:T(8,128)(2,1)S(1)} %collective-permute-, ...), custom_call_target="tpu_custom_call" | custom-call | flops 10737418240 | bytes 704516 | tf_op jit(solution)/shard_map/near_attention/pallas_call | solution.py:61
  18.9 2.5 %all-gather = bf16[3584,128]{1,0:T(8,128)(2,1)S(1)} all-gather(bf16[1792,128]{1,0:T(8,128)(2,1)S(1)} %get-tuple-element.28), channel_id=2, replica_groups=mesh['x'=4,'y'=8,'z'=8,'c'=2] {'c'}, dimensions={0}, use_global_device_ids=true | all-gather | bytes 1376256 | tf_op jit(solution)/shard_map/all_gather | solution.py:404
  21.4 0.0 copy-start.7
  21.4 5.1 %all-to-all-done = bf16[8,72,256]{2,1,0:T(8,128)(2,1)S(1)} async-done(((bf16[8,72,256]{2,1,0:T(8,128)(2,1)}), bf16[8,72,256]{2,1,0:T(8,128)(2,1)S(1)}, u32[]{:S(2)}, u32[]{:S(2)}) %all-to-all-start) | async-done | bytes 294944 | tf_op jit(solution)/shard_map/all_to_all | solution.py:369
  26.5 2.2 %all_gather.15.parts_ref = bf16[16,72,256]{2,1,0:T(8,128)(2,1)S(1)} all-gather(bf16[8,72,256]{2,1,0:T(8,128)(2,1)S(1)} %all-to-all-done), channel_id=1, replica_groups=mesh['x'=4,'y'=8,'z'=8,'c'=2] {'c'}, dimensions={0}, use_global_device_ids=true | all-gather | bytes 884736 | tf_op jit(solution)/shard_map/all_gather | solution.py:370
  28.7 0.0 copy-done.7
  28.7 5.2 %far_attention.1 = (bf16[32,24,256]{2,1,0:T(8,128)(2,1)}, bf16[256,128]{1,0:T(8,128)(2,1)S(1)}) custom-call(bf16[16,72,256]{2,1,0:T(8,128)(2,1)S(1)} %all_gather.15.parts_ref, f32[64,64]{1,0:T(8,128)S(1)} %copy-done.7, bf16[2,1792,128]{2,1,0:T(8,128)(2,1)S(1)} %bitcast.6, bf16[128,256]{1,0:T(8,128)(2,1)S(1)} %copy-done.6, bf16[256,256]{1,0:T(8,128)(2,1)S(1)} %copy-done.5, ...), custom_call_target="tpu_custom_call" | custom-call | flops 10737418240 | bytes 2998276 | tf_op jit(solution)/shard_map/far_attention/pallas_call | solution.py:61
  33.9 5.5 %all-to-all-start.1 = ((bf16[32,24,256]{2,1,0:T(8,128)(2,1)}), bf16[32,24,256]{2,1,0:T(8,128)(2,1)S(1)}, u32[]{:S(2)}, u32[]{:S(2)}) async-start(bf16[32,24,256]{2,1,0:T(8,128)(2,1)} %get-tuple-element.36), calls=%async_computation.1 | async-start | bytes 786432 | tf_op jit(solution)/shard_map/all_to_all | solution.py:336
  39.4 0.3 halo_returns.1
  39.6 0.0 collective-permute-start.2
  39.6 2.9 %collective-permute-start.3 = (bf16[32,256]{1,0:T(8,128)(2,1)S(1)}, bf16[32,256]{1,0:T(8,128)(2,1)S(1)}, u32[]{:S(2)}, u32[]{:S(2)}) collective-permute-start(bf16[32,256]{1,0:T(8,128)(2,1)S(1)} %get-tuple-element.41), channel_id=1, source_target_pairs={{0,15},{1,0},{2,1},{3,2},{4,3},{5,4},{6,5},{7,6},{8,7},{9,8},{10,9... | collective-permute-start | bytes 49160 | tf_op jit(solution)/shard_map/ppermute | solution.py:393
  42.6 4.8 %collective-permute-done.2.below_ref = bf16[32,256]{1,0:T(8,128)(2,1)S(1)} collective-permute-done((bf16[32,256]{1,0:T(8,128)(2,1)S(1)}, bf16[32,256]{1,0:T(8,128)(2,1)S(1)}, u32[]{:S(2)}, u32[]{:S(2)}) %collective-permute-start.2) | collective-permute-done | bytes 16416 | tf_op jit(solution)/shard_map/ppermute | solution.py:394
  47.4 0.0 collective-permute-done.3.above_ref
  47.4 0.2 own_nodes.1.own_ref
  47.6 6.4 %all-to-all-done.1.pieces_ref = bf16[32,24,256]{2,1,0:T(8,128)(2,1)S(1)} async-done(((bf16[32,24,256]{2,1,0:T(8,128)(2,1)}), bf16[32,24,256]{2,1,0:T(8,128)(2,1)S(1)}, u32[]{:S(2)}, u32[]{:S(2)}) %all-to-all-start.1) | async-done | bytes 393248 | tf_op jit(solution)/shard_map/all_to_all | solution.py:336
  54.0 0.7 weight_shares.1
  54.6 8.1 %all-to-all-start.2 = ((bf16[8,16,256]{2,1,0:T(8,128)(2,1)}), bf16[8,16,256]{2,1,0:T(8,128)(2,1)S(1)}, u32[]{:S(2)}, u32[]{:S(2)}) async-start(bf16[8,16,256]{2,1,0:T(8,128)(2,1)} %get-tuple-element.42), calls=%async_computation.2 | async-start | bytes 131072 | tf_op jit(solution)/shard_map/all_to_all | solution.py:341
  62.7 1.8 %all-gather.1 = bf16[64,256]{1,0:T(8,128)(2,1)S(1)} all-gather(bf16[32,256]{1,0:T(8,128)(2,1)S(1)} %get-tuple-element.43), channel_id=3, replica_groups=mesh['x'=4,'y'=8,'z'=8,'c'=2] {'c'}, dimensions={0}, use_global_device_ids=true | all-gather | bytes 49152 | tf_op jit(solution)/shard_map/all_gather | solution.py:427
  64.5 1.9 %all-to-all-done.2.parts_ref = bf16[8,16,256]{2,1,0:T(8,128)(2,1)S(1)} async-done(((bf16[8,16,256]{2,1,0:T(8,128)(2,1)}), bf16[8,16,256]{2,1,0:T(8,128)(2,1)S(1)}, u32[]{:S(2)}, u32[]{:S(2)}) %all-to-all-start.2) | async-done | bytes 65568 | tf_op jit(solution)/shard_map/all_to_all | solution.py:341
  66.5 0.0 copy-start.1
  66.5 8.8 %all_to_all.20.parts_ref = bf16[4,32,256]{2,1,0:T(8,128)(2,1)S(1)} all-to-all(bf16[4,32,256]{2,1,0:T(8,128)(2,1)S(1)} %weight_columns.1), channel_id=1, replica_groups=mesh['x'=4,'y'=8,'z'=8,'c'=2] {'x'}, dimensions={0} | all-to-all | bytes 131072 | tf_op jit(solution)/shard_map/all_to_all | solution.py:336
  75.2 0.0 copy-done.1
  75.2 0.9 %gradients.1 = (f32[4,16,256]{2,1,0:T(8,128)}, bf16[128,256]{1,0:T(8,128)(2,1)}) custom-call(bf16[4,32,256]{2,1,0:T(8,128)(2,1)S(1)} %all_to_all.20.parts_ref, f32[128,256]{1,0:T(8,128)S(1)} %own_nodes.1.own_ref, s32[1,128]{1,0:T(1,128)S(1)} %bitcast.9), custom_call_target="tpu_custom_call" | custom-call | flops 1048576 | bytes 197120 | tf_op jit(solution)/shard_map/gradients/pallas_call | solution.py:61
  (1 shorter events, 0.0 us)
Async XLA Ops:
  0.6 15.2 %copy-start.6 = (bf16[128,256]{1,0:T(8,128)(2,1)S(1)}, bf16[128,256]{1,0:T(8,128)(2,1)}, u32[]{:S(2)}) copy-start(bf16[128,256]{1,0:T(8,128)(2,1)} %grad_ref.5) | copy-start | bytes 196612
  0.6 15.2 %copy-start.8 = (s32[128,32]{0,1:T(8,128)S(1)}, s32[128,32]{0,1:T(8,128)}, u32[]{:S(2)}) copy-start(s32[128,32]{0,1:T(8,128)} %param.11) | copy-start | bytes 49156
  2.4 13.4 %collective-permute-start = (bf16[32,256]{1,0:T(8,128)(2,1)}, bf16[32,256]{1,0:T(8,128)(2,1)S(1)}, u32[]{:S(2)}, u32[]{:S(2)}) collective-permute-start(bf16[32,256]{1,0:T(8,128)(2,1)} %get-tuple-element.26), channel_id=1, source_target_pairs={{0,1},{1,2},{2,3},{3,4},{4,5},{5,6},{6,7},{7,8},{8,9},{9,10},{10,1... | collective-permute-start | bytes 49160 | tf_op jit(solution)/shard_map/ppermute | solution.py:366
  2.5 13.4 %collective-permute-start.1 = (bf16[32,256]{1,0:T(8,128)(2,1)}, bf16[32,256]{1,0:T(8,128)(2,1)S(1)}, u32[]{:S(2)}, u32[]{:S(2)}) collective-permute-start(bf16[32,256]{1,0:T(8,128)(2,1)} %get-tuple-element.27), channel_id=1, source_target_pairs={{0,15},{1,0},{2,1},{3,2},{4,3},{5,4},{6,5},{7,6},{8,7},{9,8},{10,9... | collective-permute-start | bytes 49160 | tf_op jit(solution)/shard_map/ppermute | solution.py:367
  11.0 4.9 %copy-start = (bf16[128,256]{1,0:T(8,128)(2,1)S(1)}, bf16[128,256]{1,0:T(8,128)(2,1)}, u32[]{:S(2)}) copy-start(bf16[128,256]{1,0:T(8,128)(2,1)} %x_ref.1) | copy-start | bytes 196612
  11.0 5.0 %copy-start.2 = (bf16[256,256]{1,0:T(8,128)(2,1)S(1)}, bf16[256,256]{1,0:T(8,128)(2,1)}, u32[]{:S(2)}) copy-start(bf16[256,256]{1,0:T(8,128)(2,1)} %wo_ref.1) | copy-start | bytes 393220
  11.0 5.0 %copy-start.3 = (bf16[256,256]{1,0:T(8,128)(2,1)S(1)}, bf16[256,256]{1,0:T(8,128)(2,1)}, u32[]{:S(2)}) copy-start(bf16[256,256]{1,0:T(8,128)(2,1)} %wk_ref.5) | copy-start | bytes 393220
  11.0 5.0 %copy-start.4 = (bf16[256,256]{1,0:T(8,128)(2,1)S(1)}, bf16[256,256]{1,0:T(8,128)(2,1)}, u32[]{:S(2)}) copy-start(bf16[256,256]{1,0:T(8,128)(2,1)} %wv_ref.5) | copy-start | bytes 393220
  11.0 5.0 %copy-start.5 = (bf16[256,256]{1,0:T(8,128)(2,1)S(1)}, bf16[256,256]{1,0:T(8,128)(2,1)}, u32[]{:S(2)}) copy-start(bf16[256,256]{1,0:T(8,128)(2,1)} %wq_ref.5) | copy-start | bytes 393220
  11.0 15.5 %all-to-all-start = ((bf16[8,72,256]{2,1,0:T(8,128)(2,1)}), bf16[8,72,256]{2,1,0:T(8,128)(2,1)S(1)}, u32[]{:S(2)}, u32[]{:S(2)}) async-start(bf16[8,72,256]{2,1,0:T(8,128)(2,1)} %get-tuple-element.24), calls=%async_computation | async-start | bytes 589824 | tf_op jit(solution)/shard_map/all_to_all | solution.py:369
  21.4 7.3 %copy-start.7 = (f32[64,64]{1,0:T(8,128)S(1)}, f32[64,64]{1,0:T(8,128)}, u32[]{:S(2)}) copy-start(f32[64,64]{1,0:T(8,128)} %get-tuple-element.25.allowed_ref) | copy-start | bytes 49156
  33.9 20.1 %all-to-all-start.1 = ((bf16[32,24,256]{2,1,0:T(8,128)(2,1)}), bf16[32,24,256]{2,1,0:T(8,128)(2,1)S(1)}, u32[]{:S(2)}, u32[]{:S(2)}) async-start(bf16[32,24,256]{2,1,0:T(8,128)(2,1)} %get-tuple-element.36), calls=%async_computation.1 | async-start | bytes 786432 | tf_op jit(solution)/shard_map/all_to_all | solution.py:336
  39.6 7.7 %collective-permute-start.2 = (bf16[32,256]{1,0:T(8,128)(2,1)S(1)}, bf16[32,256]{1,0:T(8,128)(2,1)S(1)}, u32[]{:S(2)}, u32[]{:S(2)}) collective-permute-start(bf16[32,256]{1,0:T(8,128)(2,1)S(1)} %get-tuple-element.40), channel_id=1, source_target_pairs={{0,1},{1,2},{2,3},{3,4},{4,5},{5,6},{6,7},{7,8},{8,9},{9,10},{10,1... | collective-permute-start | bytes 49160 | tf_op jit(solution)/shard_map/ppermute | solution.py:394
  39.6 7.7 %collective-permute-start.3 = (bf16[32,256]{1,0:T(8,128)(2,1)S(1)}, bf16[32,256]{1,0:T(8,128)(2,1)S(1)}, u32[]{:S(2)}, u32[]{:S(2)}) collective-permute-start(bf16[32,256]{1,0:T(8,128)(2,1)S(1)} %get-tuple-element.41), channel_id=1, source_target_pairs={{0,15},{1,0},{2,1},{3,2},{4,3},{5,4},{6,5},{7,6},{8,7},{9,8},{10,9... | collective-permute-start | bytes 49160 | tf_op jit(solution)/shard_map/ppermute | solution.py:393
  54.6 11.8 %all-to-all-start.2 = ((bf16[8,16,256]{2,1,0:T(8,128)(2,1)}), bf16[8,16,256]{2,1,0:T(8,128)(2,1)S(1)}, u32[]{:S(2)}, u32[]{:S(2)}) async-start(bf16[8,16,256]{2,1,0:T(8,128)(2,1)} %get-tuple-element.42), calls=%async_computation.2 | async-start | bytes 131072 | tf_op jit(solution)/shard_map/all_to_all | solution.py:341
  66.5 8.8 %copy-start.1 = (s32[128]{0:T(128)S(1)}, s32[128]{0:T(128)}, u32[]{:S(2)}) copy-start(s32[128]{0:T(128)} %param.12) | copy-start | bytes 1540
